TPU v7x, 32 devices: a whole 2x2x4 slice. The times are simulated.
32 devices in a mesh: ctx: 4 (over z), exp: 8 (over y, x, core).
Axes of the slice: x: 2, y: 2, z: 4, core: 2. Of those that a mesh axis runs over, the one named last changes fastest.
Arguments:
- tokens: bfloat16 [2, 8, 1024, 2048], P(None, 'exp', 'ctx'), may hold values from -6 to 6
- routes: int32 [2, 8, 1024, 8], P(None, 'exp', 'ctx'), may hold values from 0 to 31, all different within a row; in each aligned block of 256 rows (0 to 255, 256 to 511, ..., all dimensions but the last counted through in order) at most 80 rows name the same one
- route_weights: float32 [2, 8, 1024, 8], P(None, 'exp', 'ctx'), may hold values from 0.05 to 0.25
- bounds: int32 [2, 8], P(None, 'exp'), may hold values from 1 to 1023, as said below
- norm_attn: float32 [2048], replicated, may hold values from 0.5 to 1.5
- norm_ffn: float32 [2048], replicated, may hold values from 0.5 to 1.5
- q_gain: float32 [128], replicated, may hold values from 0.25 to 1.75
- k_gain: float32 [128], replicated, may hold values from 0.25 to 1.75
- w_q: bfloat16 [2048, 4096], P('exp'), may hold values from -0.125 to 0.125
- w_k: bfloat16 [2048, 512], P('exp'), may hold values from -0.125 to 0.125
- w_v: bfloat16 [2048, 512], P('exp'), may hold values from -0.125 to 0.125
- w_o: bfloat16 [4096, 2048], P('exp'), may hold values from -0.75 to 0.75
- w_gate: bfloat16 [32, 2048, 768], P(('ctx', 'exp')), may hold values from -0.125 to 0.125
- w_up: bfloat16 [32, 2048, 768], P(('ctx', 'exp')), may hold values from -0.125 to 0.125
- w_down: bfloat16 [32, 768, 2048], P(('ctx', 'exp')), may hold values from -0.875 to 0.875
- cotangent: bfloat16 [2, 8, 1024, 2048], P(None, 'exp', 'ctx'), may hold values from -6 to 6
Outputs:
- output: bfloat16 [2, 8, 1024, 2048], P(None, 'exp', 'ctx')
- tokens_grad: float32 [2, 8, 1024, 2048], P(None, 'exp', 'ctx')
- route_weights_grad: float32 [2, 8, 1024, 8], P(None, 'exp', 'ctx')
- w_q_grad: float32 [2048, 4096], P(('ctx', 'exp'))
- w_k_grad: float32 [2048, 512], P(('ctx', 'exp'))
- w_v_grad: float32 [2048, 512], P(('ctx', 'exp'))
- w_o_grad: float32 [4096, 2048], P(('ctx', 'exp'))
- gains_grad: float32 [4352], P(('ctx', 'exp'))
- w_gate_grad: float32 [32, 2048, 768], P(('ctx', 'exp'))
- w_up_grad: float32 [32, 2048, 768], P(('ctx', 'exp'))
- w_down_grad: float32 [32, 768, 2048], P(('ctx', 'exp'))
Inputs may be any that keep to these rules, and one draw needn't show every extreme that they name: `routes`: each position names 8 different experts; within one micro-batch the 256 positions of one device name no expert more than 80 times, a bound that some block reaches in some of these blocks. `bounds`: each packed row holds two documents, the second beginning at the bound; one of the two is longer than 768 positions.
All inputs are finite; a program needn't handle non-finite values.
Results may differ from a plain program's by a relative error of at most 0.018.
Values may be sent and summed in bfloat16 or wider, within the bound.
A program may use at most 640 MiB of HBM per device.

v0:
```python
import jax
import jax.numpy as jnp
from jax import lax
from jax.sharding import PartitionSpec as P

EPSILON = 1e-06
ROPE_BASE = 1000000.0
MASKED = -1e30


def norm_rows(value, gain):
    scale = lax.rsqrt(jnp.mean(value * value, -1, keepdims=True) + EPSILON)
    return (value * scale * gain, scale)


def norm_back(value, scale, gain, grad):
    inner = grad * gain
    first = scale * inner - value * (scale * scale * scale) * jnp.mean(
        inner * value, -1, keepdims=True
    )
    return (first, grad * value * scale)


def rope_tables(positions, width):
    half = width // 2
    inverse = ROPE_BASE ** (-jnp.arange(half, dtype=jnp.float32) * 2.0 / width)
    angle = positions.astype(jnp.float32)[:, None] * inverse[None, :]
    return (jnp.cos(angle), jnp.sin(angle))


def rotate(value, cosine, sine):
    half = value.shape[-1] // 2
    first = value[..., :half]
    second = value[..., half:]
    cos_b = cosine[:, None, :]
    sin_b = sine[:, None, :]
    return jnp.concatenate([first * cos_b - second * sin_b, second * cos_b + first * sin_b], -1)


def rotate_back(value, cosine, sine):
    half = value.shape[-1] // 2
    first = value[..., :half]
    second = value[..., half:]
    cos_b = cosine[:, None, :]
    sin_b = sine[:, None, :]
    return jnp.concatenate([first * cos_b + second * sin_b, second * cos_b - first * sin_b], -1)


def slot_layout(route_block, experts, capacity, top):
    flat = route_block.reshape(-1)
    one_hot = (flat[:, None] == jnp.arange(experts, dtype=jnp.int32)[None, :]).astype(jnp.int32)
    before = jnp.cumsum(one_hot, 0) - one_hot
    place = jnp.sum(before * one_hot, 1)
    slot = flat * capacity + place
    owner_token = jnp.arange(flat.shape[0], dtype=jnp.int32) // top
    table = jnp.zeros((experts * capacity,), jnp.int32).at[slot].set(owner_token)
    filled = jnp.zeros((experts * capacity,), jnp.float32).at[slot].set(1.0)
    return (slot, table, filled)


def attention_terms(
    hidden_rows, query_rows, key_rows, value_rows, attended_rows, branch_rows, gain_rows
):
    query_term = jnp.einsum(
        "td,te->de", hidden_rows, query_rows, preferred_element_type=jnp.float32
    )
    key_term = jnp.einsum("td,te->de", hidden_rows, key_rows, preferred_element_type=jnp.float32)
    value_term = jnp.einsum(
        "td,te->de", hidden_rows, value_rows, preferred_element_type=jnp.float32
    )
    out_term = jnp.einsum(
        "td,te->de", attended_rows, branch_rows, preferred_element_type=jnp.float32
    )
    return (query_term, key_term, value_term, out_term, gain_rows)


def per_device(
    tokens,
    routes,
    route_weights,
    bounds,
    norm_attn,
    norm_ffn,
    q_gain,
    k_gain,
    w_q,
    w_k,
    w_v,
    w_o,
    w_gate,
    w_up,
    w_down,
    cotangent,
):
    micro = tokens.shape[0]
    local = tokens.shape[2]
    width = tokens.shape[3]
    head_dim = q_gain.shape[0]
    heads = w_q.shape[1] // head_dim
    kv_heads = w_k.shape[1] // head_dim
    group = heads // kv_heads
    top = routes.shape[3]
    owned = w_gate.shape[0]
    sources = lax.axis_size(("ctx", "exp"))
    experts = sources * owned
    capacity = max(2, local * top * 5 // (4 * experts))
    seq_len = local * lax.axis_size("ctx")
    scale = head_dim ** (-0.5)
    pair_width = kv_heads * head_dim
    positions = lax.axis_index("ctx") * local + jnp.arange(local, dtype=jnp.int32)
    every_place = jnp.arange(seq_len, dtype=jnp.int32)
    cosine, sine = rope_tables(positions, head_dim)
    query_weight, key_weight, value_weight, out_weight = (
        lax.all_gather(w_q, "exp", axis=0, tiled=True),
        lax.all_gather(w_k, "exp", axis=0, tiled=True),
        lax.all_gather(w_v, "exp", axis=0, tiled=True),
        lax.all_gather(w_o, "exp", axis=0, tiled=True),
    )
    totals = None
    outputs = []
    token_grads = []
    route_grads = []
    hidden_list = []
    query_list = []
    key_list = []
    value_list = []
    attended_list = []
    branch_list = []
    gain_list = []
    received_list = []
    active_list = []
    incoming_list = []
    gate_grad_list = []
    upper_grad_list = []
    for step in range(micro):
        row = tokens[step, 0].astype(jnp.float32)
        hidden, first_scale = norm_rows(row, norm_attn)
        hidden = hidden.astype(jnp.bfloat16)
        query_raw = jnp.dot(hidden, query_weight, preferred_element_type=jnp.float32).reshape(
            local, heads, head_dim
        )
        key_raw = jnp.dot(hidden, key_weight, preferred_element_type=jnp.float32).reshape(
            local, kv_heads, head_dim
        )
        value_low = jnp.dot(hidden, value_weight, preferred_element_type=jnp.float32).astype(
            jnp.bfloat16
        )
        query_normed, query_scale = norm_rows(query_raw, q_gain)
        key_normed, key_scale = norm_rows(key_raw, k_gain)
        queries = (
            rotate(query_normed, cosine, sine)
            .astype(jnp.bfloat16)
            .reshape(local, kv_heads, group, head_dim)
        )
        keys = rotate(key_normed, cosine, sine).astype(jnp.bfloat16).reshape(local, pair_width)
        all_keys, all_values = (
            lax.all_gather(keys, "ctx", axis=0, tiled=True),
            lax.all_gather(value_low, "ctx", axis=0, tiled=True),
        )
        all_keys = all_keys.reshape(seq_len, kv_heads, head_dim)
        all_values = all_values.reshape(seq_len, kv_heads, head_dim)
        bound = bounds[step, 0]
        allowed = (every_place[None, :] <= positions[:, None]) & (
            (every_place[None, :] >= bound) == (positions[:, None] >= bound)
        )

        def masked_scores():
            raw = (
                jnp.einsum("qgjd,kgd->gjqk", queries, all_keys, preferred_element_type=jnp.float32)
                * scale
            )
            return jnp.where(allowed[None, None], raw, MASKED)

        scores = masked_scores()
        top_score = jnp.max(scores, -1, keepdims=True)
        total = jnp.sum(jnp.exp(scores - top_score), -1, keepdims=True)
        log_total = top_score + jnp.log(total)
        chances = jnp.exp(scores - log_total).astype(jnp.bfloat16)
        attended = jnp.einsum(
            "gjqk,kgd->qgjd", chances, all_values, preferred_element_type=jnp.float32
        )
        attended = attended.reshape(local, heads * head_dim).astype(jnp.bfloat16)
        middle = row + jnp.dot(attended, out_weight, preferred_element_type=jnp.float32)
        feed_in, second_scale = norm_rows(middle, norm_ffn)
        feed_in = feed_in.astype(jnp.bfloat16)
        slot, table, filled = slot_layout(routes[step, 0], experts, capacity, top)
        dispatch_map = (
            (table[:, None] == jnp.arange(local, dtype=jnp.int32)[None, :]) & (filled[:, None] > 0)
        ).astype(jnp.bfloat16)
        sent = jnp.dot(dispatch_map, feed_in, preferred_element_type=jnp.float32).astype(
            jnp.bfloat16
        )
        sent = sent.reshape(experts, capacity, width)
        piece = lax.all_to_all(sent, ("ctx", "exp"), split_axis=0, concat_axis=0, tiled=True)
        count = piece.shape[1]
        grouped = piece.reshape(sources, owned, count, width)
        gate = jnp.einsum("sjcd,jdf->sjcf", grouped, w_gate, preferred_element_type=jnp.float32)
        upper = jnp.einsum("sjcd,jdf->sjcf", grouped, w_up, preferred_element_type=jnp.float32)
        active = (gate * jax.nn.sigmoid(gate) * upper).astype(jnp.bfloat16)
        produced = jnp.einsum(
            "sjcf,jfd->sjcd", active, w_down, preferred_element_type=jnp.float32
        ).astype(jnp.bfloat16)
        hidden_units = gate.shape[-1]
        received, gate, upper, produced = (
            piece,
            gate.reshape(experts, count, hidden_units),
            upper.reshape(experts, count, hidden_units),
            produced.reshape(experts, count, width),
        )
        returned = lax.all_to_all(produced, ("ctx", "exp"), split_axis=0, concat_axis=0, tiled=True)
        picked = (
            jnp.take(returned.reshape(experts * capacity, width), slot, axis=0)
            .reshape(local, top, width)
            .astype(jnp.float32)
        )
        route_row = route_weights[step, 0]
        outputs.append((middle + jnp.sum(picked * route_row[:, :, None], 1)).astype(jnp.bfloat16))
        grad = cotangent[step, 0].astype(jnp.float32)
        route_grads.append(jnp.sum(picked * grad[:, None, :], -1))
        slot_weight = (
            jnp.zeros((experts * capacity,), jnp.float32).at[slot].set(route_row.reshape(-1))
        )
        slot_grad = (
            (jnp.take(grad, table, axis=0) * slot_weight[:, None])
            .astype(jnp.bfloat16)
            .reshape(experts, capacity, width)
        )
        grad_in = lax.all_to_all(
            slot_grad, ("ctx", "exp"), split_axis=0, concat_axis=0, tiled=True
        ).reshape(sources, owned, capacity, width)
        gate_grouped = gate.reshape(sources, owned, capacity, -1)
        upper_grouped = upper.reshape(sources, owned, capacity, -1)
        received_grouped = received.reshape(sources, owned, capacity, width)
        sigma = jax.nn.sigmoid(gate_grouped)
        swish = gate_grouped * sigma
        active = (swish * upper_grouped).astype(jnp.bfloat16)
        active_grad = jnp.einsum(
            "sjcd,jfd->sjcf", grad_in, w_down, preferred_element_type=jnp.float32
        )
        gate_grad = (
            active_grad * upper_grouped * sigma * (1.0 + gate_grouped * (1.0 - sigma))
        ).astype(jnp.bfloat16)
        upper_grad = (active_grad * swish).astype(jnp.bfloat16)
        received_list.append(received_grouped)
        active_list.append(active)
        incoming_list.append(grad_in)
        gate_grad_list.append(gate_grad)
        upper_grad_list.append(upper_grad)
        back = jnp.einsum(
            "sjcf,jdf->sjcd", gate_grad, w_gate, preferred_element_type=jnp.float32
        ) + jnp.einsum("sjcf,jdf->sjcd", upper_grad, w_up, preferred_element_type=jnp.float32)
        back = back.astype(jnp.bfloat16).reshape(experts, capacity, width)
        back_home = lax.all_to_all(back, ("ctx", "exp"), split_axis=0, concat_axis=0, tiled=True)
        feed_grad = jnp.einsum(
            "st,sd->td",
            dispatch_map,
            back_home.reshape(experts * capacity, width),
            preferred_element_type=jnp.float32,
        )
        middle_norm_grad, second_gain = norm_back(middle, second_scale, norm_ffn, feed_grad)
        middle_grad = grad + middle_norm_grad
        branch_grad = middle_grad.astype(jnp.bfloat16)
        attended_grad = jnp.einsum(
            "te,de->td", branch_grad, out_weight, preferred_element_type=jnp.float32
        )
        attended_grad = attended_grad.astype(jnp.bfloat16).reshape(local, kv_heads, group, head_dim)
        chances_again = jnp.exp(masked_scores() - log_total)
        chance_grad = jnp.einsum(
            "qgjd,kgd->gjqk", attended_grad, all_values, preferred_element_type=jnp.float32
        )
        score_grad = chances_again * (
            chance_grad - jnp.sum(chances_again * chance_grad, -1, keepdims=True)
        )
        score_grad = score_grad.astype(jnp.bfloat16)
        query_grad = (
            jnp.einsum("gjqk,kgd->qgjd", score_grad, all_keys, preferred_element_type=jnp.float32)
            * scale
        ).astype(jnp.bfloat16)
        key_part = (
            jnp.einsum("gjqk,qgjd->kgd", score_grad, queries, preferred_element_type=jnp.float32)
            * scale
        )
        value_part = jnp.einsum(
            "gjqk,qgjd->kgd", chances, attended_grad, preferred_element_type=jnp.float32
        )
        key_value_grad = lax.psum_scatter(
            jnp.concatenate(
                [key_part.reshape(seq_len, pair_width), value_part.reshape(seq_len, pair_width)], -1
            ).astype(jnp.bfloat16),
            "ctx",
            scatter_dimension=0,
            tiled=True,
        ).astype(jnp.float32)
        key_grad = lax.optimization_barrier(
            key_value_grad[:, :pair_width].astype(jnp.bfloat16)
        ).astype(jnp.float32)
        value_grad = key_value_grad[:, pair_width:].astype(jnp.bfloat16)
        query_grad = (
            lax.optimization_barrier(query_grad).astype(jnp.float32).reshape(local, heads, head_dim)
        )
        query_turned = rotate_back(query_grad, cosine, sine)
        key_turned = rotate_back(key_grad.reshape(local, kv_heads, head_dim), cosine, sine)
        query_raw_grad, query_gain_part = norm_back(query_raw, query_scale, q_gain, query_turned)
        key_raw_grad, key_gain_part = norm_back(key_raw, key_scale, k_gain, key_turned)
        query_raw_low = query_raw_grad.astype(jnp.bfloat16).reshape(local, heads * head_dim)
        key_raw_low = key_raw_grad.astype(jnp.bfloat16).reshape(local, pair_width)
        hidden_grad = (
            jnp.einsum("te,de->td", query_raw_low, query_weight, preferred_element_type=jnp.float32)
            + jnp.einsum("te,de->td", key_raw_low, key_weight, preferred_element_type=jnp.float32)
            + jnp.einsum("te,de->td", value_grad, value_weight, preferred_element_type=jnp.float32)
        )
        first_grad, first_gain = norm_back(row, first_scale, norm_attn, hidden_grad)
        token_grads.append(middle_grad + first_grad)
        gain_term = jnp.concatenate(
            [
                jnp.sum(first_gain, 0),
                jnp.sum(second_gain, 0),
                jnp.sum(query_gain_part, (0, 1)),
                jnp.sum(key_gain_part, (0, 1)),
            ]
        )
        hidden_list.append(hidden)
        query_list.append(query_raw_low)
        key_list.append(key_raw_low)
        value_list.append(value_grad)
        attended_list.append(attended)
        branch_list.append(branch_grad)
        gain_list.append(gain_term)
    terms = attention_terms(
        jnp.concatenate(hidden_list, 0),
        jnp.concatenate(query_list, 0),
        jnp.concatenate(key_list, 0),
        jnp.concatenate(value_list, 0),
        jnp.concatenate(attended_list, 0),
        jnp.concatenate(branch_list, 0),
        jnp.sum(jnp.stack(gain_list), 0),
    )
    totals = (
        lax.psum_scatter(terms[0], ("ctx", "exp"), scatter_dimension=0, tiled=True),
        lax.psum_scatter(terms[1], ("ctx", "exp"), scatter_dimension=0, tiled=True),
        lax.psum_scatter(terms[2], ("ctx", "exp"), scatter_dimension=0, tiled=True),
        lax.psum_scatter(terms[3], ("ctx", "exp"), scatter_dimension=0, tiled=True),
        lax.psum_scatter(terms[4], ("ctx", "exp"), scatter_dimension=0, tiled=True),
    )
    received_all = jnp.concatenate(received_list, 2)
    active_all = jnp.concatenate(active_list, 2)
    incoming_all = jnp.concatenate(incoming_list, 2)
    gate_grad_all = jnp.concatenate(gate_grad_list, 2)
    upper_grad_all = jnp.concatenate(upper_grad_list, 2)
    down_term = jnp.einsum(
        "sjcf,sjcd->jfd", active_all, incoming_all, preferred_element_type=jnp.float32
    )
    gate_term = jnp.einsum(
        "sjcd,sjcf->jdf", received_all, gate_grad_all, preferred_element_type=jnp.float32
    )
    up_term = jnp.einsum(
        "sjcd,sjcf->jdf", received_all, upper_grad_all, preferred_element_type=jnp.float32
    )
    output = jnp.stack(outputs)[:, None]
    tokens_grad = jnp.stack(token_grads)[:, None]
    route_weights_grad = jnp.stack(route_grads)[:, None]
    return (
        output,
        tokens_grad,
        route_weights_grad,
        totals[0],
        totals[1],
        totals[2],
        totals[3],
        totals[4],
        gate_term,
        up_term,
        down_term,
    )


def solution(mesh):
    in_specs = (
        P(None, "exp", "ctx", None),
        P(None, "exp", "ctx", None),
        P(None, "exp", "ctx", None),
        P(None, "exp"),
        P(),
        P(),
        P(),
        P(),
        P("exp", None),
        P("exp", None),
        P("exp", None),
        P("exp", None),
        P(("ctx", "exp"), None, None),
        P(("ctx", "exp"), None, None),
        P(("ctx", "exp"), None, None),
        P(None, "exp", "ctx", None),
    )
    out_specs = (
        P(None, "exp", "ctx", None),
        P(None, "exp", "ctx", None),
        P(None, "exp", "ctx", None),
        P(("ctx", "exp"), None),
        P(("ctx", "exp"), None),
        P(("ctx", "exp"), None),
        P(("ctx", "exp"), None),
        P(("ctx", "exp")),
        P(("ctx", "exp"), None, None),
        P(("ctx", "exp"), None, None),
        P(("ctx", "exp"), None, None),
    )
    return jax.shard_map(
        per_device, mesh=mesh, in_specs=in_specs, out_specs=out_specs, check_vma=False
    )
```

profile of v0, /device:TPU:0, one launch (start us, length us, event | category | flops | bytes accessed | tf_op | source)
XLA Modules:
  0.0 3352.6 jit_solution(221421843514616750)
XLA Ops:
  15.3 25.3 all-gather.9.cloned.1.call-done
  46.7 15.9 reduce-window.14
  85.9 21.3 gather_fusion.2
  107.2 14.3 fusion.12
  139.9 15.9 reduce-window.16
  178.0 21.3 gather_fusion.3
  212.1 166.6 %all-to-all-done.4 = bf16[32,80,2048]{2,1,0:T(8,128)(2,1)} async-done(((bf16[32,80,2048]{2,1,0:T(8,128)(2,1)}), bf16[32,80,2048]{2,1,0:T(8,128)(2,1)}, u32[]{:S(2)}, u32[]{:S(2)}) %all-to-all-start.4) | async-done | bytes 10485792 | tf_op jit(solution)/shard_map/all_to_all | solution.py:228
  398.5 22.6 copy.101
  452.4 16.9 fusion.14
  469.3 15.1 exponential_reduce_fusion
  509.9 21.2 all-gather.19.cloned.1.call-done
  549.8 67.0 %all-to-all-done.6 = bf16[32,80,2048]{2,1,0:T(8,128)(2,1)} async-done(((bf16[32,80,2048]{2,1,0:T(8,128)(2,1)}), bf16[32,80,2048]{2,1,0:T(8,128)(2,1)}, u32[]{:S(2)}, u32[]{:S(2)}) %all-to-all-start.6) | async-done | bytes 10485792 | tf_op jit(solution)/shard_map/all_to_all | solution.py:228
  633.2 46.1 %all-gather.11.cloned.1.call-done = bf16[1024,512]{1,0:T(8,128)(2,1)} async-done(((bf16[256,512]{1,0:T(8,128)(2,1)}), bf16[1024,512]{1,0:T(8,128)(2,1)}) %all-gather.11.cloned.1.call-update) | async-done | bytes 1048592 | tf_op jit(solution)/shard_map/all_gather | solution.py:158
  687.1 54.3 %all-gather.15.cloned.1.call-done = bf16[1024,512]{0,1:T(8,128)(2,1)} async-done(((bf16[256,512]{0,1:T(8,128)(2,1)}), bf16[1024,512]{0,1:T(8,128)(2,1)}) %all-gather.15.cloned.1.call-update) | async-done | bytes 1048592 | tf_op jit(solution)/shard_map/all_gather | solution.py:157
  741.4 16.3 fusion.13
  757.7 15.1 exponential_reduce_fusion.1
  813.9 69.4 %all-to-all-done.2 = bf16[32,80,2048]{2,1,0:T(8,128)(2,1)} async-done(((bf16[32,80,2048]{2,1,0:T(8,128)(2,1)}), bf16[32,80,2048]{2,1,0:T(8,128)(2,1)}, u32[]{:S(2)}, u32[]{:S(2)}) %all-to-all-start.2) | async-done | bytes 10485792 | tf_op jit(solution)/shard_map/all_to_all | solution.py:194
  888.7 14.1 fusion.74
  915.9 19.7 fusion.32
  948.6 172.3 %all-to-all-done = bf16[32,80,2048]{2,1,0:T(8,128)(2,1)} async-done(((bf16[32,80,2048]{2,1,0:T(8,128)(2,1)}), bf16[32,80,2048]{2,1,0:T(8,128)(2,1)}, u32[]{:S(2)}, u32[]{:S(2)}) %all-to-all-start) | async-done | bytes 10485792 | tf_op jit(solution)/shard_map/all_to_all | solution.py:194
  1124.7 15.1 fusion.56
  1139.8 16.5 add_convert_fusion
  1156.3 200.9 %all-to-all-done.3 = bf16[32,80,2048]{2,1,0:T(8,128)(2,1)} async-done(((bf16[32,80,2048]{2,1,0:T(8,128)(2,1)}), bf16[32,80,2048]{2,1,0:T(8,128)(2,1)}, u32[]{:S(2)}, u32[]{:S(2)}) %all-to-all-start.3) | async-done | bytes 10485792 | tf_op jit(solution)/shard_map/all_to_all | solution.py:210
  1388.1 20.0 fusion.37
  1408.1 15.5 fusion.59
  1423.6 16.5 add_convert_fusion.1
  1440.1 153.4 %all-to-all-done.7 = bf16[32,80,2048]{2,1,0:T(8,128)(2,1)} async-done(((bf16[32,80,2048]{2,1,0:T(8,128)(2,1)}), bf16[32,80,2048]{2,1,0:T(8,128)(2,1)}, u32[]{:S(2)}, u32[]{:S(2)}) %all-to-all-start.7) | async-done | bytes 10485792 | tf_op jit(solution)/shard_map/all_to_all | solution.py:253
  1610.4 219.3 %all-to-all-done.5 = bf16[32,80,2048]{2,1,0:T(8,128)(2,1)} async-done(((bf16[32,80,2048]{2,1,0:T(8,128)(2,1)}), bf16[32,80,2048]{2,1,0:T(8,128)(2,1)}, u32[]{:S(2)}, u32[]{:S(2)}) %all-to-all-start.5) | async-done | bytes 10485792 | tf_op jit(solution)/shard_map/all_to_all | solution.py:253
  1834.0 23.6 copy.137
  1857.6 23.6 copy.130
  1881.2 21.7 gather_fusion.1
  1920.5 145.4 %all-to-all-done.1 = bf16[32,80,2048]{2,1,0:T(8,128)(2,1)} async-done(((bf16[32,80,2048]{2,1,0:T(8,128)(2,1)}), bf16[32,80,2048]{2,1,0:T(8,128)(2,1)}, u32[]{:S(2)}, u32[]{:S(2)}) %all-to-all-start.1) | async-done | bytes 10485792 | tf_op jit(solution)/shard_map/all_to_all | solution.py:210
  2065.9 21.8 gather_fusion
  2110.7 18.1 fusion.140
  2130.9 25.2 fusion
  2179.4 24.9 fusion.3
  2213.5 28.1 fusion.5
  2253.7 29.1 fusion.2
  2296.0 43.5 %reduce-scatter.9.cloned.1.call-done = bf16[256,1024]{0,1:T(8,128)(2,1)} async-done(((bf16[1024,1024]{0,1:T(8,128)(2,1)}), bf16[256,1024]{0,1:T(8,128)(2,1)}) %reduce-scatter.9.cloned.1.call-update) | async-done | bytes 524304 | tf_op jit(solution)/shard_map/reduce_scatter | solution.py:286
  2354.3 17.4 fusion.51
  2407.1 17.1 fusion.47
  2424.2 26.3 fusion.65
  2450.5 26.2 fusion.64
  2476.6 26.6 fusion.63
  2549.9 40.2 %all-reduce = f32[4352]{0:T(1024)S(1)} all-reduce(f32[4352]{0:T(1024)S(1)} %maximum_add_fusion), channel_id=8, replica_groups=mesh['ctx'=4,'exp'=8] {'ctx','exp'}, use_global_device_ids=true, to_apply=%region_52.55.clone | all-reduce | flops 4352 | bytes 34816
  2597.2 30.9 reduce-scatter.15.cloned.1.call-done
  2628.1 353.1 %reduce-scatter.17.cloned.1.call-done = f32[128,2048]{1,0:T(8,128)} async-done(((f32[4096,2048]{1,0:T(8,128)}), f32[128,2048]{1,0:T(8,128)}) %reduce-scatter.17.cloned.1.call-update) | async-done | bytes 1048592 | tf_op jit(solution)/shard_map/reduce_scatter | solution.py:342
  2981.2 364.7 %reduce-scatter.11.cloned.1.call-done = f32[64,4096]{1,0:T(8,128)} async-done(((f32[2048,4096]{1,0:T(8,128)}), f32[64,4096]{1,0:T(8,128)}) %reduce-scatter.11.cloned.1.call-update) | async-done | bytes 1048592 | tf_op jit(solution)/shard_map/reduce_scatter | solution.py:339
  (494 shorter events, 541.4 us)
Async XLA Ops:
  7.2 908.7 %copy-start = (bf16[1,768,2048]{2,1,0:T(8,128)(2,1)S(1)}, bf16[1,768,2048]{2,1,0:T(8,128)(2,1)}, u32[]{:S(2)}) copy-start(bf16[1,768,2048]{2,1,0:T(8,128)(2,1)} %param.34) | copy-start | bytes 9437188
  7.2 33.4 all-gather.9.cloned.1.call-start
  7.9 118.4 %all-gather.13.cloned.1.call-start = ((), (), s32[]{:S(2)}) async-start(), calls=%async_computation.16 | async-start | bytes 2359296 | tf_op jit(solution)/shard_map/all_gather | solution.py:115
  8.7 387.5 %all-gather.21.cloned.1.call-start = ((), (), s32[]{:S(2)}) async-start(), calls=%async_computation.20 | async-start | bytes 1310720 | tf_op jit(solution)/shard_map/all_gather | solution.py:158
  43.9 354.6 %all-gather.17.cloned.1.call-start = ((), (), s32[]{:S(2)}) async-start(), calls=%async_computation.18 | async-start | bytes 18874368 | tf_op jit(solution)/shard_map/all_gather | solution.py:114
  121.6 257.2 %all-to-all-start.4 = ((bf16[32,80,2048]{2,1,0:T(8,128)(2,1)}), bf16[32,80,2048]{2,1,0:T(8,128)(2,1)}, u32[]{:S(2)}, u32[]{:S(2)}) async-start(bf16[32,80,2048]{2,1,0:T(8,128)(2,1)} %bitcast.587), calls=%async_computation.4 | async-start | bytes 20971520 | tf_op jit(solution)/shard_map/all_to_all | solution.py:228
  125.4 327.1 %all-gather.23.cloned.1.call-start = ((), (), s32[]{:S(2)}) async-start(), calls=%async_computation.21 | async-start | bytes 1310720 | tf_op jit(solution)/shard_map/all_gather | solution.py:157
  126.3 317.1 %copy-start.48 = (f32[256,64]{0,1:T(8,128)}, f32[256,64]{0,1:T(8,128)S(1)}, u32[]{:S(2)}) copy-start(f32[256,64]{0,1:T(8,128)S(1)} %get-tuple-element.132) | copy-start | bytes 196612
  126.3 317.1 %copy-start.50 = (f32[256,64]{0,1:T(8,128)}, f32[256,64]{0,1:T(8,128)S(1)}, u32[]{:S(2)}) copy-start(f32[256,64]{0,1:T(8,128)S(1)} %get-tuple-element.133) | copy-start | bytes 196612
  137.2 393.9 %all-gather.19.cloned.1.call-start = ((), (), s32[]{:S(2)}) async-start(), calls=%async_computation.19 | async-start | bytes 18874368 | tf_op jit(solution)/shard_map/all_gather | solution.py:117
  169.8 373.1 %copy-start.79 = (s32[2560]{0:T(1024)}, s32[2560]{0:T(1024)S(1)}, u32[]{:S(2)}) copy-start(s32[2560]{0:T(1024)S(1)} %scatter_custom_fusion.2) | copy-start | bytes 30724
  378.7 238.1 %all-to-all-start.6 = ((bf16[32,80,2048]{2,1,0:T(8,128)(2,1)}), bf16[32,80,2048]{2,1,0:T(8,128)(2,1)}, u32[]{:S(2)}, u32[]{:S(2)}) async-start(bf16[32,80,2048]{2,1,0:T(8,128)(2,1)} %bitcast.588), calls=%async_computation.7 | async-start | bytes 20971520 | tf_op jit(solution)/shard_map/all_to_all | solution.py:228
  394.1 148.8 %copy-start.104 = (pred[2560]{0:T(1024)(128)(4,1)}, pred[2560]{0:T(1024)(128)(4,1)S(1)}, u32[]{:S(2)}) copy-start(pred[2560]{0:T(1024)(128)(4,1)S(1)} %broadcast_compare_fusion) | copy-start | bytes 7684
  396.2 88.3 %copy-start.6 = (pred[256,1024]{0,1:T(8,128)(4,1)}, pred[256,1024]{0,1:T(8,128)(4,1)S(1)}, u32[]{:S(2)}) copy-start(pred[256,1024]{0,1:T(8,128)(4,1)S(1)} %get-tuple-element.143) | copy-start | bytes 786436
  616.9 266.4 %all-to-all-start.2 = ((bf16[32,80,2048]{2,1,0:T(8,128)(2,1)}), bf16[32,80,2048]{2,1,0:T(8,128)(2,1)}, u32[]{:S(2)}, u32[]{:S(2)}) async-start(bf16[32,80,2048]{2,1,0:T(8,128)(2,1)} %bitcast.589), calls=%async_computation.2 | async-start | bytes 20971520 | tf_op jit(solution)/shard_map/all_to_all | solution.py:194
  620.7 58.6 %all-gather.11.cloned.1.call-start = ((), (), s32[]{:S(2)}) async-start(), calls=%async_computation.15 | async-start | bytes 1310720 | tf_op jit(solution)/shard_map/all_gather | solution.py:158
  624.1 117.3 %all-gather.15.cloned.1.call-start = ((), (), s32[]{:S(2)}) async-start(), calls=%async_computation.17 | async-start | bytes 1310720 | tf_op jit(solution)/shard_map/all_gather | solution.py:157
  633.1 173.6 %copy-start.106 = (pred[2560]{0:T(1024)(128)(4,1)}, pred[2560]{0:T(1024)(128)(4,1)S(1)}, u32[]{:S(2)}) copy-start(pred[2560]{0:T(1024)(128)(4,1)S(1)} %broadcast_compare_fusion.1) | copy-start | bytes 7684
  633.2 108.2 %copy-start.8 = (pred[256,1024]{0,1:T(8,128)(4,1)S(1)}, pred[256,1024]{0,1:T(8,128)(4,1)}, u32[]{:S(2)}) copy-start(pred[256,1024]{0,1:T(8,128)(4,1)} %get-tuple-element.142) | copy-start | bytes 786436
  883.2 237.7 %all-to-all-start = ((bf16[32,80,2048]{2,1,0:T(8,128)(2,1)}), bf16[32,80,2048]{2,1,0:T(8,128)(2,1)}, u32[]{:S(2)}, u32[]{:S(2)}) async-start(bf16[32,80,2048]{2,1,0:T(8,128)(2,1)} %bitcast.590), calls=%async_computation | async-start | bytes 20971520 | tf_op jit(solution)/shard_map/all_to_all | solution.py:194
  1121.0 236.2 %all-to-all-start.3 = ((bf16[32,80,2048]{2,1,0:T(8,128)(2,1)}), bf16[32,80,2048]{2,1,0:T(8,128)(2,1)}, u32[]{:S(2)}, u32[]{:S(2)}) async-start(bf16[32,80,2048]{2,1,0:T(8,128)(2,1)} %convolution_convert_fusion.2), calls=%async_computation.3 | async-start | bytes 20971520 | tf_op jit(solution)/shard_map/all_to_all | solution.py:210
  1357.1 236.4 %all-to-all-start.7 = ((bf16[32,80,2048]{2,1,0:T(8,128)(2,1)}), bf16[32,80,2048]{2,1,0:T(8,128)(2,1)}, u32[]{:S(2)}, u32[]{:S(2)}) async-start(bf16[32,80,2048]{2,1,0:T(8,128)(2,1)} %add_convert_fusion), calls=%async_computation.8 | async-start | bytes 20971520 | tf_op jit(solution)/shard_map/all_to_all | solution.py:253
  1593.5 236.2 %all-to-all-start.5 = ((bf16[32,80,2048]{2,1,0:T(8,128)(2,1)}), bf16[32,80,2048]{2,1,0:T(8,128)(2,1)}, u32[]{:S(2)}, u32[]{:S(2)}) async-start(bf16[32,80,2048]{2,1,0:T(8,128)(2,1)} %add_convert_fusion.1), calls=%async_computation.5 | async-start | bytes 20971520 | tf_op jit(solution)/shard_map/all_to_all | solution.py:253
  1610.3 223.3 %copy-start.102 = (f32[256,8]{0,1:T(8,128)S(1)}, f32[256,8]{0,1:T(8,128)}, u32[]{:S(2)}) copy-start(f32[256,8]{0,1:T(8,128)} %get-tuple-element.119) | copy-start | bytes 24580
  1610.3 223.5 %copy-start.101 = (f32[256,8]{0,1:T(8,128)S(1)}, f32[256,8]{0,1:T(8,128)}, u32[]{:S(2)}) copy-start(f32[256,8]{0,1:T(8,128)} %get-tuple-element.120) | copy-start | bytes 24580
  1610.3 223.6 %copy-start.85 = (s32[2048]{0:T(1024)S(1)}, s32[2048]{0:T(1024)}, u32[]{:S(2)}) copy-start(s32[2048]{0:T(1024)} %copy-done.84) | copy-start | bytes 24580
  1610.3 223.6 %copy-start.87 = (s32[2048]{0:T(1024)S(1)}, s32[2048]{0:T(1024)}, u32[]{:S(2)}) copy-start(s32[2048]{0:T(1024)} %copy-done.86) | copy-start | bytes 24580
  1610.3 223.6 %copy-start.89 = (s32[2048]{0:T(1024)S(1)}, s32[2048]{0:T(1024)}, u32[]{:S(2)}) copy-start(s32[2048]{0:T(1024)} %copy-done.88) | copy-start | bytes 24580
  1610.3 223.6 %copy-start.91 = (s32[2048]{0:T(1024)S(1)}, s32[2048]{0:T(1024)}, u32[]{:S(2)}) copy-start(s32[2048]{0:T(1024)} %copy-done.90) | copy-start | bytes 24580
  1829.7 236.2 %all-to-all-start.1 = ((bf16[32,80,2048]{2,1,0:T(8,128)(2,1)}), bf16[32,80,2048]{2,1,0:T(8,128)(2,1)}, u32[]{:S(2)}, u32[]{:S(2)}) async-start(bf16[32,80,2048]{2,1,0:T(8,128)(2,1)} %convolution_convert_fusion.3), calls=%async_computation.1 | async-start | bytes 20971520 | tf_op jit(solution)/shard_map/all_to_all | solution.py:210
  1833.4 461.4 %reduce-scatter.7.cloned.1.call-start = ((), (), s32[]{:S(2)}) async-start(), calls=%async_computation.22 | async-start | bytes 2621440 | tf_op jit(solution)/shard_map/reduce_scatter | solution.py:286
  1834.0 263.6 %copy-start.108 = (pred[2048]{0:T(1024)(128)(4,1)}, pred[2048]{0:T(1024)(128)(4,1)S(1)}, u32[]{:S(2)}) copy-start(pred[2048]{0:T(1024)(128)(4,1)S(1)} %compare_and_fusion.3) | copy-start | bytes 6148
  1834.0 253.7 %copy-start.110 = (pred[2048]{0:T(1024)(128)(4,1)}, pred[2048]{0:T(1024)(128)(4,1)S(1)}, u32[]{:S(2)}) copy-start(pred[2048]{0:T(1024)(128)(4,1)S(1)} %compare_and_fusion.2) | copy-start | bytes 6148
  2253.6 85.9 %reduce-scatter.9.cloned.1.call-start = ((), (), s32[]{:S(2)}) async-start(), calls=%async_computation.23 | async-start | bytes 2621440 | tf_op jit(solution)/shard_map/reduce_scatter | solution.py:286
  2293.2 48.3 %copy-start.49 = (f32[256,64]{0,1:T(8,128)S(1)}, f32[256,64]{0,1:T(8,128)}, u32[]{:S(2)}) copy-start(f32[256,64]{0,1:T(8,128)} %copy-done.48) | copy-start | bytes 196612
  2293.2 48.3 %copy-start.51 = (f32[256,64]{0,1:T(8,128)S(1)}, f32[256,64]{0,1:T(8,128)}, u32[]{:S(2)}) copy-start(f32[256,64]{0,1:T(8,128)} %copy-done.50) | copy-start | bytes 196612
  2294.7 46.9 %copy-start.33 = (f32[256,4,128]{0,2,1:T(8,128)S(1)}, f32[256,4,128]{0,2,1:T(8,128)}, u32[]{:S(2)}) copy-start(f32[256,4,128]{0,2,1:T(8,128)} %copy-done.32) | copy-start | bytes 1572868
  2294.7 46.9 %copy-start.35 = (f32[256,4,128]{0,2,1:T(8,128)S(1)}, f32[256,4,128]{0,2,1:T(8,128)}, u32[]{:S(2)}) copy-start(f32[256,4,128]{0,2,1:T(8,128)} %copy-done.34) | copy-start | bytes 1572868
  2294.7 46.9 %copy-start.95 = (f32[256,4]{0,1:T(4,128)S(1)}, f32[256,4]{0,1:T(4,128)}, u32[]{:S(2)}) copy-start(f32[256,4]{0,1:T(4,128)} %copy-done.94) | copy-start | bytes 12292
  2294.7 46.9 %copy-start.97 = (f32[256,4]{0,1:T(4,128)S(1)}, f32[256,4]{0,1:T(4,128)}, u32[]{:S(2)}) copy-start(f32[256,4]{0,1:T(4,128)} %copy-done.96) | copy-start | bytes 12292
  2294.8 48.5 %copy-start.112 = (f32[256,4]{0,1:T(4,128)S(1)}, f32[256,4]{0,1:T(4,128)}, u32[]{:S(2)}) copy-start(f32[256,4]{0,1:T(4,128)} %get-tuple-element.130) | copy-start | bytes 12292
  2294.8 48.5 %copy-start.113 = (f32[256,4]{0,1:T(4,128)S(1)}, f32[256,4]{0,1:T(4,128)}, u32[]{:S(2)}) copy-start(f32[256,4]{0,1:T(4,128)} %get-tuple-element.128) | copy-start | bytes 12292
  2294.8 302.4 %reduce-scatter.13.cloned.1.call-start = ((), (), s32[]{:S(2)}) async-start(), calls=%async_computation.25 | async-start | bytes 4325376 | tf_op jit(solution)/shard_map/reduce_scatter | solution.py:340
  2347.6 280.6 %reduce-scatter.15.cloned.1.call-start = ((), (), s32[]{:S(2)}) async-start(), calls=%async_computation.26 | async-start | bytes 4325376 | tf_op jit(solution)/shard_map/reduce_scatter | solution.py:341
  2352.4 628.8 %reduce-scatter.17.cloned.1.call-start = ((), (), s32[]{:S(2)}) async-start(), calls=%async_computation.27 | async-start | bytes 34603008 | tf_op jit(solution)/shard_map/reduce_scatter | solution.py:342
  2371.8 974.1 %reduce-scatter.11.cloned.1.call-start = ((), (), s32[]{:S(2)}) async-start(), calls=%async_computation.24 | async-start | bytes 34603008 | tf_op jit(solution)/shard_map/reduce_scatter | solution.py:339
  2547.3 43.4 %copy-start.137 = (f32[256]{0:T(256)S(1)}, f32[256]{0:T(256)}, u32[]{:S(2)}) copy-start(f32[256]{0:T(256)} %get-tuple-element.136) | copy-start | bytes 3076
  2594.8 751.1 %copy-start.1 = (bf16[1,768,2048]{2,1,0:T(8,128)(2,1)S(1)}, bf16[1,768,2048]{2,1,0:T(8,128)(2,1)}, u32[]{:S(2)}) copy-start(bf16[1,768,2048]{2,1,0:T(8,128)(2,1)} %param.34) | copy-start | bytes 9437188
  (120 other events, 1026.3 us)
Sparse Core Ops, SparseCore 0:
  9.9 30.5 all-gather.8
  42.4 27.9 all-gather.12
  72.5 27.9 all-gather.20
  102.3 182.3 all-gather.16
  286.7 47.5 all-gather.22
  336.1 194.9 all-gather.18
  624.2 55.0 all-gather.10
  681.4 59.9 all-gather.14
  2253.7 39.7 reduce-scatter.6
  2296.3 43.1 reduce-scatter.8
  2347.7 140.4 reduce-scatter.12
  2490.9 137.2 reduce-scatter.14
  2631.0 350.1 reduce-scatter.16
  2983.9 361.9 reduce-scatter.10
where the time goes:
time: 3370 us; the launch traced here: 3350 us
  waiting for transfers between devices  2140 us (64%)
  matrix products  599 us (18%)
  other arithmetic  265 us (8%)
  local copies, waits for them, and re-layouts  263 us (8%)
  blocking collectives  40.2 us (1%)
    all_to_all x2, waiting for transfers between devices, per_device(): lax.all_to_all(back, ('ctx', 'exp'), split_axis=0, concat_axis=0, tiled=T...  373 us
    reduce_scatter x1, waiting for transfers between devices, per_device(): lax.psum_scatter(terms[0], ('ctx', 'exp'), scatter_dimension=0, tiled=True)  365 us
    reduce_scatter x1, waiting for transfers between devices, per_device(): lax.psum_scatter(terms[3], ('ctx', 'exp'), scatter_dimension=0, tiled=True)  353 us
    all_to_all x2, waiting for transfers between devices, per_device(): lax.all_to_all(produced, ('ctx', 'exp'), split_axis=0, concat_axis=0, til...  346 us
    all_to_all x2, waiting for transfers between devices, per_device(): lax.all_to_all(sent, ('ctx', 'exp'), split_axis=0, concat_axis=0, tiled=T...  242 us
    all_to_all x2, waiting for transfers between devices, per_device(): lax.all_to_all(slot_grad, ('ctx', 'exp'), split_axis=0, concat_axis=0, ti...  234 us
  transfers between devices with their start and end apart: 22, of which 16 were waited for; matrix products, arithmetic and copies ran while one was open for 27% of the time, Pallas kernels for 0%

commit v1 on v0

v1 whole, which is shorter than its diff:
```python
import jax
import jax.numpy as jnp
from jax import lax
from jax.sharding import PartitionSpec as P

EPSILON = 1e-06
ROPE_BASE = 1000000.0
MASKED = -1e30


def norm_rows(value, gain):
    scale = lax.rsqrt(jnp.mean(value * value, -1, keepdims=True) + EPSILON)
    return (value * scale * gain, scale)


def norm_back(value, scale, gain, grad):
    inner = grad * gain
    first = scale * inner - value * (scale * scale * scale) * jnp.mean(
        inner * value, -1, keepdims=True
    )
    return (first, grad * value * scale)


def rope_tables(positions, width):
    half = width // 2
    inverse = ROPE_BASE ** (-jnp.arange(half, dtype=jnp.float32) * 2.0 / width)
    angle = positions.astype(jnp.float32)[:, None] * inverse[None, :]
    return (jnp.cos(angle), jnp.sin(angle))


def rotate(value, cosine, sine):
    half = value.shape[-1] // 2
    first = value[..., :half]
    second = value[..., half:]
    cos_b = cosine[:, None, :]
    sin_b = sine[:, None, :]
    return jnp.concatenate([first * cos_b - second * sin_b, second * cos_b + first * sin_b], -1)


def rotate_back(value, cosine, sine):
    half = value.shape[-1] // 2
    first = value[..., :half]
    second = value[..., half:]
    cos_b = cosine[:, None, :]
    sin_b = sine[:, None, :]
    return jnp.concatenate([first * cos_b + second * sin_b, second * cos_b - first * sin_b], -1)

def plane_tables(routes_all, weights_all, first, planned, capacity):
    hit = routes_all[..., None] == first + jnp.arange(planned, dtype=jnp.int32)
    named = jnp.any(hit, -2)
    weight = jnp.sum(jnp.where(hit, weights_all[..., None], 0.0), -2)
    rows = routes_all.shape[-2]
    earlier = (
        jnp.arange(rows, dtype=jnp.int32)[:, None] > jnp.arange(rows, dtype=jnp.int32)[None, :]
    ).astype(jnp.bfloat16)
    rank = jnp.einsum(
        "tu,cuj->ctj", earlier, named.astype(jnp.bfloat16), preferred_element_type=jnp.float32
    ).astype(jnp.int32)
    place = jnp.where(named, rank, -1)
    chosen = place.transpose(2, 0, 1)[:, :, None, :] == jnp.arange(capacity, dtype=jnp.int32)[
        None, None, :, None
    ]
    return chosen, weight.transpose(2, 0, 1)


def per_device(
    tokens,
    routes,
    route_weights,
    bounds,
    norm_attn,
    norm_ffn,
    q_gain,
    k_gain,
    w_q,
    w_k,
    w_v,
    w_o,
    w_gate,
    w_up,
    w_down,
    cotangent,
):
    micro = tokens.shape[0]
    local = tokens.shape[2]
    width = tokens.shape[3]
    head_dim = q_gain.shape[0]
    heads = w_q.shape[1] // head_dim
    kv_heads = w_k.shape[1] // head_dim
    group = heads // kv_heads
    top = routes.shape[3]
    ring = lax.axis_size("ctx")
    plane = lax.axis_size("exp")
    assert w_gate.shape[0] == 1
    experts = ring * plane
    capacity = max(2, local * top * 5 // (4 * experts))
    seq_len = local * ring
    scale = head_dim ** (-0.5)
    query_width = heads * head_dim
    pair_width = kv_heads * head_dim
    here = lax.axis_index("ctx")
    positions = here * local + jnp.arange(local, dtype=jnp.int32)
    every_place = jnp.arange(seq_len, dtype=jnp.int32)
    cosine, sine = rope_tables(positions, head_dim)
    in_weight = lax.all_gather(jnp.concatenate([w_q, w_k, w_v], 1), "exp", axis=0, tiled=True)
    out_weight = lax.all_gather(w_o, "exp", axis=0, tiled=True)
    query_weight = in_weight[:, :query_width]
    key_weight = in_weight[:, query_width : query_width + pair_width]
    value_weight = in_weight[:, query_width + pair_width :]
    gate_weight, up_weight, down_weight = w_gate[0], w_up[0], w_down[0]

    def dot(a, b):
        return jnp.dot(a, b, preferred_element_type=jnp.float32)

    def dot_t(a, b):
        return jnp.einsum("te,de->td", a, b, preferred_element_type=jnp.float32)

    def t_dot(a, b):
        return jnp.einsum("td,te->de", a, b, preferred_element_type=jnp.float32)

    meta = jnp.concatenate([routes[:, 0].astype(jnp.float32), route_weights[:, 0]], -1)
    meta = lax.all_gather(meta, "ctx", axis=0)
    chosen, slot_weights = [], []
    for step in range(micro):
        taken, weight = plane_tables(
            meta[:, step, :, :top].astype(jnp.int32),
            meta[:, step, :, top:],
            here * plane,
            plane,
            capacity,
        )
        chosen.append(taken)
        slot_weights.append(weight)

    def to_experts(rows, step, weighted):
        blocks = lax.all_gather(rows, "ctx", axis=0)
        picked = jnp.einsum(
            "jcst,ctd->jcsd",
            chosen[step].astype(jnp.bfloat16),
            blocks,
            preferred_element_type=jnp.float32,
        )
        if weighted:
            factor = jnp.sum(jnp.where(chosen[step], slot_weights[step][:, :, None, :], 0.0), -1)
            picked = picked * factor[..., None]
        picked = picked.astype(jnp.bfloat16).reshape(plane, ring * capacity, width)
        return lax.all_to_all(picked, "exp", split_axis=0, concat_axis=0, tiled=True).reshape(
            plane * ring * capacity, width
        )

    def from_experts(rows, step, weighted):
        back = lax.all_to_all(
            rows.reshape(plane, ring * capacity, width),
            "exp",
            split_axis=0,
            concat_axis=0,
            tiled=True,
        ).reshape(plane, ring, capacity, width)
        if weighted:
            factor = jnp.where(chosen[step], slot_weights[step][:, :, None, :], 0.0)
        else:
            factor = chosen[step]
        part = jnp.einsum(
            "jcst,jcsd->ctd",
            factor.astype(jnp.bfloat16),
            back,
            preferred_element_type=jnp.float32,
        )
        return lax.psum_scatter(
            part.astype(jnp.bfloat16).reshape(seq_len, width),
            "ctx",
            scatter_dimension=0,
            tiled=True,
        ).astype(jnp.float32)

    kept = []
    for step in range(micro):
        row = tokens[step, 0].astype(jnp.float32)
        hidden, first_scale = norm_rows(row, norm_attn)
        hidden = hidden.astype(jnp.bfloat16)
        query_raw = dot(hidden, query_weight).reshape(local, heads, head_dim)
        key_raw = dot(hidden, key_weight).reshape(local, kv_heads, head_dim)
        value_low = dot(hidden, value_weight).astype(jnp.bfloat16)
        query_normed, query_scale = norm_rows(query_raw, q_gain)
        key_normed, key_scale = norm_rows(key_raw, k_gain)
        queries = (
            rotate(query_normed, cosine, sine)
            .astype(jnp.bfloat16)
            .reshape(local, kv_heads, group, head_dim)
        )
        keys = rotate(key_normed, cosine, sine).astype(jnp.bfloat16).reshape(local, pair_width)
        both = lax.all_gather(jnp.concatenate([keys, value_low], 1), "ctx", axis=0, tiled=True)
        all_keys = both[:, :pair_width].reshape(seq_len, kv_heads, head_dim)
        all_values = both[:, pair_width:].reshape(seq_len, kv_heads, head_dim)
        bound = bounds[step, 0]
        allowed = (every_place[None, :] <= positions[:, None]) & (
            (every_place[None, :] >= bound) == (positions[:, None] >= bound)
        )
        raw = (
            jnp.einsum("qgjd,kgd->gjqk", queries, all_keys, preferred_element_type=jnp.float32)
            * scale
        )
        scores = jnp.where(allowed[None, None], raw, MASKED)
        top_score = jnp.max(scores, -1, keepdims=True)
        total = jnp.sum(jnp.exp(scores - top_score), -1, keepdims=True)
        log_total = top_score + jnp.log(total)
        chances = jnp.exp(scores - log_total).astype(jnp.bfloat16)
        attended = jnp.einsum(
            "gjqk,kgd->qgjd", chances, all_values, preferred_element_type=jnp.float32
        )
        attended = attended.reshape(local, query_width).astype(jnp.bfloat16)
        middle = row + dot(attended, out_weight)
        feed_in, second_scale = norm_rows(middle, norm_ffn)
        feed_in = feed_in.astype(jnp.bfloat16)
        kept.append(
            (
                row,
                hidden,
                first_scale,
                query_raw,
                query_scale,
                key_raw,
                key_scale,
                queries,
                all_keys,
                all_values,
                allowed,
                log_total,
                attended,
                middle,
                feed_in,
                second_scale,
            )
        )

    outputs, token_grads, value_rows = [], [], []
    received_list, active_list, incoming_list, gate_grad_list, up_grad_list = [], [], [], [], []
    hidden_list, raw_grad_list, attended_list, branch_list, gain_list = [], [], [], [], []
    for step in range(micro):
        (
            row,
            hidden,
            first_scale,
            query_raw,
            query_scale,
            key_raw,
            key_scale,
            queries,
            all_keys,
            all_values,
            allowed,
            log_total,
            attended,
            middle,
            feed_in,
            second_scale,
        ) = kept[step]
        grad = cotangent[step, 0].astype(jnp.float32)
        incoming = to_experts(cotangent[step, 0], step, True)
        received = to_experts(feed_in, step, False)
        gate = dot(received, gate_weight)
        upper = dot(received, up_weight)
        sigma = jax.nn.sigmoid(gate)
        swish = gate * sigma
        active = (swish * upper).astype(jnp.bfloat16)
        produced = dot(active, down_weight).astype(jnp.bfloat16)
        active_grad = dot_t(incoming, down_weight)
        gate_grad = (active_grad * upper * sigma * (1.0 + gate * (1.0 - sigma))).astype(
            jnp.bfloat16
        )
        upper_grad = (active_grad * swish).astype(jnp.bfloat16)
        pair_value = jnp.sum(active_grad * active.astype(jnp.float32), -1)
        back = (dot_t(gate_grad, gate_weight) + dot_t(upper_grad, up_weight)).astype(jnp.bfloat16)
        received_list.append(received)
        active_list.append(active)
        incoming_list.append(incoming)
        gate_grad_list.append(gate_grad)
        up_grad_list.append(upper_grad)
        feed_grad = from_experts(back, step, False)
        outputs.append((middle + from_experts(produced, step, True)).astype(jnp.bfloat16))
        pair_value = lax.all_to_all(
            pair_value.reshape(plane, ring * capacity),
            "exp",
            split_axis=0,
            concat_axis=0,
            tiled=True,
        ).reshape(plane, ring, capacity)
        value_rows.append(
            jnp.sum(jnp.where(chosen[step], pair_value[..., None], 0.0), 2).transpose(1, 2, 0)
        )

        middle_norm_grad, second_gain = norm_back(middle, second_scale, norm_ffn, feed_grad)
        middle_grad = grad + middle_norm_grad
        branch_grad = middle_grad.astype(jnp.bfloat16)
        attended_grad = dot_t(branch_grad, out_weight)
        attended_grad = attended_grad.astype(jnp.bfloat16).reshape(local, kv_heads, group, head_dim)
        raw = (
            jnp.einsum("qgjd,kgd->gjqk", queries, all_keys, preferred_element_type=jnp.float32)
            * scale
        )
        chances_again = jnp.exp(jnp.where(allowed[None, None], raw, MASKED) - log_total)
        chance_grad = jnp.einsum(
            "qgjd,kgd->gjqk", attended_grad, all_values, preferred_element_type=jnp.float32
        )
        score_grad = chances_again * (
            chance_grad - jnp.sum(chances_again * chance_grad, -1, keepdims=True)
        )
        score_grad = score_grad.astype(jnp.bfloat16)
        query_grad = (
            jnp.einsum("gjqk,kgd->qgjd", score_grad, all_keys, preferred_element_type=jnp.float32)
            * scale
        ).astype(jnp.bfloat16)
        key_part = (
            jnp.einsum("gjqk,qgjd->kgd", score_grad, queries, preferred_element_type=jnp.float32)
            * scale
        )
        value_part = jnp.einsum(
            "gjqk,qgjd->kgd",
            chances_again.astype(jnp.bfloat16),
            attended_grad,
            preferred_element_type=jnp.float32,
        )
        key_value_grad = lax.psum_scatter(
            jnp.concatenate(
                [key_part.reshape(seq_len, pair_width), value_part.reshape(seq_len, pair_width)], -1
            ).astype(jnp.bfloat16),
            "ctx",
            scatter_dimension=0,
            tiled=True,
        )
        key_grad = key_value_grad[:, :pair_width].astype(jnp.float32)
        value_grad = key_value_grad[:, pair_width:]
        query_grad = query_grad.astype(jnp.float32).reshape(local, heads, head_dim)
        query_turned = rotate_back(query_grad, cosine, sine)
        key_turned = rotate_back(key_grad.reshape(local, kv_heads, head_dim), cosine, sine)
        query_raw_grad, query_gain_part = norm_back(query_raw, query_scale, q_gain, query_turned)
        key_raw_grad, key_gain_part = norm_back(key_raw, key_scale, k_gain, key_turned)
        raw_grad = jnp.concatenate(
            [
                query_raw_grad.astype(jnp.bfloat16).reshape(local, query_width),
                key_raw_grad.astype(jnp.bfloat16).reshape(local, pair_width),
                value_grad,
            ],
            1,
        )
        hidden_grad = dot_t(raw_grad, in_weight)
        first_grad, first_gain = norm_back(row, first_scale, norm_attn, hidden_grad)
        token_grads.append(middle_grad + first_grad)
        gain_list.append(
            jnp.concatenate(
                [
                    jnp.sum(first_gain, 0),
                    jnp.sum(second_gain, 0),
                    jnp.sum(query_gain_part, (0, 1)),
                    jnp.sum(key_gain_part, (0, 1)),
                ]
            )
        )
        hidden_list.append(hidden)
        raw_grad_list.append(raw_grad)
        attended_list.append(attended)
        branch_list.append(branch_grad)

    def sum_over_devices(left, right):
        left = jnp.concatenate(left, 0)
        share = left.shape[1] // experts
        left = left.reshape(-1, ring, plane, share).transpose(0, 2, 1, 3)
        term = t_dot(left.reshape(-1, experts * share), jnp.concatenate(right, 0))
        term = lax.psum_scatter(
            term.astype(jnp.bfloat16), "exp", scatter_dimension=0, tiled=True
        )
        return lax.psum_scatter(term, "ctx", scatter_dimension=0, tiled=True).astype(jnp.float32)

    out_total = sum_over_devices(attended_list, branch_list)
    in_total = sum_over_devices(hidden_list, raw_grad_list)
    gain_total = lax.psum_scatter(
        sum(gain_list), ("ctx", "exp"), scatter_dimension=0, tiled=True
    )
    received_all = jnp.concatenate(received_list, 0)
    gate_term = t_dot(received_all, jnp.concatenate(gate_grad_list, 0))[None]
    up_term = t_dot(received_all, jnp.concatenate(up_grad_list, 0))[None]
    down_term = t_dot(jnp.concatenate(active_list, 0), jnp.concatenate(incoming_list, 0))[None]

    values = lax.all_to_all(
        jnp.stack(value_rows, 1), "ctx", split_axis=0, concat_axis=0, tiled=True
    )
    values = values.transpose(1, 2, 0, 3).reshape(micro, local, experts)
    match = routes[:, 0, :, :, None] == jnp.arange(experts, dtype=jnp.int32)
    route_grads = jnp.sum(jnp.where(match, values[:, :, None, :], 0.0), -1) / route_weights[:, 0]
    return (
        jnp.stack(outputs)[:, None],
        jnp.stack(token_grads)[:, None],
        route_grads[:, None],
        in_total[:, :query_width],
        in_total[:, query_width : query_width + pair_width],
        in_total[:, query_width + pair_width :],
        out_total,
        gain_total,
        gate_term,
        up_term,
        down_term,
    )


def solution(mesh):
    in_specs = (
        P(None, "exp", "ctx", None),
        P(None, "exp", "ctx", None),
        P(None, "exp", "ctx", None),
        P(None, "exp"),
        P(),
        P(),
        P(),
        P(),
        P("exp", None),
        P("exp", None),
        P("exp", None),
        P("exp", None),
        P(("ctx", "exp"), None, None),
        P(("ctx", "exp"), None, None),
        P(("ctx", "exp"), None, None),
        P(None, "exp", "ctx", None),
    )
    out_specs = (
        P(None, "exp", "ctx", None),
        P(None, "exp", "ctx", None),
        P(None, "exp", "ctx", None),
        P(("ctx", "exp"), None),
        P(("ctx", "exp"), None),
        P(("ctx", "exp"), None),
        P(("ctx", "exp"), None),
        P(("ctx", "exp")),
        P(("ctx", "exp"), None, None),
        P(("ctx", "exp"), None, None),
        P(("ctx", "exp"), None, None),
    )
    return jax.shard_map(
        per_device, mesh=mesh, in_specs=in_specs, out_specs=out_specs, check_vma=False
    )
```

time: 3370 us -> 2410 us (0.72)
  waiting for transfers between devices: 2140 us -> 1080 us
  blocking collectives: 40.2 us -> 217 us
  other arithmetic: 265 us -> 195 us
  local copies, waits for them, and re-layouts: 263 us -> 211 us
  matrix products: 599 us -> 638 us
    all_to_all x8 -> x10, waiting for transfers between devices: 1190 us -> 482 us  [the longest x3 267 us: from_experts(): lax.all_to_all(rows.reshape(plane, ring * capacity, width), 'exp', split_...]
    reduce_scatter x4 -> x8, waiting for transfers between devices: 749 us -> 138 us  [the longest x2 87.1 us: sum_over_devices(): lax.psum_scatter(term, 'ctx', scatter_dimension=0, tiled=True)]
    all_gather x8, waiting for transfers between devices: 147 us -> 453 us  [the longest x4 306 us: to_experts(): blocks = lax.all_gather(rows, 'ctx', axis=0)]
    all_to_all x0 -> x1, blocking collectives: none -> 160 us  [from_experts(): lax.all_to_all(rows.reshape(plane, ring * capacity, width), 'exp', split_...]
    gather x4 -> x0, local copies, waits for them, and re-layouts: 86.1 us -> none  [the longest x2 43.5 us: per_device(): jnp.take(returned.reshape(experts * capacity, width), slot, axis=0)]
    scatter x6 -> x0, local copies, waits for them, and re-layouts: 49 us -> none  [the longest x2 16.4 us: slot_layout(): filled = jnp.zeros((experts * capacity,), jnp.float32).at[slot].set(1.0)]
    convert_element_type x0 -> x8, local copies, waits for them, and re-layouts: none -> 47.8 us  [the longest x4 40.3 us: to_experts(): picked = picked.astype(jnp.bfloat16).reshape(plane, ring * capacity, width)]
    reduce_scatter x2, waiting for transfers between devices: 43.5 us -> 0.02 us  [per_device(): lax.psum_scatter(jnp.concatenate([key_part.reshape(seq_len, pair_width),...]
  transfers between devices with their start and end apart: 22 -> 28, of which waited for: 16 -> 20; matrix products, arithmetic and copies ran while one was open for 27% -> 28% of each run, Pallas kernels for 0% -> 0%
where the time goes in v1:
time: 2410 us; the launch traced here: 2400 us
  waiting for transfers between devices  1080 us (45%)
  matrix products  638 us (26%)
  blocking collectives  217 us (9%)
  local copies, waits for them, and re-layouts  211 us (9%)
  other arithmetic  195 us (8%)
  starting transfers between devices  49.8 us (2%)
    all_gather x4, waiting for transfers between devices, to_experts(): blocks = lax.all_gather(rows, 'ctx', axis=0)  306 us
    all_to_all x3, waiting for transfers between devices, from_experts(): lax.all_to_all(rows.reshape(plane, ring * capacity, width), 'exp', split_...  267 us
    all_to_all x4, waiting for transfers between devices, to_experts(): lax.all_to_all(picked, 'exp', split_axis=0, concat_axis=0, tiled=True)  211 us
    all_to_all x1, blocking collectives, from_experts(): lax.all_to_all(rows.reshape(plane, ring * capacity, width), 'exp', split_...  160 us
    dot_general x10, matrix products, dot_t(): return jnp.einsum('te,de->td', a, b, preferred_element_type=jnp.float32)  155 us
    dot_general x14, matrix products, dot(): return jnp.dot(a, b, preferred_element_type=jnp.float32)  132 us
    dot_general x5, matrix products, t_dot(): return jnp.einsum('td,te->de', a, b, preferred_element_type=jnp.float32)  120 us
    all_gather x1, waiting for transfers between devices, per_device(): lax.all_gather(jnp.concatenate([w_q, w_k, w_v], 1), 'exp', axis=0, tiled=...  107 us
  transfers between devices with their start and end apart: 28, of which 20 were waited for; matrix products, arithmetic and copies ran while one was open for 28% of the time, Pallas kernels for 0%

profile of v1, /device:TPU:0, one launch (start us, length us, event | category | flops | bytes accessed | tf_op | source)
XLA Modules:
  0.0 2402.3 jit_solution(4424085071508556563)
XLA Ops:
  14.5 106.8 %all-gather.14.cloned.1.call-done = bf16[2048,5120]{1,0:T(8,128)(2,1)} async-done(((bf16[256,5120]{1,0:T(8,128)(2,1)}), bf16[2048,5120]{1,0:T(8,128)(2,1)}) %all-gather.14.cloned.1.call-update) | async-done | bytes 20971536 | tf_op jit(solution)/shard_map/all_gather | solution.py:105
  145.7 14.3 slice_bitcast_fusion
  160.0 22.6 copy.169
  224.7 17.3 fusion.14
  242.0 15.4 exponential_reduce_fusion.1
  296.8 13.8 all-gather
  311.5 66.5 %all-gather.22.cloned.1.call-done = bf16[1024,2048]{1,0:T(8,128)(2,1)} async-done(((bf16[256,2048]{1,0:T(8,128)(2,1)}), bf16[1024,2048]{1,0:T(8,128)(2,1)}) %all-gather.22.cloned.1.call-update) | async-done | bytes 4194320 | tf_op jit(solution)/shard_map/all_gather | solution.py:136
  406.0 77.8 %all-gather.26.cloned.1.call-done = bf16[4,1,256,2048]{3,2,1,0:T(8,128)(2,1)} async-done(((bf16[1,1,256,2048]{3,2,1,0:T(8,128)(2,1)}), bf16[4,1,256,2048]{3,2,1,0:T(8,128)(2,1)}) %all-gather.26.cloned.1.call-update) | async-done | bytes 4194320 | tf_op jit(solution)/shard_map/all_gather | solution.py:136
  501.6 15.8 all-to-all-done
  522.7 14.1 fusion.79
  536.8 13.0 fusion.87
  549.8 89.5 %all-to-all-done.4 = bf16[8,320,2048]{2,1,0:T(8,128)(2,1)} async-done(((bf16[8,320,2048]{2,1,0:T(8,128)(2,1)}), bf16[8,320,2048]{2,1,0:T(8,128)(2,1)}, u32[]{:S(2)}, u32[]{:S(2)}) %all-to-all-start.4) | async-done | bytes 10485792 | tf_op jit(solution)/shard_map/all_to_all | solution.py:147
  639.2 20.8 multiply_reduce_fusion.1
  660.1 15.5 fusion.83
  675.6 16.5 add_convert_fusion.1
  708.4 39.4 %all-gather.20.cloned.1.call-done = bf16[1024,1024]{1,0:T(8,128)(2,1)} async-done(((bf16[256,1024]{1,0:T(8,128)(2,1)}), bf16[1024,1024]{1,0:T(8,128)(2,1)}) %all-gather.20.cloned.1.call-update) | async-done | bytes 2097168 | tf_op jit(solution)/shard_map/all_gather | solution.py:192
  757.5 56.5 %all-to-all-done.5 = bf16[8,320,2048]{2,1,0:T(8,128)(2,1)} async-done(((bf16[8,320,2048]{2,1,0:T(8,128)(2,1)}), bf16[8,320,2048]{2,1,0:T(8,128)(2,1)}, u32[]{:S(2)}, u32[]{:S(2)}) %all-to-all-start.5) | async-done | bytes 10485792 | tf_op jit(solution)/shard_map/all_to_all | solution.py:152
  824.3 16.8 fusion.15
  841.1 15.1 exponential_reduce_fusion
  902.1 81.3 %all-gather.24.cloned.1.call-done = bf16[1024,2048]{1,0:T(8,128)(2,1)} async-done(((bf16[256,2048]{1,0:T(8,128)(2,1)}), bf16[1024,2048]{1,0:T(8,128)(2,1)}) %all-gather.24.cloned.1.call-update) | async-done | bytes 4194320 | tf_op jit(solution)/shard_map/all_gather | solution.py:136
  1007.9 80.9 %all-gather.28.cloned.1.call-done = bf16[4,1,256,2048]{3,2,1,0:T(8,128)(2,1)} async-done(((bf16[1,1,256,2048]{3,2,1,0:T(8,128)(2,1)}), bf16[4,1,256,2048]{3,2,1,0:T(8,128)(2,1)}) %all-gather.28.cloned.1.call-update) | async-done | bytes 4194320 | tf_op jit(solution)/shard_map/all_gather | solution.py:136
  1106.5 16.6 all-to-all-done.2
  1128.6 14.1 fusion.77
  1142.7 13.1 fusion.85
  1155.8 89.4 %all-to-all-done.6 = bf16[8,320,2048]{2,1,0:T(8,128)(2,1)} async-done(((bf16[8,320,2048]{2,1,0:T(8,128)(2,1)}), bf16[8,320,2048]{2,1,0:T(8,128)(2,1)}, u32[]{:S(2)}, u32[]{:S(2)}) %all-to-all-start.6) | async-done | bytes 10485792 | tf_op jit(solution)/shard_map/all_to_all | solution.py:147
  1245.1 21.0 multiply_reduce_fusion
  1266.1 15.2 fusion.81
  1281.3 16.5 add_convert_fusion
  1303.1 13.0 convolution_convert_fusion.2
  1316.1 103.5 %all-to-all-done.7 = bf16[8,320,2048]{2,1,0:T(8,128)(2,1)} async-done(((bf16[8,320,2048]{2,1,0:T(8,128)(2,1)}), bf16[8,320,2048]{2,1,0:T(8,128)(2,1)}, u32[]{:S(2)}, u32[]{:S(2)}) %all-to-all-start.7) | async-done | bytes 10485792 | tf_op jit(solution)/shard_map/all_to_all | solution.py:152
  1434.8 106.6 %all-to-all-done.3 = bf16[8,320,2048]{2,1,0:T(8,128)(2,1)} async-done(((bf16[8,320,2048]{2,1,0:T(8,128)(2,1)}), bf16[8,320,2048]{2,1,0:T(8,128)(2,1)}, u32[]{:S(2)}, u32[]{:S(2)}) %all-to-all-start.3) | async-done | bytes 10485792 | tf_op jit(solution)/shard_map/all_to_all | solution.py:152
  1550.9 23.8 copy.202
  1574.7 23.6 copy.193
  1601.5 23.0 reduce-scatter.13.cloned.1.call-done
  1645.4 29.0 %fusion = (f32[4,8,256]{2,1,0:T(8,128)S(1)}, f32[4,1024,256,8]{2,1,3,0:T(8,128)}) fusion(f32[4,1024,256,8]{2,1,3,0:T(8,128)} %get-tuple-element.184, f32[4,8,256]{2,1,0:T(8,128)S(1)} %copy-done.45, pred[256,1024]{0,1:T(8,128)(4,1)S(1)} %copy-done.6, bf16[256,4,8,128]{3,2,1,0:T(8,128)(2,1)} %bitcast.440, bf16[1024,4,128,1]{2,1,0,3:T(4,128)(2,1)} %bitcast.455), kind=kOutput, calls=%fused_computation.2 | convolution fusion | flops 2189418496 | bytes 70582272 | tf_op jit(solution)/shard_map/qgjd,kgd->gjqk/dot_general | solution.py:302
  1699.7 29.2 %fusion.3 = (f32[4,8,256]{2,1,0:T(8,128)S(1)}, f32[4,1024,256,8]{2,1,3,0:T(8,128)}) fusion(f32[4,1024,256,8]{2,1,3,0:T(8,128)} %get-tuple-element.180, f32[4,8,256]{2,1,0:T(8,128)S(1)} %copy-done.43, pred[256,1024]{0,1:T(8,128)(4,1)} %copy-done.7, bf16[256,4,8,128]{3,2,1,0:T(8,128)(2,1)} %bitcast.442, bf16[1024,4,128,1]{2,1,0,3:T(4,128)(2,1)} %bitcast.453), kind=kOutput, calls=%fused_computation.7 | convolution fusion | flops 2189418496 | bytes 70582272 | tf_op jit(solution)/shard_map/qgjd,kgd->gjqk/dot_general | solution.py:302
  1738.7 28.1 %fusion.5 = bf16[4,8,256,1024]{2,3,1,0:T(8,128)(2,1)} fusion(f32[4,1024,256,8]{2,1,3,0:T(8,128)} %get-tuple-element.188, f32[4,1024,256,8]{2,1,3,0:T(8,128)} %get-tuple-element.180, f32[4,8,256]{2,1,0:T(8,128)S(1)} %get-tuple-element.187, f32[4,8,256]{2,1,0:T(8,128)S(1)} %copy-done.43, pred[256,1024]{0,1:T(8,128)(4,1)} %copy-done.7), kind=kLoop, calls=%fused_computation.9 | loop fusion | flops 50331648 | bytes 84213760 | tf_op jit(solution)/shard_map/convert_element_type | solution.py:308
  1779.4 28.5 %fusion.2 = bf16[4,8,256,1024]{2,3,1,0:T(8,128)(2,1)} fusion(f32[4,1024,256,8]{2,1,3,0:T(8,128)} %get-tuple-element.190, f32[4,1024,256,8]{2,1,3,0:T(8,128)} %get-tuple-element.184, f32[4,8,256]{2,1,0:T(8,128)S(1)} %get-tuple-element.189, f32[4,8,256]{2,1,0:T(8,128)S(1)} %copy-done.45, pred[256,1024]{0,1:T(8,128)(4,1)S(1)} %copy-done.6), kind=kLoop, calls=%fused_computation.4 | loop fusion | flops 50331648 | bytes 84213760 | tf_op jit(solution)/shard_map/convert_element_type | solution.py:308
  1891.1 27.1 %convolution_convert_fusion = bf16[2048,5120]{1,0:T(8,128)(2,1)} fusion(bf16[512,2048]{0,1:T(8,128)(2,1)} %bitcast.478, bf16[256,512]{0,1:T(8,128)(2,1)} %get-tuple-element.121, bf16[256,512]{0,1:T(8,128)(2,1)S(1)} %bitcast.488, bf16[256,4096]{0,1:T(8,128)(2,1)S(1)} %bitcast.477, bf16[256,512]{0,1:T(8,128)(2,1)S(1)} %copy-done.56, ...), kind=kOutput, calls=%fused_computation.29 | convolution fusion | flops 10779361280 | bytes 28311552 | tf_op jit(solution)/shard_map/td,te->de/dot_general | solution.py:119
  1918.3 13.2 convolution_convert_fusion.3
  1931.6 160.3 %all_to_all.63 = bf16[8,320,2048]{2,1,0:T(8,128)(2,1)S(1)} all-to-all(bf16[8,320,2048]{2,1,0:T(8,128)(2,1)} %bitcast.452), channel_id=1, replica_groups=mesh['ctx'=4,'exp'=8] {'exp'}, dimensions={0} | all-to-all | bytes 20971520 | tf_op jit(solution)/shard_map/all_to_all | solution.py:152
  2111.4 27.8 %fusion.58 = f32[1,2048,768]{2,1,0:T(8,128)} fusion(bf16[2560,768]{1,0:T(8,128)(2,1)} %get-tuple-element.84, bf16[2560,768]{1,0:T(8,128)(2,1)} %get-tuple-element.83, bf16[2560,2048]{1,0:T(8,128)(2,1)} %bitcast.64, bf16[2560,2048]{1,0:T(8,128)(2,1)} %bitcast.31), kind=kOutput, calls=%fused_computation.104 | convolution fusion | flops 16163799040 | bytes 35127296 | tf_op jit(solution)/shard_map/td,te->de/dot_general | solution.py:119
  2139.2 27.0 %fusion.61 = f32[1,2048,768]{2,1,0:T(8,128)} fusion(bf16[2560,768]{1,0:T(8,128)(2,1)} %get-tuple-element.86, bf16[2560,768]{1,0:T(8,128)(2,1)} %get-tuple-element.85, bf16[2560,2048]{1,0:T(8,128)(2,1)} %bitcast.64, bf16[2560,2048]{1,0:T(8,128)(2,1)} %bitcast.31), kind=kOutput, calls=%fused_computation.105 | convolution fusion | flops 16163799040 | bytes 35127296 | tf_op jit(solution)/shard_map/td,te->de/dot_general | solution.py:119
  2172.4 26.3 %fusion.64 = f32[1,768,2048]{2,1,0:T(8,128)} fusion(bf16[2560,2048]{1,0:T(8,128)(2,1)} %bitcast.109, bf16[2560,2048]{1,0:T(8,128)(2,1)} %bitcast.79, bf16[2560,768]{1,0:T(8,128)(2,1)} %get-tuple-element.82, bf16[2560,768]{1,0:T(8,128)(2,1)} %get-tuple-element.80), kind=kOutput, calls=%fused_computation.106 | convolution fusion | flops 16163799040 | bytes 35127296 | tf_op jit(solution)/shard_map/td,te->de/dot_general | solution.py:119
  2222.5 13.4 fusion.145
  2236.0 42.6 %all-reduce = f32[4352]{0:T(1024)S(1)} all-reduce(f32[4352]{0:T(1024)S(1)} %maximum_add_fusion), channel_id=17, replica_groups=mesh['ctx'=4,'exp'=8] {'ctx','exp'}, use_global_device_ids=true, to_apply=%region_51.52.clone | all-reduce | flops 4352 | bytes 34816
  2302.4 35.5 %reduce-scatter.29.cloned.1.call-done = bf16[128,2048]{1,0:T(8,128)(2,1)} async-done(((bf16[512,2048]{1,0:T(8,128)(2,1)}), bf16[128,2048]{1,0:T(8,128)(2,1)}) %reduce-scatter.29.cloned.1.call-update) | async-done | bytes 524304 | tf_op jit(solution)/shard_map/reduce_scatter | solution.py:372
  2339.9 51.6 %reduce-scatter.25.cloned.1.call-done = bf16[64,5120]{1,0:T(8,128)(2,1)} async-done(((bf16[256,5120]{1,0:T(8,128)(2,1)}), bf16[64,5120]{1,0:T(8,128)(2,1)}) %reduce-scatter.25.cloned.1.call-update) | async-done | bytes 655376 | tf_op jit(solution)/shard_map/reduce_scatter | solution.py:372
  (458 shorter events, 558.0 us)
Async XLA Ops:
  7.2 632.1 %copy-start = (bf16[1,768,2048]{2,1,0:T(8,128)(2,1)S(1)}, bf16[1,768,2048]{2,1,0:T(8,128)(2,1)}, u32[]{:S(2)}) copy-start(bf16[1,768,2048]{2,1,0:T(8,128)(2,1)} %param.30) | copy-start | bytes 9437188
  7.2 114.1 %all-gather.14.cloned.1.call-start = ((), (), s32[]{:S(2)}) async-start(), calls=%async_computation.21 | async-start | bytes 23592960 | tf_op jit(solution)/shard_map/all_gather | solution.py:105
  10.9 204.1 %all-gather.16.cloned.1.call-start = ((), (), s32[]{:S(2)}) async-start(), calls=%async_computation.22 | async-start | bytes 2621440 | tf_op jit(solution)/shard_map/all_gather | solution.py:192
  14.2 168.5 %copy-start.101 = (f32[256]{0:T(256)}, f32[256]{0:T(256)S(1)}, u32[]{:S(2)}) copy-start(f32[256]{0:T(256)S(1)} %get-tuple-element.150) | copy-start | bytes 3076
  14.2 178.2 %copy-start.105 = (f32[256]{0:T(256)}, f32[256]{0:T(256)S(1)}, u32[]{:S(2)}) copy-start(f32[256]{0:T(256)S(1)} %get-tuple-element.198) | copy-start | bytes 3076
  14.5 191.5 %copy-start.34 = (f32[256,64]{0,1:T(8,128)}, f32[256,64]{0,1:T(8,128)S(1)}, u32[]{:S(2)}) copy-start(f32[256,64]{0,1:T(8,128)S(1)} %get-tuple-element.145) | copy-start | bytes 196612
  14.5 191.5 %copy-start.36 = (f32[256,64]{0,1:T(8,128)}, f32[256,64]{0,1:T(8,128)S(1)}, u32[]{:S(2)}) copy-start(f32[256,64]{0,1:T(8,128)S(1)} %get-tuple-element.146) | copy-start | bytes 196612
  14.5 113.8 %copy-start.68 = (f32[2048]{0:T(1024)S(1)}, f32[2048]{0:T(1024)}, u32[]{:S(2)}) copy-start(f32[2048]{0:T(1024)} %param.20) | copy-start | bytes 24580
  139.5 143.5 %all-gather.18.cloned.1.call-start = ((), (), s32[]{:S(2)}) async-start(), calls=%async_computation.23 | async-start | bytes 18874368 | tf_op jit(solution)/shard_map/all_gather | solution.py:106
  140.2 237.7 %all-gather.22.cloned.1.call-start = ((), (), s32[]{:S(2)}) async-start(), calls=%async_computation.35 | async-start | bytes 5242880 | tf_op jit(solution)/shard_map/all_gather | solution.py:136
  145.7 111.6 %copy-start.7 = (pred[256,1024]{0,1:T(8,128)(4,1)}, pred[256,1024]{0,1:T(8,128)(4,1)S(1)}, u32[]{:S(2)}) copy-start(pred[256,1024]{0,1:T(8,128)(4,1)S(1)} %get-tuple-element.155) | copy-start | bytes 786436
  311.5 172.3 %copy-start.59 = (s32[8,4,256]{2,0,1:T(8,128)}, s32[8,4,256]{2,0,1:T(8,128)S(1)}, u32[]{:S(2)}) copy-start(s32[8,4,256]{2,0,1:T(8,128)S(1)} %fusion.177) | copy-start | bytes 98308
  395.7 121.7 %all-to-all-start = ((bf16[8,320,2048]{2,1,0:T(8,128)(2,1)}), bf16[8,320,2048]{2,1,0:T(8,128)(2,1)}, u32[]{:S(2)}, u32[]{:S(2)}) async-start(bf16[8,320,2048]{2,1,0:T(8,128)(2,1)} %bitcast.432), calls=%async_computation | async-start | bytes 20971520 | tf_op jit(solution)/shard_map/all_to_all | solution.py:147
  400.8 83.0 %all-gather.26.cloned.1.call-start = ((), (), s32[]{:S(2)}) async-start(), calls=%async_computation.37 | async-start | bytes 5242880 | tf_op jit(solution)/shard_map/all_gather | solution.py:136
  517.4 121.9 %all-to-all-start.4 = ((bf16[8,320,2048]{2,1,0:T(8,128)(2,1)}), bf16[8,320,2048]{2,1,0:T(8,128)(2,1)}, u32[]{:S(2)}, u32[]{:S(2)}) async-start(bf16[8,320,2048]{2,1,0:T(8,128)(2,1)} %bitcast.434), calls=%async_computation.6 | async-start | bytes 20971520 | tf_op jit(solution)/shard_map/all_to_all | solution.py:147
  692.1 121.9 %all-to-all-start.5 = ((bf16[8,320,2048]{2,1,0:T(8,128)(2,1)}), bf16[8,320,2048]{2,1,0:T(8,128)(2,1)}, u32[]{:S(2)}, u32[]{:S(2)}) async-start(bf16[8,320,2048]{2,1,0:T(8,128)(2,1)} %bitcast.448), calls=%async_computation.7 | async-start | bytes 20971520 | tf_op jit(solution)/shard_map/all_to_all | solution.py:152
  697.4 50.4 %all-gather.20.cloned.1.call-start = ((), (), s32[]{:S(2)}) async-start(), calls=%async_computation.25 | async-start | bytes 2621440 | tf_op jit(solution)/shard_map/all_gather | solution.py:192
  702.9 194.1 %reduce-scatter.15.cloned.1.call-start = ((), (), s32[]{:S(2)}) async-start(), calls=%async_computation.27 | async-start | bytes 5242880 | tf_op jit(solution)/shard_map/reduce_scatter | solution.py:169
  750.8 63.2 %copy-start.60 = (s32[8,4,256]{2,0,1:T(8,128)S(1)}, s32[8,4,256]{2,0,1:T(8,128)}, u32[]{:S(2)}) copy-start(s32[8,4,256]{2,0,1:T(8,128)} %copy-done.59) | copy-start | bytes 98308
  823.4 159.9 %all-gather.24.cloned.1.call-start = ((), (), s32[]{:S(2)}) async-start(), calls=%async_computation.36 | async-start | bytes 5242880 | tf_op jit(solution)/shard_map/all_gather | solution.py:136
  902.1 639.2 %copy-start.62 = (s32[8,4,256]{2,0,1:T(8,128)}, s32[8,4,256]{2,0,1:T(8,128)S(1)}, u32[]{:S(2)}) copy-start(s32[8,4,256]{2,0,1:T(8,128)S(1)} %fusion.175) | copy-start | bytes 98308
  1001.2 121.8 %all-to-all-start.2 = ((bf16[8,320,2048]{2,1,0:T(8,128)(2,1)}), bf16[8,320,2048]{2,1,0:T(8,128)(2,1)}, u32[]{:S(2)}, u32[]{:S(2)}) async-start(bf16[8,320,2048]{2,1,0:T(8,128)(2,1)} %bitcast.433), calls=%async_computation.3 | async-start | bytes 20971520 | tf_op jit(solution)/shard_map/all_to_all | solution.py:147
  1006.5 82.2 %all-gather.28.cloned.1.call-start = ((), (), s32[]{:S(2)}) async-start(), calls=%async_computation.38 | async-start | bytes 5242880 | tf_op jit(solution)/shard_map/all_gather | solution.py:136
  1123.0 122.1 %all-to-all-start.6 = ((bf16[8,320,2048]{2,1,0:T(8,128)(2,1)}), bf16[8,320,2048]{2,1,0:T(8,128)(2,1)}, u32[]{:S(2)}, u32[]{:S(2)}) async-start(bf16[8,320,2048]{2,1,0:T(8,128)(2,1)} %bitcast.435), calls=%async_computation.10 | async-start | bytes 20971520 | tf_op jit(solution)/shard_map/all_to_all | solution.py:147
  1297.9 121.8 %all-to-all-start.7 = ((bf16[8,320,2048]{2,1,0:T(8,128)(2,1)}), bf16[8,320,2048]{2,1,0:T(8,128)(2,1)}, u32[]{:S(2)}, u32[]{:S(2)}) async-start(bf16[8,320,2048]{2,1,0:T(8,128)(2,1)} %bitcast.450), calls=%async_computation.11 | async-start | bytes 20971520 | tf_op jit(solution)/shard_map/all_to_all | solution.py:152
  1419.6 121.7 %all-to-all-start.3 = ((bf16[8,320,2048]{2,1,0:T(8,128)(2,1)}), bf16[8,320,2048]{2,1,0:T(8,128)(2,1)}, u32[]{:S(2)}, u32[]{:S(2)}) async-start(bf16[8,320,2048]{2,1,0:T(8,128)(2,1)} %bitcast.449), calls=%async_computation.4 | async-start | bytes 20971520 | tf_op jit(solution)/shard_map/all_to_all | solution.py:152
  1424.8 173.5 %reduce-scatter.19.cloned.1.call-start = ((), (), s32[]{:S(2)}) async-start(), calls=%async_computation.29 | async-start | bytes 5242880 | tf_op jit(solution)/shard_map/reduce_scatter | solution.py:169
  1434.7 106.6 %copy-start.67 = (f32[4,256,8]{1,2,0:T(8,128)S(1)}, f32[4,256,8]{1,2,0:T(8,128)}, u32[]{:S(2)}) copy-start(f32[4,256,8]{1,2,0:T(8,128)} %get-tuple-element.76) | copy-start | bytes 98308
  1434.7 189.8 %reduce-scatter.13.cloned.1.call-start = ((), (), s32[]{:S(2)}) async-start(), calls=%async_computation.26 | async-start | bytes 5242880 | tf_op jit(solution)/shard_map/reduce_scatter | solution.py:169
  1550.8 331.5 %reduce-scatter.17.cloned.1.call-start = ((), (), s32[]{:S(2)}) async-start(), calls=%async_computation.28 | async-start | bytes 2621440 | tf_op jit(solution)/shard_map/reduce_scatter | solution.py:323
  1574.7 49.8 %copy-start.84 = (f32[256]{0:T(256)S(1)}, f32[256]{0:T(256)}, u32[]{:S(2)}) copy-start(f32[256]{0:T(256)} %copy-done.82) | copy-start | bytes 3076
  1574.7 49.8 %copy-start.93 = (f32[256]{0:T(256)S(1)}, f32[256]{0:T(256)}, u32[]{:S(2)}) copy-start(f32[256]{0:T(256)} %get-tuple-element.151) | copy-start | bytes 3076
  1779.4 105.7 %reduce-scatter.21.cloned.1.call-start = ((), (), s32[]{:S(2)}) async-start(), calls=%async_computation.30 | async-start | bytes 2621440 | tf_op jit(solution)/shard_map/reduce_scatter | solution.py:323
  1820.5 318.7 %reduce-scatter.27.cloned.1.call-start = ((), (), s32[]{:S(2)}) async-start(), calls=%async_computation.33 | async-start | bytes 18874368 | tf_op jit(solution)/shard_map/reduce_scatter | solution.py:369
  1836.5 374.1 %reduce-scatter.23.cloned.1.call-start = ((), (), s32[]{:S(2)}) async-start(), calls=%async_computation.31 | async-start | bytes 23592960 | tf_op jit(solution)/shard_map/reduce_scatter | solution.py:369
  1918.3 373.0 %reduce-scatter.11.cloned.1.call-start = ((), (), s32[]{:S(2)}) async-start(), calls=%async_computation.24 | async-start | bytes 5242880 | tf_op jit(solution)/shard_map/reduce_scatter | solution.py:169
  1931.5 160.3 %copy-start.61 = (s32[8,4,256]{2,0,1:T(8,128)S(1)}, s32[8,4,256]{2,0,1:T(8,128)}, u32[]{:S(2)}) copy-start(s32[8,4,256]{2,0,1:T(8,128)} %copy-done.59) | copy-start | bytes 98308
  1931.5 160.3 %copy-start.65 = (f32[4,256,8]{1,2,0:T(8,128)S(1)}, f32[4,256,8]{1,2,0:T(8,128)}, u32[]{:S(2)}) copy-start(f32[4,256,8]{1,2,0:T(8,128)} %copy-done.64) | copy-start | bytes 98308
  2098.3 8.0 all-to-all-start.8
  2108.0 58.3 %all-to-all-start.9 = ((f32[8,1,320]{2,1,0:T(1,128)}), f32[8,1,320]{2,1,0:T(1,128)S(1)}, u32[]{:S(2)}, u32[]{:S(2)}) async-start(f32[8,1,320]{2,1,0:T(1,128)} %all_to_all.49), calls=%async_computation.15 | async-start | bytes 24576 | tf_op jit(solution)/shard_map/all_to_all | solution.py:281
  2111.3 226.5 %reduce-scatter.29.cloned.1.call-start = ((), (), s32[]{:S(2)}) async-start(), calls=%async_computation.34 | async-start | bytes 2621440 | tf_op jit(solution)/shard_map/reduce_scatter | solution.py:372
  2167.8 30.9 %all-to-all-start.10 = ((f32[4,2,256,8]{2,3,1,0:T(8,128)}), f32[4,2,256,8]{2,3,1,0:T(8,128)S(1)}, u32[]{:S(2)}, u32[]{:S(2)}) async-start(f32[4,2,256,8]{2,3,1,0:T(8,128)} %pad_maximum_fusion.24), calls=%async_computation.16 | async-start | bytes 131072 | tf_op jit(solution)/shard_map/all_to_all | solution.py:384
  2172.4 219.2 %reduce-scatter.25.cloned.1.call-start = ((), (), s32[]{:S(2)}) async-start(), calls=%async_computation.32 | async-start | bytes 3276800 | tf_op jit(solution)/shard_map/reduce_scatter | solution.py:372
  2222.4 68.9 %copy-start.54 = (f32[2048]{0:T(1024)S(1)}, f32[2048]{0:T(1024)}, u32[]{:S(2)}) copy-start(f32[2048]{0:T(1024)} %param.21) | copy-start | bytes 24580
  2222.4 68.9 %copy-start.85 = (f32[256]{0:T(256)S(1)}, f32[256]{0:T(256)}, u32[]{:S(2)}) copy-start(f32[256]{0:T(256)} %copy-done.82) | copy-start | bytes 3076
  2222.4 68.8 %copy-start.94 = (f32[256]{0:T(256)S(1)}, f32[256]{0:T(256)}, u32[]{:S(2)}) copy-start(f32[256]{0:T(256)} %get-tuple-element.151) | copy-start | bytes 3076
  2222.4 68.8 %copy-start.100 = (f32[256]{0:T(256)S(1)}, f32[256]{0:T(256)}, u32[]{:S(2)}) copy-start(f32[256]{0:T(256)} %copy-done.99) | copy-start | bytes 3076
  2222.4 68.8 %copy-start.115 = (f32[256]{0:T(256)S(1)}, f32[256]{0:T(256)}, u32[]{:S(2)}) copy-start(f32[256]{0:T(256)} %get-tuple-element.199) | copy-start | bytes 3076
  (107 other events, 952.0 us)
Sparse Core Ops, SparseCore 0:
  11.0 110.2 all-gather.13
  139.6 45.9 all-gather.15
  187.5 88.5 all-gather.17
  296.8 81.0 all-gather.21
  404.1 79.5 all-gather.25
  703.0 44.7 all-gather.19
  823.5 73.3 reduce-scatter.14
  902.0 81.2 all-gather.23
  1009.0 79.7 all-gather.27
  1434.9 75.6 reduce-scatter.18
  1550.9 73.5 reduce-scatter.12
  1779.5 44.3 reduce-scatter.16
  1826.7 43.1 reduce-scatter.20
  1873.8 196.3 reduce-scatter.26
  2074.1 136.4 reduce-scatter.22
  2213.4 77.7 reduce-scatter.10
  2293.4 44.3 reduce-scatter.28
  2340.1 51.4 reduce-scatter.24

commit v2 on v1

v2 whole, which is shorter than its diff:
```python
import functools
import math

import jax
import jax.numpy as jnp
from jax import lax
from jax.experimental import pallas as pl
from jax.experimental.pallas import tpu as pltpu
from jax.sharding import PartitionSpec as P

EPSILON = 1e-06
ROPE_BASE = 1000000.0
MASKED = -1e30
VMEM_BYTES = 56 * 2**20


def norm_rows(value, gain):
    scale = lax.rsqrt(jnp.mean(value * value, -1, keepdims=True) + EPSILON)
    return (value * scale * gain, scale)


def norm_back(value, scale, gain, grad):
    inner = grad * gain
    first = scale * inner - value * (scale * scale * scale) * jnp.mean(
        inner * value, -1, keepdims=True
    )
    return (first, grad * value * scale)


def rope_tables(positions, width):
    half = width // 2
    inverse = ROPE_BASE ** (-jnp.arange(half, dtype=jnp.float32) * 2.0 / width)
    angle = positions.astype(jnp.float32)[:, None] * inverse[None, :]
    cosine, sine = jnp.cos(angle), jnp.sin(angle)
    return (jnp.concatenate([cosine, cosine], -1), jnp.concatenate([-sine, sine], -1))


def swap_halves(value):
    half = value.shape[-1] // 2
    return jnp.concatenate([value[..., half:], value[..., :half]], -1)


def nothing_kernel(*refs):
    pass


def after(value, *others):
    return pl.pallas_call(
        nothing_kernel,
        in_specs=[pl.BlockSpec(memory_space=pl.ANY)] * (1 + len(others)),
        out_specs=pl.BlockSpec(memory_space=pl.ANY),
        out_shape=jax.ShapeDtypeStruct(value.shape, value.dtype),
        input_output_aliases={0: 0},
    )(value, *others)


def gather_kernel(count, arrays, *refs):
    own, full = refs[:arrays], refs[arrays : 2 * arrays]
    send_sem, recv_sem, own_sem = refs[2 * arrays :]
    me = lax.axis_index("ctx")
    barrier = pltpu.get_barrier_semaphore()
    for other in (lax.rem(me + 1, count), lax.rem(me + count - 1, count)):
        pl.semaphore_signal(
            barrier, inc=1, device_id={"ctx": other}, device_id_type=pl.DeviceIdType.MESH
        )
    pl.semaphore_wait(barrier, 2)

    def block(i, at):
        rows = own[i].shape[0]
        return full[i].at[pl.ds(at * rows, rows)]

    def passing(way, step, i, at):
        return pltpu.make_async_remote_copy(
            src_ref=own[i] if step == 0 else block(i, at),
            dst_ref=block(i, at),
            send_sem=send_sem.at[way, step, i],
            recv_sem=recv_sem.at[way, step, i],
            device_id={"ctx": me + (1 if way == 0 else -1)},
            device_id_type=pl.DeviceIdType.MESH,
        )

    def sends(way, step):
        if way == 0:
            return (me >= step) & (me < count - 1)
        return (me + step < count) & (me > 0)

    def receives(way, step):
        return me >= step + 1 if way == 0 else me + step + 1 < count

    kept = [pltpu.make_async_copy(own[i], block(i, me), own_sem.at[i]) for i in range(arrays)]
    for step in range(count - 1):
        for i in range(arrays):
            for way in (0, 1):
                sign = 1 if way == 0 else -1

                @pl.when(sends(way, step))
                def _():
                    passing(way, step, i, me - sign * step).start()

        if step == 0:
            for copy in kept:
                copy.start()
        for i in range(arrays):
            for way in (0, 1):
                sign = 1 if way == 0 else -1

                @pl.when(receives(way, step))
                def _():
                    passing(way, step, i, me - sign * (step + 1)).wait_recv()

    for copy in kept:
        copy.wait()
    for step in range(count - 1):
        for i in range(arrays):
            for way in (0, 1):
                sign = 1 if way == 0 else -1

                @pl.when(sends(way, step))
                def _():
                    passing(way, step, i, me - sign * step).wait_send()


def line_gather(*blocks):
    count = lax.axis_size("ctx")
    arrays = len(blocks)
    return pl.pallas_call(
        functools.partial(gather_kernel, count, arrays),
        in_specs=[pl.BlockSpec(memory_space=pl.ANY)] * arrays,
        out_specs=[pl.BlockSpec(memory_space=pl.ANY)] * arrays,
        out_shape=[
            jax.ShapeDtypeStruct((count * block.shape[0],) + block.shape[1:], block.dtype)
            for block in blocks
        ],
        scratch_shapes=[
            pltpu.SemaphoreType.DMA((2, count - 1, arrays)),
            pltpu.SemaphoreType.DMA((2, count - 1, arrays)),
            pltpu.SemaphoreType.DMA((arrays,)),
        ],
        compiler_params=pltpu.CompilerParams(collective_id=0, has_side_effects=True),
        cost_estimate=pl.CostEstimate(flops=0, bytes_accessed=200 * 2**20, transcendentals=0),
    )(*blocks)


def expert_kernel(
    rows_ref,
    grad_ref,
    gate_ref,
    up_ref,
    down_ref,
    active_ref,
    gate_grad_ref,
    up_grad_ref,
    out_ref,
    back_ref,
    value_ref,
):
    gate = along(rows_ref[...], gate_ref[...])
    upper = along(rows_ref[...], up_ref[...])
    active_grad = across(grad_ref[...], down_ref[...])
    sigma = jax.nn.sigmoid(gate)
    swish = gate * sigma
    active = (swish * upper).astype(jnp.bfloat16)
    active_ref[...] = active
    out_ref[...] = along(active, down_ref[...]).astype(jnp.bfloat16)
    gate_grad = (active_grad * upper * sigma * (1.0 + gate * (1.0 - sigma))).astype(jnp.bfloat16)
    up_grad = (active_grad * swish).astype(jnp.bfloat16)
    gate_grad_ref[...] = gate_grad
    up_grad_ref[...] = up_grad
    value_ref[...] = jnp.sum(active_grad * active.astype(jnp.float32), -1, keepdims=True)
    back_ref[...] = (across(gate_grad, gate_ref[...]) + across(up_grad, up_ref[...])).astype(
        jnp.bfloat16
    )


def run_expert(rows, grad, gate, up, down):
    total, width = rows.shape
    units = gate.shape[1]
    block = 256 if total % 256 == 0 else total
    wide = pl.BlockSpec((block, width), lambda i: (i, 0))
    narrow = pl.BlockSpec((block, units), lambda i: (i, 0))

    def whole(shape):
        return pl.BlockSpec(shape, lambda i: (0, 0), pipeline_mode=pl.Buffered(1))

    low = jax.ShapeDtypeStruct((total, units), jnp.bfloat16)
    full = jax.ShapeDtypeStruct((total, width), jnp.bfloat16)
    return pl.pallas_call(
        expert_kernel,
        grid=(total // block,),
        in_specs=[wide, wide, whole(gate.shape), whole(up.shape), whole(down.shape)],
        out_specs=(narrow, narrow, narrow, wide, wide, pl.BlockSpec((block, 1), lambda i: (i, 0))),
        out_shape=(low, low, low, full, full, jax.ShapeDtypeStruct((total, 1), jnp.float32)),
        compiler_params=pltpu.CompilerParams(vmem_limit_bytes=VMEM_BYTES),
        cost_estimate=pl.CostEstimate(
            flops=14 * total * width * units,
            bytes_accessed=8 * total * width,
            transcendentals=total * units,
        ),
    )(rows, grad, gate, up, down)


def plane_tables(routes_all, weights_all, first, planned):
    hit = routes_all[..., None] == first + jnp.arange(planned, dtype=jnp.int32)
    named = jnp.any(hit, -2)
    weight = jnp.sum(jnp.where(hit, weights_all[..., None], 0.0), -2)
    rows = routes_all.shape[-2]
    earlier = (
        jnp.arange(rows, dtype=jnp.int32)[:, None] > jnp.arange(rows, dtype=jnp.int32)[None, :]
    ).astype(jnp.bfloat16)
    rank = jnp.einsum(
        "tu,cuj->ctj", earlier, named.astype(jnp.bfloat16), preferred_element_type=jnp.float32
    ).astype(jnp.int32)
    place = jnp.where(named, rank, -1)
    return place.transpose(0, 2, 1), weight.transpose(0, 2, 1)


def pick_kernel(planes, place_ref, weight_ref, rows_ref, out_ref, weighted):
    capacity = out_ref.shape[2]
    local = rows_ref.shape[0]
    slots = lax.broadcasted_iota(jnp.int32, (capacity, local), 0)
    for j in range(planes):
        chosen = place_ref[0, 0, j : j + 1, :] == slots
        picked = jnp.dot(
            jnp.where(chosen, 1.0, 0.0).astype(jnp.bfloat16),
            rows_ref[...],
            preferred_element_type=jnp.float32,
        )
        if weighted:
            picked = picked * jnp.sum(
                jnp.where(chosen, weight_ref[0, 0, j : j + 1, :], 0.0), -1, keepdims=True
            )
        out_ref[j, 0] = picked.astype(jnp.bfloat16)


def pick_rows(place, weight, blocks, capacity, weighted):
    count, planned, local = place.shape
    width = blocks.shape[1]
    part = 4 if planned % 4 == 0 else planned
    shape = (count, planned // part, part, local)
    return pl.pallas_call(
        functools.partial(pick_kernel, part, weighted=weighted),
        grid=(count, planned // part),
        in_specs=[
            pl.BlockSpec((1, 1, part, local), lambda c, g: (c, g, 0, 0)),
            pl.BlockSpec((1, 1, part, local), lambda c, g: (c, g, 0, 0)),
            pl.BlockSpec((local, width), lambda c, g: (c, 0)),
        ],
        out_specs=pl.BlockSpec((part, 1, capacity, width), lambda c, g: (g, c, 0, 0)),
        out_shape=jax.ShapeDtypeStruct((planned, count, capacity, width), jnp.bfloat16),
        compiler_params=pltpu.CompilerParams(vmem_limit_bytes=VMEM_BYTES),
        cost_estimate=pl.CostEstimate(
            flops=2 * count * planned * capacity * local * width,
            bytes_accessed=2 * count * planned * capacity * width,
            transcendentals=0,
        ),
    )(place.reshape(shape), weight.reshape(shape), blocks)


def fill_mask(place_ref, mask_ref):
    base, bound = place_ref[0], place_ref[1]
    keys, rows = mask_ref.shape
    key_at = lax.broadcasted_iota(jnp.int32, (keys, rows), 0)
    row_at = lax.broadcasted_iota(jnp.int32, (keys, rows), 1) + base
    least = jnp.where(row_at >= bound, bound, 0)
    mask_ref[...] = jnp.where((key_at <= row_at) & (key_at >= least), 0.0, MASKED)


def head_queries(raw, gain, cosine, sine):
    scale = lax.rsqrt(jnp.mean(raw * raw, -1, keepdims=True) + EPSILON)
    value = raw * scale * gain
    turned = value * cosine + pltpu.roll(value, value.shape[-1] // 2, 1) * sine
    return turned.astype(jnp.bfloat16), scale


def across(a, b):
    return lax.dot_general(a, b, (((1,), (1,)), ((), ())), preferred_element_type=jnp.float32)


def along(a, b):
    return jnp.dot(a, b, preferred_element_type=jnp.float32)


def keyed(both_ref, width, which):
    count, rows = both_ref.shape[:2]
    return both_ref[:, :, which * width : (which + 1) * width].reshape(count * rows, width)


def attend_kernel(
    per, factor, place_ref, raw_ref, both_ref, gain_ref, cos_ref, sin_ref, out_ref, mask_ref, turned_ref
):
    width = gain_ref.shape[1]
    group_step, step = pl.program_id(0), pl.program_id(1)

    @pl.when((group_step == 0) & (step == 0))
    def _():
        fill_mask(place_ref, mask_ref)

    @pl.when(step == 0)
    def _():
        turned_ref[...] = keyed(both_ref, width, 1).T

    for head in range(per):
        columns = slice(head * width, (head + 1) * width)
        queries, _ = head_queries(raw_ref[:, columns], gain_ref[...], cos_ref[...], sin_ref[...])
        chances = jnp.exp2(across(keyed(both_ref, width, 0), queries) * factor + mask_ref[...])
        total = jnp.sum(chances, 0, keepdims=True)
        result = along(turned_ref[...], chances.astype(jnp.bfloat16)) * (1.0 / total)
        out_ref[:, columns] = result.T.astype(jnp.bfloat16)


def attend_back_kernel(
    per,
    steps,
    factor,
    scale,
    place_ref,
    raw_ref,
    grad_ref,
    both_ref,
    gain_ref,
    cos_ref,
    sin_ref,
    raw_grad_ref,
    both_grad_ref,
    gain_grad_ref,
    mask_ref,
    turned_ref,
    sums_ref,
):
    width = gain_ref.shape[1]
    group_step, step = pl.program_id(0), pl.program_id(1)

    @pl.when((group_step == 0) & (step == 0))
    def _():
        fill_mask(place_ref, mask_ref)
        gain_grad_ref[...] = jnp.zeros_like(gain_grad_ref)

    @pl.when(step == 0)
    def _():
        turned_ref[...] = keyed(both_ref, width, 0).T
        sums_ref[...] = jnp.zeros_like(sums_ref)

    for head in range(per):
        columns = slice(head * width, (head + 1) * width)
        raw = raw_ref[:, columns]
        queries, norm = head_queries(raw, gain_ref[...], cos_ref[...], sin_ref[...])
        grad = grad_ref[:, columns]
        chances = jnp.exp2(across(keyed(both_ref, width, 0), queries) * factor + mask_ref[...])
        chances = chances * (1.0 / jnp.sum(chances, 0, keepdims=True))
        chance_grad = across(keyed(both_ref, width, 1), grad)
        mean = jnp.sum(chances * chance_grad, 0, keepdims=True)
        score_grad = (chances * (chance_grad - mean)).astype(jnp.bfloat16)
        sums_ref[:, :width] += along(score_grad, queries)
        sums_ref[:, width:] += along(chances.astype(jnp.bfloat16), grad)
        query_grad = (along(turned_ref[...], score_grad) * scale).astype(jnp.bfloat16)
        query_grad = query_grad.astype(jnp.float32).T
        back = query_grad * cos_ref[...] - pltpu.roll(query_grad, width // 2, 1) * sin_ref[...]
        inner = back * gain_ref[...]
        first = norm * inner - raw * (norm * norm * norm) * jnp.mean(inner * raw, -1, keepdims=True)
        raw_grad_ref[:, columns] = first.astype(jnp.bfloat16)
        gain_grad_ref[0:1, :] += jnp.sum(back * raw * norm, 0, keepdims=True)

    @pl.when(step == steps - 1)
    def _():
        both_grad_ref[:, :width] = (sums_ref[:, :width] * scale).astype(jnp.bfloat16)
        both_grad_ref[:, width:] = sums_ref[:, width:].astype(jnp.bfloat16)


def attention_specs(raw, both, width, rows, step, per):
    kv_heads = both.shape[2] // (2 * width)
    heads = raw.shape[1] // width - 2 * kv_heads
    steps = heads // kv_heads // per
    count = both.shape[0]
    keys = count * rows
    wide = pl.BlockSpec((rows, per * width), lambda g, j: (0, g * steps + j))
    specs = dict(
        place=pl.BlockSpec(memory_space=pltpu.SMEM),
        raw=pl.BlockSpec((rows, per * width), lambda g, j: (step, g * steps + j)),
        heads=wide,
        both=pl.BlockSpec((count, rows, 2 * width), lambda g, j: (0, step, g)),
        both_grad=pl.BlockSpec((keys, 2 * width), lambda g, j: (0, g)),
        gain=pl.BlockSpec((1, width), lambda g, j: (0, 0)),
        table=pl.BlockSpec((rows, width), lambda g, j: (0, 0)),
    )
    params = pltpu.CompilerParams(vmem_limit_bytes=VMEM_BYTES)
    work = 2 * heads * rows * keys * width
    return kv_heads, heads, steps, keys, specs, params, work


def attend(raw, both, gain, cosine, sine, place, step, per=2):
    rows, width = cosine.shape
    kv_heads, heads, steps, keys, specs, params, work = attention_specs(
        raw, both, width, rows, step, per
    )
    return pl.pallas_call(
        functools.partial(attend_kernel, per, width ** (-0.5) * math.log2(math.e)),
        grid=(kv_heads, steps),
        in_specs=[specs[k] for k in ("place", "raw", "both", "gain", "table", "table")],
        out_specs=specs["heads"],
        out_shape=jax.ShapeDtypeStruct((rows, heads * width), jnp.bfloat16),
        scratch_shapes=[
            pltpu.VMEM((keys, rows), jnp.float32),
            pltpu.VMEM((width, keys), jnp.bfloat16),
        ],
        compiler_params=params,
        cost_estimate=pl.CostEstimate(
            flops=4 * work, bytes_accessed=4 * rows * heads * width, transcendentals=work // width
        ),
    )(place, raw, both, gain, cosine, sine)


def attend_back(raw, grad, both, gain, cosine, sine, place, step, per=2):
    rows, width = cosine.shape
    kv_heads, heads, steps, keys, specs, params, work = attention_specs(
        raw, both, width, rows, step, per
    )
    return pl.pallas_call(
        functools.partial(
            attend_back_kernel, per, steps, width ** (-0.5) * math.log2(math.e), width ** (-0.5)
        ),
        grid=(kv_heads, steps),
        in_specs=[specs[k] for k in ("place", "raw", "heads", "both", "gain", "table", "table")],
        out_specs=(
            specs["heads"],
            specs["both_grad"],
            pl.BlockSpec((8, width), lambda g, j: (0, 0)),
        ),
        out_shape=(
            jax.ShapeDtypeStruct((rows, heads * width), jnp.bfloat16),
            jax.ShapeDtypeStruct((keys, both.shape[2]), jnp.bfloat16),
            jax.ShapeDtypeStruct((8, width), jnp.float32),
        ),
        scratch_shapes=[
            pltpu.VMEM((keys, rows), jnp.float32),
            pltpu.VMEM((width, keys), jnp.bfloat16),
            pltpu.VMEM((keys, 2 * width), jnp.float32),
        ],
        compiler_params=params,
        cost_estimate=pl.CostEstimate(
            flops=10 * work, bytes_accessed=8 * rows * heads * width, transcendentals=work // width
        ),
    )(place, raw, grad, both, gain, cosine, sine)


def per_device(
    tokens,
    routes,
    route_weights,
    bounds,
    norm_attn,
    norm_ffn,
    q_gain,
    k_gain,
    w_q,
    w_k,
    w_v,
    w_o,
    w_gate,
    w_up,
    w_down,
    cotangent,
):
    micro = tokens.shape[0]
    local = tokens.shape[2]
    width = tokens.shape[3]
    head_dim = q_gain.shape[0]
    kv_heads = w_k.shape[1] // head_dim
    top = routes.shape[3]
    ring = lax.axis_size("ctx")
    plane = lax.axis_size("exp")
    assert w_gate.shape[0] == 1
    experts = ring * plane
    capacity = max(2, local * top * 5 // (4 * experts))
    seq_len = local * ring
    query_width = w_q.shape[1]
    pair_width = kv_heads * head_dim
    here = lax.axis_index("ctx")
    base = here * local
    cosine, sine = rope_tables(base + jnp.arange(local, dtype=jnp.int32), head_dim)
    gate_weight, up_weight, down_weight = w_gate[0], w_up[0], w_down[0]

    def dot(a, b):
        return jnp.dot(a, b, preferred_element_type=jnp.float32)

    def dot_t(a, b):
        return jnp.einsum("te,de->td", a, b, preferred_element_type=jnp.float32)

    def t_dot(a, b):
        return jnp.einsum("td,te->de", a, b, preferred_element_type=jnp.float32)

    def paired(keys, values):
        rows = keys.shape[0]
        return jnp.stack(
            [keys.reshape(rows, kv_heads, head_dim), values.reshape(rows, kv_heads, head_dim)], 2
        ).reshape(rows, 2 * pair_width)

    in_weight = lax.all_gather(
        jnp.concatenate([w_q, paired(w_k, w_v)], 1), "exp", axis=0, tiled=True
    )
    out_weight = lax.all_gather(w_o, "exp", axis=0, tiled=True)

    meta = jnp.concatenate([routes[:, 0].astype(jnp.float32), route_weights[:, 0]], -1)
    grads_low = [cotangent[step, 0] for step in range(micro)]
    *grad_blocks, meta = line_gather(*grads_low, meta.reshape(-1, 128))
    meta = meta.reshape(ring, micro, local, 2 * top)
    tables = [
        plane_tables(
            meta[:, step, :, :top].astype(jnp.int32), meta[:, step, :, top:], here * plane, plane
        )
        for step in range(micro)
    ]
    slots = jnp.arange(capacity, dtype=jnp.int32)
    chosen = [
        place.transpose(1, 0, 2)[:, :, None, :] == slots[None, None, :, None] for place, _ in tables
    ]

    def exchange(rows, *waits):
        if waits:
            rows = after(rows, *waits)
        rows = rows.reshape(plane, ring * capacity, width)
        return lax.all_to_all(rows, "exp", split_axis=0, concat_axis=0, tiled=True).reshape(
            plane * ring * capacity, width
        )

    def pick(blocks, step, weighted):
        return pick_rows(*tables[step], blocks, capacity, weighted)

    def from_experts(back, step, weighted):
        back = back.reshape(plane, ring, capacity, width)
        factor = chosen[step]
        if weighted:
            weight = tables[step][1].transpose(1, 0, 2)
            factor = jnp.where(factor, weight[:, :, None, :], 0.0)
        part = jnp.einsum(
            "jcst,jcsd->ctd",
            factor.astype(jnp.bfloat16),
            back,
            preferred_element_type=jnp.float32,
        )
        return lax.psum_scatter(
            part.astype(jnp.bfloat16).reshape(seq_len, width),
            "ctx",
            scatter_dimension=0,
            tiled=True,
        ).astype(jnp.float32)

    incoming = [exchange(pick(grad_blocks[0], 0, True))]
    for step in range(1, micro):
        incoming.append(exchange(pick(grad_blocks[step], step, True), incoming[-1]))

    rows = tokens[:, 0].astype(jnp.float32).reshape(micro * local, width)
    hidden, first_scale = norm_rows(rows, norm_attn)
    hidden = after(hidden.astype(jnp.bfloat16), grad_blocks[0])
    raw = dot(hidden, in_weight)
    pair_raw = raw[:, query_width:].reshape(micro * local, kv_heads, 2, head_dim)
    key_raw = pair_raw[:, :, 0]
    key_normed, key_scale = norm_rows(key_raw, k_gain)
    key_cos = jnp.tile(cosine, (micro, 1))[:, None, :]
    key_sin = jnp.tile(sine, (micro, 1))[:, None, :]
    keys = (key_normed * key_cos + swap_halves(key_normed) * key_sin).astype(jnp.bfloat16)
    pairs = jnp.stack([keys, pair_raw[:, :, 1].astype(jnp.bfloat16)], 2).reshape(
        micro * local, 2 * pair_width
    )
    both = lax.all_gather(pairs, "ctx", axis=0)
    gain_row = q_gain[None, :]
    places, attended, middles, feeds, scales = [], [], [], [], []
    for step in range(micro):
        part = slice(step * local, (step + 1) * local)
        places.append(jnp.stack([base, bounds[step, 0]]).astype(jnp.int32))
        attended.append(attend(raw, both, gain_row, cosine, sine, places[step], step))
        middles.append(rows[part] + dot(attended[step], out_weight))
        feed_in, second_scale = norm_rows(middles[step], norm_ffn)
        feeds.append(feed_in.astype(jnp.bfloat16))
        scales.append(second_scale)
    feed_blocks = [lax.all_gather(feed, "ctx", axis=0, tiled=True) for feed in feeds]

    received = []
    last = incoming[-1]
    for step in range(micro):
        received.append(exchange(pick(feed_blocks[step], step, False), last))
        last = received[-1]

    active, gate_grad, up_grad, produced, backs, pair_values = [], [], [], [], [], []
    for step in range(micro):
        parts = run_expert(received[step], incoming[step], gate_weight, up_weight, down_weight)
        for held, item in zip((active, gate_grad, up_grad, produced, backs, pair_values), parts):
            held.append(item)

    returned = []
    for step in range(micro):
        returned.append(exchange(backs[step], last))
        last = returned[-1]

    branches, raw_grads, middle_grads, gain_list, results = [], [], [], [], []
    for step in range(micro):
        results.append(exchange(produced[step], last, *raw_grads))
        last = results[-1]
        part = slice(step * local, (step + 1) * local)
        feed_grad = from_experts(returned[step], step, False)
        middle_norm_grad, second_gain = norm_back(middles[step], scales[step], norm_ffn, feed_grad)
        middle_grads.append(grads_low[step].astype(jnp.float32) + middle_norm_grad)
        branches.append(middle_grads[step].astype(jnp.bfloat16))
        attended_grad = dot_t(branches[step], out_weight).astype(jnp.bfloat16)
        raw_grad, pair_part, query_gain_part = attend_back(
            raw, attended_grad, both, gain_row, cosine, sine, places[step], step
        )
        raw_grads.append(raw_grad)
        gain_list.append([jnp.sum(second_gain, 0), query_gain_part[0], pair_part])
    pair_grads = []
    for step in range(micro):
        part = slice(step * local, (step + 1) * local)
        pair_grad = lax.psum_scatter(
            gain_list[step][2], "ctx", scatter_dimension=0, tiled=True
        ).reshape(local, kv_heads, 2, head_dim)
        key_grad = pair_grad[:, :, 0].astype(jnp.float32)
        key_turned = key_grad * cosine[:, None, :] - swap_halves(key_grad) * sine[:, None, :]
        key_raw_grad, key_gain_part = norm_back(key_raw[part], key_scale[part], k_gain, key_turned)
        pair_grad = jnp.stack([key_raw_grad.astype(jnp.bfloat16), pair_grad[:, :, 1]], 2)
        pair_grads.append(pair_grad.reshape(local, 2 * pair_width))
        gain_list[step][2] = jnp.sum(key_gain_part, (0, 1))
    results[-1] = after(results[-1], raw_grads[-1])

    def sum_over_devices(left, right):
        share = left.shape[1] // experts
        left = left.reshape(-1, ring, plane, share).transpose(0, 2, 1, 3)
        term = t_dot(left.reshape(-1, experts * share), right)
        term = lax.psum_scatter(term.astype(jnp.bfloat16), "exp", scatter_dimension=0, tiled=True)
        return lax.psum_scatter(term, "ctx", scatter_dimension=0, tiled=True).astype(jnp.float32)

    out_total = sum_over_devices(jnp.concatenate(attended, 0), jnp.concatenate(branches, 0))
    query_grad, pair_grad = jnp.concatenate(raw_grads, 0), jnp.concatenate(pair_grads, 0)
    query_total = sum_over_devices(hidden, query_grad)
    pair_total = sum_over_devices(hidden, pair_grad).reshape(-1, kv_heads, 2, head_dim)
    hidden_grad = dot_t(query_grad, in_weight[:, :query_width]) + dot_t(
        pair_grad, in_weight[:, query_width:]
    )
    first_grad, first_gain = norm_back(rows, first_scale, norm_attn, hidden_grad)
    tokens_grad = jnp.concatenate(middle_grads, 0) + first_grad
    gain_total = lax.psum_scatter(
        jnp.concatenate([jnp.sum(first_gain, 0)] + [sum(parts) for parts in zip(*gain_list)]),
        ("ctx", "exp"),
        scatter_dimension=0,
        tiled=True,
    )
    received_all = jnp.concatenate(received, 0)
    gate_term = t_dot(received_all, jnp.concatenate(gate_grad, 0))[None]
    up_term = t_dot(received_all, jnp.concatenate(up_grad, 0))[None]
    down_term = t_dot(jnp.concatenate(active, 0), jnp.concatenate(incoming, 0))[None]

    outputs = [
        (middles[step] + from_experts(results[step], step, True)).astype(jnp.bfloat16)
        for step in range(micro)
    ]

    pair_values = lax.all_to_all(
        jnp.stack([v.reshape(plane, ring, capacity) for v in pair_values], 1),
        "exp",
        split_axis=0,
        concat_axis=0,
        tiled=True,
    )
    values = jnp.stack(
        [
            jnp.sum(jnp.where(chosen[step], pair_values[:, step, :, :, None], 0.0), 2)
            for step in range(micro)
        ],
        1,
    )
    values = lax.all_to_all(
        values.transpose(2, 1, 3, 0), "ctx", split_axis=0, concat_axis=0, tiled=True
    )
    values = values.transpose(1, 2, 0, 3).reshape(micro, local, experts)
    match = routes[:, 0, :, :, None] == jnp.arange(experts, dtype=jnp.int32)
    route_grads = jnp.sum(jnp.where(match, values[:, :, None, :], 0.0), -1) / route_weights[:, 0]

    return (
        jnp.stack(outputs)[:, None],
        tokens_grad.reshape(micro, 1, local, width),
        route_grads[:, None],
        query_total,
        pair_total[:, :, 0].reshape(-1, pair_width),
        pair_total[:, :, 1].reshape(-1, pair_width),
        out_total,
        gain_total,
        gate_term,
        up_term,
        down_term,
    )


def solution(mesh):
    in_specs = (
        P(None, "exp", "ctx", None),
        P(None, "exp", "ctx", None),
        P(None, "exp", "ctx", None),
        P(None, "exp"),
        P(),
        P(),
        P(),
        P(),
        P("exp", None),
        P("exp", None),
        P("exp", None),
        P("exp", None),
        P(("ctx", "exp"), None, None),
        P(("ctx", "exp"), None, None),
        P(("ctx", "exp"), None, None),
        P(None, "exp", "ctx", None),
    )
    out_specs = (
        P(None, "exp", "ctx", None),
        P(None, "exp", "ctx", None),
        P(None, "exp", "ctx", None),
        P(("ctx", "exp"), None),
        P(("ctx", "exp"), None),
        P(("ctx", "exp"), None),
        P(("ctx", "exp"), None),
        P(("ctx", "exp")),
        P(("ctx", "exp"), None, None),
        P(("ctx", "exp"), None, None),
        P(("ctx", "exp"), None, None),
    )
    return jax.shard_map(
        per_device, mesh=mesh, in_specs=in_specs, out_specs=out_specs, check_vma=False
    )
```

time: 2410 us -> 2100 us (0.87)
  Pallas kernels: 0 us -> 443 us
  matrix products: 638 us -> 243 us
  blocking collectives: 217 us -> 43.2 us
  other arithmetic: 195 us -> 55.1 us
  local copies, waits for them, and re-layouts: 211 us -> 77.1 us
  waiting for transfers between devices: 1080 us -> 1160 us
    pallas_call x0 -> x20, Pallas kernels: none -> 443 us  [the longest x1 145 us: line_gather(): pl.pallas_call(functools.partial(gather_kernel, count, arrays), in_specs=...]
    all_gather x7 -> x4, waiting for transfers between devices: 453 us -> 192 us  [the longest x2 192 us: per_device(): lax.all_gather(feed, 'ctx', axis=0, tiled=True)]
    dot_general x16 -> x0, matrix products: 199 us -> none  [the longest x2 58.2 us: per_device(): jnp.einsum('qgjd,kgd->gjqk', attended_grad, all_values, preferred_element...]
    all_to_all x1 -> x0, blocking collectives: 160 us -> none  [from_experts(): lax.all_to_all(rows.reshape(plane, ring * capacity, width), 'exp', split_...]
    all_to_all x10, waiting for transfers between devices: 482 us -> 634 us  [the longest x8 634 us: exchange(): lax.all_to_all(rows, 'exp', split_axis=0, concat_axis=0, tiled=True)]
    dot_general x10 -> x4, matrix products: 155 us -> 53.3 us  [dot_t(): return jnp.einsum('te,de->td', a, b, preferred_element_type=jnp.float32)]
    dot_general x14 -> x3, matrix products: 132 us -> 35.6 us  [dot(): return jnp.dot(a, b, preferred_element_type=jnp.float32)]
    convert_element_type x10 -> x2, local copies, waits for them, and re-layouts: 95.2 us -> 2.42 us  [per_device(): meta[:, step, :, :top].astype(jnp.int32)]
  transfers between devices with their start and end apart: 28 -> 27, of which waited for: 20 -> 17; matrix products, arithmetic and copies ran while one was open for 28% -> 14% of each run, Pallas kernels for 0% -> 19%
where the time goes in v2:
time: 2100 us; the launch traced here: 2090 us
  waiting for transfers between devices  1160 us (55%)
  Pallas kernels  443 us (21%)
  matrix products  243 us (12%)
  local copies, waits for them, and re-layouts  77.1 us (4%)
  other arithmetic  55.1 us (3%)
  starting transfers between devices  50.5 us (2%)
  blocking collectives  43.2 us (2%)
    all_to_all x8, waiting for transfers between devices, exchange(): lax.all_to_all(rows, 'exp', split_axis=0, concat_axis=0, tiled=True)  634 us
    all_gather x2, waiting for transfers between devices, per_device(): lax.all_gather(feed, 'ctx', axis=0, tiled=True)  192 us
    pallas_call x1, Pallas kernels, line_gather(): pl.pallas_call(functools.partial(gather_kernel, count, arrays), in_specs=...  145 us
    pallas_call x2, Pallas kernels, run_expert(): pl.pallas_call(expert_kernel, grid=(total // block,), in_specs=[wide, wid...  115 us
    dot_general x6, matrix products, t_dot(): return jnp.einsum('td,te->de', a, b, preferred_element_type=jnp.float32)  114 us
    reduce_scatter x4, waiting for transfers between devices, from_experts(): lax.psum_scatter(part.astype(jnp.bfloat16).reshape(seq_len, width), 'ctx'...  98.3 us
    reduce_scatter x3, waiting for transfers between devices, sum_over_devices(): lax.psum_scatter(term, 'ctx', scatter_dimension=0, tiled=True)  86.8 us
    pallas_call x2, Pallas kernels, attend_back(): pl.pallas_call(functools.partial(attend_back_kernel, per, steps, width **...  85.5 us
  transfers between devices with their start and end apart: 27, of which 17 were waited for; matrix products, arithmetic and copies ran while one was open for 14% of the time, Pallas kernels for 19%

profile of v2, /device:TPU:0, one launch (start us, length us, event | category | flops | bytes accessed | tf_op | source)
XLA Modules:
  0.0 2089.6 jit_solution(12854212747079807972)
XLA Ops:
  19.0 145.2 %shard_map.239 = (bf16[1024,2048]{1,0:T(8,128)(2,1)}, bf16[1024,2048]{1,0:T(8,128)(2,1)}, f32[256,128]{1,0:T(8,128)}) custom-call(bf16[256,2048]{1,0:T(8,128)(2,1)} %get-tuple-element.125.refs_0_, bf16[256,2048]{1,0:T(8,128)(2,1)} %get-tuple-element.124.refs_1_, f32[64,128]{1,0:T(8,128)} %reshape.408.refs_2_), custom_call_target="tpu_custom_call" | custom-call | bytes 209715200 | tf_op jit(solution)/shard_map/pallas_call | solution.py:126
  166.8 15.2 fusion.136.raw_ref
  214.3 12.1 shard_map.244
  238.6 11.8 shard_map.243.refs_0_
  250.4 120.0 %all-to-all-done = bf16[8,320,2048]{2,1,0:T(8,128)(2,1)} async-done(((bf16[8,320,2048]{2,1,0:T(8,128)(2,1)}), bf16[8,320,2048]{2,1,0:T(8,128)(2,1)}, u32[]{:S(2)}, u32[]{:S(2)}) %all-to-all-start) | async-done | bytes 10485792 | tf_op jit(solution)/shard_map/all_to_all | solution.py:521
  375.7 23.9 %shard_map.241 = bf16[256,4096]{1,0:T(8,128)(2,1)} custom-call(s32[2]{0:T(128)} %get-tuple-element.172.place_ref, f32[512,5120]{1,0:T(8,128)} %copy-done.32, bf16[4,512,1024]{2,1,0:T(8,128)(2,1)} %all-gather.8.cloned.1.call-done.both_ref, f32[1,128]{1,0:T(1,128)} %bitcast.314, f32[256,128]{1,0:T(8,128)} %copy-done.22, f32[256,128]{1,0:T(8,128)} %copy-done.20), custom_call_target="tpu_custom_call" | custom-call | flops 8589934592 | bytes 4194304 | tf_op jit(solution)/shard_map/pallas_call | solution.py:395
  399.6 84.0 %all-gather.10.cloned.1.call-done = bf16[4096,2048]{1,0:T(8,128)(2,1)} async-done(((bf16[512,2048]{1,0:T(8,128)(2,1)}), bf16[4096,2048]{1,0:T(8,128)(2,1)}) %all-gather.10.cloned.1.call-update) | async-done | bytes 16777232 | tf_op jit(solution)/shard_map/all_gather | solution.py:500
  483.6 11.6 multiply_reduce_fusion.1
  495.2 24.7 %shard_map.248 = bf16[256,4096]{1,0:T(8,128)(2,1)} custom-call(s32[2]{0:T(128)} %get-tuple-element.173.place_ref, f32[512,5120]{1,0:T(8,128)} %copy-done.32, bf16[4,512,1024]{2,1,0:T(8,128)(2,1)} %all-gather.8.cloned.1.call-done.both_ref, f32[1,128]{1,0:T(1,128)} %bitcast.315, f32[256,128]{1,0:T(8,128)} %copy-done.22, f32[256,128]{1,0:T(8,128)} %copy-done.20), custom_call_target="tpu_custom_call" | custom-call | flops 8589934592 | bytes 4194304 | tf_op jit(solution)/shard_map/pallas_call | solution.py:395
  520.4 8.8 multiply_reduce_fusion
  532.3 110.1 %all-gather.12.cloned.1.call-done.rows_ref = bf16[1024,2048]{1,0:T(8,128)(2,1)} async-done(((bf16[256,2048]{1,0:T(8,128)(2,1)}), bf16[1024,2048]{1,0:T(8,128)(2,1)}) %all-gather.12.cloned.1.call-update) | async-done | bytes 4194320 | tf_op jit(solution)/shard_map/all_gather | solution.py:575
  642.4 11.9 shard_map.242.refs_0_
  660.1 81.8 %all-gather.14.cloned.1.call-done.rows_ref = bf16[1024,2048]{1,0:T(8,128)(2,1)} async-done(((bf16[256,2048]{1,0:T(8,128)(2,1)}), bf16[1024,2048]{1,0:T(8,128)(2,1)}) %all-gather.14.cloned.1.call-update) | async-done | bytes 4194320 | tf_op jit(solution)/shard_map/all_gather | solution.py:575
  741.9 12.1 shard_map.249.refs_0_
  754.0 22.0 %all-to-all-done.2 = bf16[8,320,2048]{2,1,0:T(8,128)(2,1)} async-done(((bf16[8,320,2048]{2,1,0:T(8,128)(2,1)}), bf16[8,320,2048]{2,1,0:T(8,128)(2,1)}, u32[]{:S(2)}, u32[]{:S(2)}) %all-to-all-start.2) | async-done | bytes 10485792 | tf_op jit(solution)/shard_map/all_to_all | solution.py:521
  781.2 57.7 %shard_map.247 = (bf16[2560,768]{1,0:T(8,128)(2,1)}, bf16[2560,768]{1,0:T(8,128)(2,1)}, bf16[2560,768]{1,0:T(8,128)(2,1)}, bf16[2560,2048]{1,0:T(8,128)(2,1)}, b...) custom-call(bf16[2560,2048]{1,0:T(8,128)(2,1)} %bitcast.31.rows_ref.refs_1_, bf16[2560,2048]{1,0:T(8,128)(2,1)} %bitcast.27.refs_1_.grad_ref, ...), custom_call_target="tpu_custom_call" | custom-call | flops 56371445760 | bytes 41943040 | tf_op jit(solution)/shard_map/pallas_call | solution.py:187
  838.9 58.8 %all-to-all-done.3 = bf16[8,320,2048]{2,1,0:T(8,128)(2,1)} async-done(((bf16[8,320,2048]{2,1,0:T(8,128)(2,1)}), bf16[8,320,2048]{2,1,0:T(8,128)(2,1)}, u32[]{:S(2)}, u32[]{:S(2)}) %all-to-all-start.3) | async-done | bytes 10485792 | tf_op jit(solution)/shard_map/all_to_all | solution.py:521
  902.9 57.7 %shard_map.251 = (bf16[2560,768]{1,0:T(8,128)(2,1)}, bf16[2560,768]{1,0:T(8,128)(2,1)}, bf16[2560,768]{1,0:T(8,128)(2,1)}, bf16[2560,2048]{1,0:T(8,128)(2,1)}, b...) custom-call(bf16[2560,2048]{1,0:T(8,128)(2,1)} %bitcast.38.rows_ref.refs_1_, bf16[2560,2048]{1,0:T(8,128)(2,1)} %bitcast.29.refs_1_.grad_ref, ...), custom_call_target="tpu_custom_call" | custom-call | flops 56371445760 | bytes 41943040 | tf_op jit(solution)/shard_map/pallas_call | solution.py:187
  960.6 58.8 %all-to-all-done.4 = bf16[8,320,2048]{2,1,0:T(8,128)(2,1)} async-done(((bf16[8,320,2048]{2,1,0:T(8,128)(2,1)}), bf16[8,320,2048]{2,1,0:T(8,128)(2,1)}, u32[]{:S(2)}, u32[]{:S(2)}) %all-to-all-start.4) | async-done | bytes 10485792 | tf_op jit(solution)/shard_map/all_to_all | solution.py:521
  1019.5 5.3 all-to-all-start.5
  1025.3 9.5 bitcast_convert_fusion.2
  1034.8 106.6 %all-to-all-done.5 = bf16[8,320,2048]{2,1,0:T(8,128)(2,1)} async-done(((bf16[8,320,2048]{2,1,0:T(8,128)(2,1)}), bf16[8,320,2048]{2,1,0:T(8,128)(2,1)}, u32[]{:S(2)}, u32[]{:S(2)}) %all-to-all-start.5) | async-done | bytes 10485792 | tf_op jit(solution)/shard_map/all_to_all | solution.py:521
  1146.7 9.5 bitcast_convert_fusion.1
  1156.3 106.9 %all-to-all-done.6 = bf16[8,320,2048]{2,1,0:T(8,128)(2,1)} async-done(((bf16[8,320,2048]{2,1,0:T(8,128)(2,1)}), bf16[8,320,2048]{2,1,0:T(8,128)(2,1)}, u32[]{:S(2)}, u32[]{:S(2)}) %all-to-all-start.6) | async-done | bytes 10485792 | tf_op jit(solution)/shard_map/all_to_all | solution.py:521
  1263.2 9.5 bitcast_convert_fusion.3
  1279.1 67.2 %reduce-scatter.13.cloned.1.call-done = bf16[256,2048]{1,0:T(8,128)(2,1)} async-done(((bf16[1024,2048]{1,0:T(8,128)(2,1)}), bf16[256,2048]{1,0:T(8,128)(2,1)}) %reduce-scatter.13.cloned.1.call-update) | async-done | bytes 1048592 | tf_op jit(solution)/shard_map/reduce_scatter | solution.py:540
  1346.3 5.6 fusion.126
  1352.0 12.0 convolution_convert_fusion.2.grad_ref
  1363.9 42.7 %shard_map.257 = (bf16[256,4096]{1,0:T(8,128)(2,1)}, bf16[1024,1024]{1,0:T(8,128)(2,1)}, f32[8,128]{1,0:T(8,128)}) custom-call(s32[2]{0:T(128)} %get-tuple-element.173.place_ref, f32[512,5120]{1,0:T(8,128)} %copy-done.32, bf16[256,4096]{1,0:T(8,128)(2,1)} %convolution_convert_fusion.2.grad_ref, bf16[4,512,1024]{2,1,0:T(8,128)(2,1)} %all-gather.8.cloned.1.call-done.both_ref, ...), custom_call_target="tpu_custom_call" | custom-call | flops 21474836480 | bytes 8388608 | tf_op jit(solution)/shard_map/pallas_call | solution.py:417
  1406.9 18.0 convolution_convert_fusion.3.grad_ref
  1425.0 42.8 %shard_map.255 = (bf16[256,4096]{1,0:T(8,128)(2,1)}, bf16[1024,1024]{1,0:T(8,128)(2,1)}, f32[8,128]{1,0:T(8,128)}) custom-call(s32[2]{0:T(128)} %get-tuple-element.172.place_ref, f32[512,5120]{1,0:T(8,128)} %copy-done.32, bf16[256,4096]{1,0:T(8,128)(2,1)} %convolution_convert_fusion.3.grad_ref, bf16[4,512,1024]{2,1,0:T(8,128)(2,1)} %all-gather.8.cloned.1.call-done.both_ref, ...), custom_call_target="tpu_custom_call" | custom-call | flops 21474836480 | bytes 8388608 | tf_op jit(solution)/shard_map/pallas_call | solution.py:417
  1482.1 30.1 %reduce-scatter.21.cloned.1.call-done = bf16[256,1024]{1,0:T(8,128)(2,1)} async-done(((bf16[1024,1024]{1,0:T(8,128)(2,1)}), bf16[256,1024]{1,0:T(8,128)(2,1)}) %reduce-scatter.21.cloned.1.call-update) | async-done | bytes 524304 | tf_op jit(solution)/shard_map/reduce_scatter | solution.py:612
  1528.9 11.7 convolution_convert_fusion.1
  1547.5 7.6 copy.155
  1555.2 14.7 convolution_convert_fusion
  1575.8 160.9 %all-to-all-done.7 = bf16[8,320,2048]{2,1,0:T(8,128)(2,1)} async-done(((bf16[8,320,2048]{2,1,0:T(8,128)(2,1)}), bf16[8,320,2048]{2,1,0:T(8,128)(2,1)}, u32[]{:S(2)}, u32[]{:S(2)}) %all-to-all-start.7) | async-done | bytes 10485792 | tf_op jit(solution)/shard_map/all_to_all | solution.py:521
  1737.4 10.0 bitcast_convert_fusion
  1754.0 26.9 %fusion.43 = f32[1,2048,768]{2,1,0:T(8,128)} fusion(bf16[2560,768]{1,0:T(8,128)(2,1)} %get-tuple-element.48, bf16[2560,768]{1,0:T(8,128)(2,1)} %get-tuple-element.47, bf16[2560,2048]{1,0:T(8,128)(2,1)} %bitcast.38.rows_ref.refs_1_, bf16[2560,2048]{1,0:T(8,128)(2,1)} %bitcast.31.rows_ref.refs_1_), kind=kOutput, calls=%fused_computation.51 | convolution fusion | flops 16163799040 | bytes 35127296 | tf_op jit(solution)/shard_map/td,te->de/dot_general | solution.py:489
  1780.9 29.5 %fusion.46 = f32[1,2048,768]{2,1,0:T(8,128)} fusion(bf16[2560,768]{1,0:T(8,128)(2,1)} %get-tuple-element.50, bf16[2560,768]{1,0:T(8,128)(2,1)} %get-tuple-element.49, bf16[2560,2048]{1,0:T(8,128)(2,1)} %bitcast.38.rows_ref.refs_1_, bf16[2560,2048]{1,0:T(8,128)(2,1)} %bitcast.31.rows_ref.refs_1_), kind=kOutput, calls=%fused_computation.52 | convolution fusion | flops 16163799040 | bytes 35127296 | tf_op jit(solution)/shard_map/td,te->de/dot_general | solution.py:489
  1816.2 27.0 %fusion.49 = f32[1,768,2048]{2,1,0:T(8,128)} fusion(bf16[2560,2048]{1,0:T(8,128)(2,1)} %bitcast.29.refs_1_.grad_ref, bf16[2560,2048]{1,0:T(8,128)(2,1)} %bitcast.27.refs_1_.grad_ref, bf16[2560,768]{1,0:T(8,128)(2,1)} %get-tuple-element.52, bf16[2560,768]{1,0:T(8,128)(2,1)} %get-tuple-element.51), kind=kOutput, calls=%fused_computation.53 | convolution fusion | flops 16163799040 | bytes 35127296 | tf_op jit(solution)/shard_map/td,te->de/dot_general | solution.py:489
  1844.7 6.7 fusion.33
  1851.4 35.3 %reduce-scatter.33.cloned.1.call-done = bf16[512,2048]{1,0:T(8,128)(2,1)} async-done(((bf16[4096,2048]{1,0:T(8,128)(2,1)}), bf16[512,2048]{1,0:T(8,128)(2,1)}) %reduce-scatter.33.cloned.1.call-update) | async-done | bytes 2097168 | tf_op jit(solution)/shard_map/reduce_scatter | solution.py:627
  1886.8 16.6 fusion.42
  1903.4 43.2 %all-reduce = f32[4352]{0:T(1024)S(1)} all-reduce(f32[4352]{0:T(1024)S(1)} %pad_maximum_fusion.19), channel_id=14, replica_groups=mesh['ctx'=4,'exp'=8] {'ctx','exp'}, use_global_device_ids=true, to_apply=%region_33.34.clone | all-reduce | flops 4352 | bytes 34816
  1947.2 7.3 maximum_add_fusion
  1957.8 31.1 %reduce-scatter.19.cloned.1.call-done = bf16[256,2048]{1,0:T(8,128)(2,1)} async-done(((bf16[1024,2048]{1,0:T(8,128)(2,1)}), bf16[256,2048]{1,0:T(8,128)(2,1)}) %reduce-scatter.19.cloned.1.call-update) | async-done | bytes 1048592 | tf_op jit(solution)/shard_map/reduce_scatter | solution.py:540
  1991.9 43.5 %reduce-scatter.27.cloned.1.call-done = bf16[64,4096]{1,0:T(8,128)(2,1)} async-done(((bf16[256,4096]{1,0:T(8,128)(2,1)}), bf16[64,4096]{1,0:T(8,128)(2,1)}) %reduce-scatter.27.cloned.1.call-update) | async-done | bytes 524304 | tf_op jit(solution)/shard_map/reduce_scatter | solution.py:628
  2037.5 43.3 %reduce-scatter.35.cloned.1.call-done = bf16[128,2048]{1,0:T(8,128)(2,1)} async-done(((bf16[512,2048]{1,0:T(8,128)(2,1)}), bf16[128,2048]{1,0:T(8,128)(2,1)}) %reduce-scatter.35.cloned.1.call-update) | async-done | bytes 524304 | tf_op jit(solution)/shard_map/reduce_scatter | solution.py:628
  (333 shorter events, 164.9 us)
Async XLA Ops:
  7.2 159.6 %all-gather.6.cloned.1.call-start = ((), (), s32[]{:S(2)}) async-start(), calls=%async_computation.22 | async-start | bytes 23592960 | tf_op jit(solution)/shard_map/all_gather | solution.py:497
  14.3 361.3 %all-gather.8.cloned.1.call-start = ((), (), s32[]{:S(2)}) async-start(), calls=%async_computation.23 | async-start | bytes 5242880 | tf_op jit(solution)/shard_map/all_gather | solution.py:564
  14.4 149.8 %copy-start.48 = (f32[2048]{0:T(1024)S(1)}, f32[2048]{0:T(1024)}, u32[]{:S(2)}) copy-start(f32[2048]{0:T(1024)} %param.20) | copy-start | bytes 24580
  14.9 151.1 %copy-start.52 = (f32[1,2,2,128]{3,1,2,0:T(2,128)}, f32[1,2,2,128]{3,1,2,0:T(2,128)S(1)}, u32[]{:S(2)}) copy-start(f32[1,2,2,128]{3,1,2,0:T(2,128)S(1)} %copy.173) | copy-start | bytes 6148
  166.8 32.2 %copy-start.22 = (f32[256,128]{1,0:T(8,128)}, f32[256,128]{1,0:T(8,128)S(1)}, u32[]{:S(2)}) copy-start(f32[256,128]{1,0:T(8,128)S(1)} %get-tuple-element.174.cos_ref) | copy-start | bytes 393220
  166.8 32.2 %copy-start.20 = (f32[256,128]{1,0:T(8,128)}, f32[256,128]{1,0:T(8,128)S(1)}, u32[]{:S(2)}) copy-start(f32[256,128]{1,0:T(8,128)S(1)} %get-tuple-element.175.sin_ref) | copy-start | bytes 393220
  204.3 279.3 %all-gather.10.cloned.1.call-start = ((), (), s32[]{:S(2)}) async-start(), calls=%async_computation.24 | async-start | bytes 18874368 | tf_op jit(solution)/shard_map/all_gather | solution.py:500
  226.3 144.1 %all-to-all-start = ((bf16[8,320,2048]{2,1,0:T(8,128)(2,1)}), bf16[8,320,2048]{2,1,0:T(8,128)(2,1)}, u32[]{:S(2)}, u32[]{:S(2)}) async-start(bf16[8,320,2048]{2,1,0:T(8,128)(2,1)} %bitcast.271), calls=%async_computation | async-start | bytes 20971520 | tf_op jit(solution)/shard_map/all_to_all | solution.py:521
  370.5 283.9 %all-to-all-start.1 = ((bf16[8,320,2048]{2,1,0:T(8,128)(2,1)}), bf16[8,320,2048]{2,1,0:T(8,128)(2,1)}, u32[]{:S(2)}, u32[]{:S(2)}) async-start(bf16[8,320,2048]{2,1,0:T(8,128)(2,1)} %bitcast.269), calls=%async_computation.1 | async-start | bytes 20971520 | tf_op jit(solution)/shard_map/all_to_all | solution.py:521
  375.6 266.8 %all-gather.12.cloned.1.call-start = ((), (), s32[]{:S(2)}) async-start(), calls=%async_computation.25 | async-start | bytes 5242880 | tf_op jit(solution)/shard_map/all_gather | solution.py:575
  495.1 34.8 %copy-start.5 = (f32[256,2048]{1,0:T(8,128)}, f32[256,2048]{1,0:T(8,128)S(1)}, u32[]{:S(2)}) copy-start(f32[256,2048]{1,0:T(8,128)S(1)} %get-tuple-element.166) | copy-start | bytes 6291460
  654.4 121.7 %all-to-all-start.2 = ((bf16[8,320,2048]{2,1,0:T(8,128)(2,1)}), bf16[8,320,2048]{2,1,0:T(8,128)(2,1)}, u32[]{:S(2)}, u32[]{:S(2)}) async-start(bf16[8,320,2048]{2,1,0:T(8,128)(2,1)} %bitcast.267), calls=%async_computation.2 | async-start | bytes 20971520 | tf_op jit(solution)/shard_map/all_to_all | solution.py:521
  659.5 82.4 %all-gather.14.cloned.1.call-start = ((), (), s32[]{:S(2)}) async-start(), calls=%async_computation.26 | async-start | bytes 5242880 | tf_op jit(solution)/shard_map/all_gather | solution.py:575
  776.0 121.7 %all-to-all-start.3 = ((bf16[8,320,2048]{2,1,0:T(8,128)(2,1)}), bf16[8,320,2048]{2,1,0:T(8,128)(2,1)}, u32[]{:S(2)}, u32[]{:S(2)}) async-start(bf16[8,320,2048]{2,1,0:T(8,128)(2,1)} %bitcast.268), calls=%async_computation.3 | async-start | bytes 20971520 | tf_op jit(solution)/shard_map/all_to_all | solution.py:521
  897.7 121.7 %all-to-all-start.4 = ((bf16[8,320,2048]{2,1,0:T(8,128)(2,1)}), bf16[8,320,2048]{2,1,0:T(8,128)(2,1)}, u32[]{:S(2)}, u32[]{:S(2)}) async-start(bf16[8,320,2048]{2,1,0:T(8,128)(2,1)} %bitcast.273), calls=%async_computation.4 | async-start | bytes 20971520 | tf_op jit(solution)/shard_map/all_to_all | solution.py:521
  1019.5 121.9 %all-to-all-start.5 = ((bf16[8,320,2048]{2,1,0:T(8,128)(2,1)}), bf16[8,320,2048]{2,1,0:T(8,128)(2,1)}, u32[]{:S(2)}, u32[]{:S(2)}) async-start(bf16[8,320,2048]{2,1,0:T(8,128)(2,1)} %bitcast.274), calls=%async_computation.5 | async-start | bytes 20971520 | tf_op jit(solution)/shard_map/all_to_all | solution.py:521
  1024.8 248.2 %reduce-scatter.15.cloned.1.call-start = ((), (), s32[]{:S(2)}) async-start(), calls=%async_computation.28 | async-start | bytes 5242880 | tf_op jit(solution)/shard_map/reduce_scatter | solution.py:540
  1025.3 237.9 %copy-start.34 = (s32[8,4,256]{2,0,1:T(8,128)}, s32[8,4,256]{2,0,1:T(8,128)S(1)}, u32[]{:S(2)}) copy-start(s32[8,4,256]{2,0,1:T(8,128)S(1)} %bitcast_select_fusion.1) | copy-start | bytes 98308
  1141.3 121.9 %all-to-all-start.6 = ((bf16[8,320,2048]{2,1,0:T(8,128)(2,1)}), bf16[8,320,2048]{2,1,0:T(8,128)(2,1)}, u32[]{:S(2)}, u32[]{:S(2)}) async-start(bf16[8,320,2048]{2,1,0:T(8,128)(2,1)} %bitcast.272), calls=%async_computation.6 | async-start | bytes 20971520 | tf_op jit(solution)/shard_map/all_to_all | solution.py:521
  1146.6 126.3 %reduce-scatter.17.cloned.1.call-start = ((), (), s32[]{:S(2)}) async-start(), calls=%async_computation.29 | async-start | bytes 5242880 | tf_op jit(solution)/shard_map/reduce_scatter | solution.py:540
  1156.2 107.0 %copy-start.41 = (f32[4,256,8]{1,2,0:T(8,128)S(1)}, f32[4,256,8]{1,2,0:T(8,128)}, u32[]{:S(2)}) copy-start(f32[4,256,8]{1,2,0:T(8,128)} %copy-done.40) | copy-start | bytes 98308
  1156.2 190.1 %reduce-scatter.13.cloned.1.call-start = ((), (), s32[]{:S(2)}) async-start(), calls=%async_computation.27 | async-start | bytes 5242880 | tf_op jit(solution)/shard_map/reduce_scatter | solution.py:540
  1272.7 73.6 %copy-start.66 = (f32[256]{0:T(256)S(1)}, f32[256]{0:T(256)}, u32[]{:S(2)}) copy-start(f32[256]{0:T(256)} %get-tuple-element.159) | copy-start | bytes 3076
  1272.7 73.6 %copy-start.67 = (f32[256]{0:T(256)S(1)}, f32[256]{0:T(256)}, u32[]{:S(2)}) copy-start(f32[256]{0:T(256)} %get-tuple-element.157) | copy-start | bytes 3076
  1272.7 205.3 %reduce-scatter.23.cloned.1.call-start = ((), (), s32[]{:S(2)}) async-start(), calls=%async_computation.32 | async-start | bytes 2621440 | tf_op jit(solution)/shard_map/reduce_scatter | solution.py:612
  1272.9 73.4 %copy-start.14 = (bf16[256,2048]{1,0:T(8,128)(2,1)S(1)}, bf16[256,2048]{1,0:T(8,128)(2,1)}, u32[]{:S(2)}) copy-start(bf16[256,2048]{1,0:T(8,128)(2,1)} %reduce-scatter.15.cloned.1.call-done) | copy-start | bytes 3145732
  1363.9 43.0 %copy-start.25 = (bf16[256,2048]{1,0:T(8,128)(2,1)S(1)}, bf16[256,2048]{1,0:T(8,128)(2,1)}, u32[]{:S(2)}) copy-start(bf16[256,2048]{1,0:T(8,128)(2,1)} %get-tuple-element.119) | copy-start | bytes 3145732
  1406.6 105.6 %reduce-scatter.21.cloned.1.call-start = ((), (), s32[]{:S(2)}) async-start(), calls=%async_computation.31 | async-start | bytes 2621440 | tf_op jit(solution)/shard_map/reduce_scatter | solution.py:612
  1425.0 43.3 %copy-start.23 = (f32[256,128]{1,0:T(8,128)S(1)}, f32[256,128]{1,0:T(8,128)}, u32[]{:S(2)}) copy-start(f32[256,128]{1,0:T(8,128)} %copy-done.22) | copy-start | bytes 393220
  1425.0 43.4 %copy-start.21 = (f32[256,128]{1,0:T(8,128)S(1)}, f32[256,128]{1,0:T(8,128)}, u32[]{:S(2)}) copy-start(f32[256,128]{1,0:T(8,128)} %copy-done.20) | copy-start | bytes 393220
  1425.0 43.5 %copy-start.6 = (bf16[512,2048]{1,0:T(8,128)(2,1)S(1)}, bf16[512,2048]{1,0:T(8,128)(2,1)}, u32[]{:S(2)}) copy-start(bf16[512,2048]{1,0:T(8,128)(2,1)} %shard_map.240) | copy-start | bytes 6291460
  1467.8 107.6 %reduce-scatter.29.cloned.1.call-start = ((), (), s32[]{:S(2)}) async-start(), calls=%async_computation.35 | async-start | bytes 4718592 | tf_op jit(solution)/shard_map/reduce_scatter | solution.py:627
  1481.1 34.4 %copy-start.65 = (f32[128]{0:T(128)S(1)}, f32[128]{0:T(128)}, u32[]{:S(2)}) copy-start(f32[128]{0:T(128)} %param.23) | copy-start | bytes 1540
  1524.5 286.0 %reduce-scatter.25.cloned.1.call-start = ((), (), s32[]{:S(2)}) async-start(), calls=%async_computation.33 | async-start | bytes 18874368 | tf_op jit(solution)/shard_map/reduce_scatter | solution.py:627
  1540.7 346.1 %reduce-scatter.33.cloned.1.call-start = ((), (), s32[]{:S(2)}) async-start(), calls=%async_computation.37 | async-start | bytes 18874368 | tf_op jit(solution)/shard_map/reduce_scatter | solution.py:627
  1569.9 166.7 %all-to-all-start.7 = ((bf16[8,320,2048]{2,1,0:T(8,128)(2,1)}), bf16[8,320,2048]{2,1,0:T(8,128)(2,1)}, u32[]{:S(2)}, u32[]{:S(2)}) async-start(bf16[8,320,2048]{2,1,0:T(8,128)(2,1)} %bitcast.270), calls=%async_computation.9 | async-start | bytes 20971520 | tf_op jit(solution)/shard_map/all_to_all | solution.py:521
  1575.1 379.4 %reduce-scatter.31.cloned.1.call-start = ((), (), s32[]{:S(2)}) async-start(), calls=%async_computation.36 | async-start | bytes 655360 | tf_op jit(solution)/shard_map/reduce_scatter | solution.py:628
  1575.7 413.2 %reduce-scatter.19.cloned.1.call-start = ((), (), s32[]{:S(2)}) async-start(), calls=%async_computation.30 | async-start | bytes 5242880 | tf_op jit(solution)/shard_map/reduce_scatter | solution.py:540
  1750.4 60.1 %all-to-all-start.8 = ((f32[8,2,4,80]{3,2,1,0:T(4,128)}), f32[8,2,4,80]{3,2,1,0:T(4,128)S(1)}, u32[]{:S(2)}, u32[]{:S(2)}) async-start(f32[8,2,4,80]{3,2,1,0:T(4,128)} %copy.148), calls=%async_computation.14 | async-start | bytes 65536 | tf_op jit(solution)/shard_map/all_to_all | solution.py:655
  1753.8 281.6 %reduce-scatter.27.cloned.1.call-start = ((), (), s32[]{:S(2)}) async-start(), calls=%async_computation.34 | async-start | bytes 2621440 | tf_op jit(solution)/shard_map/reduce_scatter | solution.py:628
  1780.9 29.6 %copy-start.35 = (s32[8,4,256]{2,0,1:T(8,128)S(1)}, s32[8,4,256]{2,0,1:T(8,128)}, u32[]{:S(2)}) copy-start(s32[8,4,256]{2,0,1:T(8,128)} %copy-done.34) | copy-start | bytes 98308
  1812.8 30.4 %all-to-all-start.9 = ((f32[4,2,256,8]{2,3,1,0:T(8,128)}), f32[4,2,256,8]{2,3,1,0:T(8,128)S(1)}, u32[]{:S(2)}, u32[]{:S(2)}) async-start(f32[4,2,256,8]{2,3,1,0:T(8,128)} %maximum_bitcast_fusion.2), calls=%async_computation.15 | async-start | bytes 131072 | tf_op jit(solution)/shard_map/all_to_all | solution.py:669
  1816.1 264.7 %reduce-scatter.35.cloned.1.call-start = ((), (), s32[]{:S(2)}) async-start(), calls=%async_computation.38 | async-start | bytes 2621440 | tf_op jit(solution)/shard_map/reduce_scatter | solution.py:628
  1816.2 28.5 %copy-start.69 = (f32[128]{0:T(128)S(1)}, f32[128]{0:T(128)}, u32[]{:S(2)}) copy-start(f32[128]{0:T(128)} %get-tuple-element.105) | copy-start | bytes 1540
  1844.7 42.1 %copy-start.4 = (bf16[2,1,256,2048]{3,2,1,0:T(8,128)(2,1)S(1)}, bf16[2,1,256,2048]{3,2,1,0:T(8,128)(2,1)}, u32[]{:S(2)}) copy-start(bf16[2,1,256,2048]{3,2,1,0:T(8,128)(2,1)} %param.16) | copy-start | bytes 6291460
  1844.7 42.1 %copy-start.49 = (f32[2048]{0:T(1024)S(1)}, f32[2048]{0:T(1024)}, u32[]{:S(2)}) copy-start(f32[2048]{0:T(1024)} %param.20) | copy-start | bytes 24580
  1947.2 41.7 %copy-start.2 = (f32[256,2048]{1,0:T(8,128)S(1)}, f32[256,2048]{1,0:T(8,128)}, u32[]{:S(2)}) copy-start(f32[256,2048]{1,0:T(8,128)} %copy-done) | copy-start | bytes 6291460
  1954.5 35.9 %copy-start.13 = (bf16[1,256,2048]{2,1,0:T(8,128)(2,1)S(1)}, bf16[1,256,2048]{2,1,0:T(8,128)(2,1)}, u32[]{:S(2)}) copy-start(bf16[1,256,2048]{2,1,0:T(8,128)(2,1)} %get-tuple-element.121) | copy-start | bytes 3145732
  (50 other events, 432.0 us)
Sparse Core Ops, SparseCore 0:
  14.5 110.2 all-gather.5
  204.4 80.7 all-gather.7
  287.2 196.3 all-gather.9
  532.5 109.9 all-gather.11
  662.2 79.7 all-gather.13
  1034.9 75.6 reduce-scatter.14
  1156.4 75.6 reduce-scatter.16
  1272.8 73.4 reduce-scatter.12
  1406.8 44.3 reduce-scatter.22
  1467.9 44.3 reduce-scatter.20
  1524.6 50.6 reduce-scatter.28
  1578.7 188.3 reduce-scatter.24
  1770.7 115.9 reduce-scatter.32
  1888.9 21.6 reduce-scatter.30
  1912.7 76.1 reduce-scatter.18
  1991.2 44.2 reduce-scatter.26
  2037.6 43.1 reduce-scatter.34

commit v3 on v2

--- a/solution.py
+++ b/solution.py
@@ -12,6 +12,7 @@
 ROPE_BASE = 1000000.0
 MASKED = -1e30
 VMEM_BYTES = 56 * 2**20
+SMALL = pl.CostEstimate(flops=2**20, bytes_accessed=2**20, transcendentals=0)
 
 
 def norm_rows(value, gain):
@@ -120,7 +121,7 @@
                     passing(way, step, i, me - sign * step).wait_send()
 
 
-def line_gather(*blocks):
+def line_gather(*blocks, number):
     count = lax.axis_size("ctx")
     arrays = len(blocks)
     return pl.pallas_call(
@@ -136,7 +137,7 @@
             pltpu.SemaphoreType.DMA((2, count - 1, arrays)),
             pltpu.SemaphoreType.DMA((arrays,)),
         ],
-        compiler_params=pltpu.CompilerParams(collective_id=0, has_side_effects=True),
+        compiler_params=pltpu.CompilerParams(collective_id=number, has_side_effects=True),
         cost_estimate=pl.CostEstimate(flops=0, bytes_accessed=200 * 2**20, transcendentals=0),
     )(*blocks)
 
@@ -172,10 +173,10 @@
     )
 
 
-def run_expert(rows, grad, gate, up, down):
-    total, width = rows.shape
+def run_expert(rows, grad, gate, up, down, step):
+    sources, block, width = rows.shape
     units = gate.shape[1]
-    block = 256 if total % 256 == 0 else total
+    total = sources * block
     wide = pl.BlockSpec((block, width), lambda i: (i, 0))
     narrow = pl.BlockSpec((block, units), lambda i: (i, 0))
 
@@ -186,16 +187,18 @@
     full = jax.ShapeDtypeStruct((total, width), jnp.bfloat16)
     return pl.pallas_call(
         expert_kernel,
-        grid=(total // block,),
-        in_specs=[wide, wide, whole(gate.shape), whole(up.shape), whole(down.shape)],
+        grid=(sources,),
+        in_specs=[
+            pl.BlockSpec((None, block, width), lambda i: (i, 0, 0)),
+            pl.BlockSpec((None, None, block, width), lambda i: (i, step, 0, 0)),
+            whole(gate.shape),
+            whole(up.shape),
+            whole(down.shape),
+        ],
         out_specs=(narrow, narrow, narrow, wide, wide, pl.BlockSpec((block, 1), lambda i: (i, 0))),
         out_shape=(low, low, low, full, full, jax.ShapeDtypeStruct((total, 1), jnp.float32)),
         compiler_params=pltpu.CompilerParams(vmem_limit_bytes=VMEM_BYTES),
-        cost_estimate=pl.CostEstimate(
-            flops=14 * total * width * units,
-            bytes_accessed=8 * total * width,
-            transcendentals=total * units,
-        ),
+        cost_estimate=SMALL,
     )(rows, grad, gate, up, down)
 
 
@@ -248,12 +251,77 @@
         out_specs=pl.BlockSpec((part, 1, capacity, width), lambda c, g: (g, c, 0, 0)),
         out_shape=jax.ShapeDtypeStruct((planned, count, capacity, width), jnp.bfloat16),
         compiler_params=pltpu.CompilerParams(vmem_limit_bytes=VMEM_BYTES),
-        cost_estimate=pl.CostEstimate(
-            flops=2 * count * planned * capacity * local * width,
-            bytes_accessed=2 * count * planned * capacity * width,
-            transcendentals=0,
-        ),
+        cost_estimate=SMALL,
     )(place.reshape(shape), weight.reshape(shape), blocks)
+
+
+def weight_kernel(steps, micro, *refs):
+    rows, (grads_ref,) = refs[:micro], refs[micro : micro + 1]
+    actives, gates, ups = (refs[micro * i + 1 : micro * i + 1 + micro] for i in (1, 2, 3))
+    gate_ref, up_ref, down_ref = refs[4 * micro + 1 :]
+    step = pl.program_id(0)
+
+    def add(which, fresh):
+        x = rows[which][...]
+        for out_ref, left, right in (
+            (gate_ref, x, gates[which][...]),
+            (up_ref, x, ups[which][...]),
+            (down_ref, actives[which][...], grads_ref[...]),
+        ):
+            term = lax.dot_general(
+                left, right, (((0,), (0,)), ((), ())), preferred_element_type=jnp.float32
+            )
+            if fresh:
+                out_ref[0] = term
+            else:
+                out_ref[0] += term
+
+    pl.when(step == 0)(lambda: add(0, True))
+    pl.when((step > 0) & (step < steps))(lambda: add(0, False))
+    for which in range(1, micro):
+        pl.when((step >= which * steps) & (step < (which + 1) * steps))(
+            functools.partial(add, which, False)
+        )
+
+
+def expert_weight_grads(rows, grads, actives, gates, ups):
+    sources, micro, block, width = grads.shape
+    units = gates[0].shape[1]
+
+    def turn(i, which):
+        return jnp.clip(i - which * sources, 0, sources - 1)
+
+    def specs(size):
+        return [
+            pl.BlockSpec((block, size), functools.partial(lambda w, i: (turn(i, w), 0), which))
+            for which in range(micro)
+        ]
+
+    def row_specs():
+        return [
+            pl.BlockSpec(
+                (None, block, width), functools.partial(lambda w, i: (turn(i, w), 0, 0), which)
+            )
+            for which in range(micro)
+        ]
+
+    shapes = [(1, width, units), (1, width, units), (1, units, width)]
+    return pl.pallas_call(
+        functools.partial(weight_kernel, sources, micro),
+        grid=(micro * sources,),
+        in_specs=row_specs()
+        + [
+            pl.BlockSpec(
+                (None, None, block, width),
+                lambda i: (lax.rem(i, sources), lax.div(i, sources), 0, 0),
+            )
+        ]
+        + specs(units) * 3,
+        out_specs=[pl.BlockSpec(shape, lambda i: (0, 0, 0)) for shape in shapes],
+        out_shape=[jax.ShapeDtypeStruct(shape, jnp.float32) for shape in shapes],
+        compiler_params=pltpu.CompilerParams(vmem_limit_bytes=VMEM_BYTES),
+        cost_estimate=SMALL,
+    )(*rows, grads, *actives, *gates, *ups)
 
 
 def fill_mask(place_ref, mask_ref):
@@ -308,11 +376,117 @@
         out_ref[:, columns] = result.T.astype(jnp.bfloat16)
 
 
+class PlaneExchange:
+    def __init__(self, count, rows_ref, out_ref, send_sem, recv_sem, own_sem):
+        self.count, self.rows_ref, self.out_ref = count, rows_ref, out_ref
+        self.send_sem, self.recv_sem, self.own_sem = send_sem, recv_sem, own_sem
+        self.me = lax.axis_index("exp")
+
+    @staticmethod
+    def scratch(count):
+        return [
+            pltpu.SemaphoreType.DMA((count,)),
+            pltpu.SemaphoreType.DMA((count,)),
+            pltpu.SemaphoreType.DMA,
+        ]
+
+    def passing(self, k, part):
+        return pltpu.make_async_remote_copy(
+            src_ref=self.rows_ref.at[lax.rem(self.me + k, self.count)],
+            dst_ref=self.out_ref.at[part],
+            send_sem=self.send_sem.at[k],
+            recv_sem=self.recv_sem.at[k],
+            device_id={"exp": lax.rem(self.me + k, self.count)},
+            device_id_type=pl.DeviceIdType.MESH,
+        )
+
+    def kept(self):
+        return pltpu.make_async_copy(
+            self.rows_ref.at[self.me], self.out_ref.at[self.me], self.own_sem
+        )
+
+    def begin(self):
+        for k in range(1, self.count):
+            self.passing(k, self.me).start()
+        self.kept().start()
+
+    def finish(self):
+        self.kept().wait()
+        for k in range(1, self.count):
+            self.passing(k, lax.rem(self.me + self.count - k, self.count)).wait_recv()
+        for k in range(1, self.count):
+            self.passing(k, self.me).wait_send()
+
+
+def greet(**counts):
+    barrier = pltpu.get_barrier_semaphore()
+    for axis, count in counts.items():
+        me = lax.axis_index(axis)
+        for k in range(1, count):
+            pl.semaphore_signal(
+                barrier,
+                inc=1,
+                device_id={axis: lax.rem(me + k, count)},
+                device_id_type=pl.DeviceIdType.MESH,
+            )
+    pl.semaphore_wait(barrier, sum(counts.values()) - len(counts))
+
+
+class RowExchange:
+    def __init__(self, ring, held_ref, out_ref, send_sem, recv_sem, own_sem):
+        self.ring, self.held_ref, self.out_ref = ring, held_ref, out_ref
+        self.send_sem, self.recv_sem, self.own_sem = send_sem, recv_sem, own_sem
+        self.me = lax.axis_index("ctx")
+        self.rows = out_ref.shape[2]
+
+    @staticmethod
+    def scratch(ring, groups):
+        return [
+            pltpu.SemaphoreType.DMA((groups, ring)),
+            pltpu.SemaphoreType.DMA((groups, ring)),
+            pltpu.SemaphoreType.DMA((groups,)),
+        ]
+
+    def held(self, group, at):
+        return self.held_ref.at[group, pl.ds(at * self.rows, self.rows)]
+
+    def passing(self, group, k, part):
+        to = lax.rem(self.me + k, self.ring)
+        return pltpu.make_async_remote_copy(
+            src_ref=self.held(group, to),
+            dst_ref=self.out_ref.at[part, group],
+            send_sem=self.send_sem.at[group, k],
+            recv_sem=self.recv_sem.at[group, k],
+            device_id={"ctx": to},
+            device_id_type=pl.DeviceIdType.MESH,
+        )
+
+    def kept(self, group):
+        return pltpu.make_async_copy(
+            self.held(group, self.me), self.out_ref.at[self.me, group], self.own_sem.at[group]
+        )
+
+    def begin(self, group):
+        for k in range(1, self.ring):
+            self.passing(group, k, self.me).start()
+        self.kept(group).start()
+
+    def finish(self):
+        for group in range(self.out_ref.shape[1]):
+            self.kept(group).wait()
+            for k in range(1, self.ring):
+                self.passing(group, k, lax.rem(self.me + self.ring - k, self.ring)).wait_recv()
+            for k in range(1, self.ring):
+                self.passing(group, k, self.me).wait_send()
+
+
 def attend_back_kernel(
     per,
     steps,
     factor,
     scale,
+    count,
+    ring,
     place_ref,
     raw_ref,
     grad_ref,
@@ -320,15 +494,26 @@
     gain_ref,
     cos_ref,
     sin_ref,
+    rows_ref,
     raw_grad_ref,
-    both_grad_ref,
+    landed_ref,
     gain_grad_ref,
+    moved_ref,
     mask_ref,
     turned_ref,
     sums_ref,
+    held_ref,
+    *sems,
 ):
     width = gain_ref.shape[1]
     group_step, step = pl.program_id(0), pl.program_id(1)
+    moving = PlaneExchange(count, rows_ref, moved_ref, *sems[:3])
+    landing = RowExchange(ring, held_ref, landed_ref, *sems[3:])
+
+    @pl.when((group_step == 0) & (step == 0))
+    def _():
+        greet(exp=count, ctx=ring)
+        moving.begin()
 
     @pl.when((group_step == 0) & (step == 0))
     def _():
@@ -362,8 +547,14 @@
 
     @pl.when(step == steps - 1)
     def _():
-        both_grad_ref[:, :width] = (sums_ref[:, :width] * scale).astype(jnp.bfloat16)
-        both_grad_ref[:, width:] = sums_ref[:, width:].astype(jnp.bfloat16)
+        held_ref[group_step, :, :width] = (sums_ref[:, :width] * scale).astype(jnp.bfloat16)
+        held_ref[group_step, :, width:] = sums_ref[:, width:].astype(jnp.bfloat16)
+        landing.begin(group_step)
+
+    @pl.when((group_step == pl.num_programs(0) - 1) & (step == steps - 1))
+    def _():
+        landing.finish()
+        moving.finish()
 
 
 def attention_specs(raw, both, width, rows, step, per):
@@ -377,8 +568,7 @@
         place=pl.BlockSpec(memory_space=pltpu.SMEM),
         raw=pl.BlockSpec((rows, per * width), lambda g, j: (step, g * steps + j)),
         heads=wide,
-        both=pl.BlockSpec((count, rows, 2 * width), lambda g, j: (0, step, g)),
-        both_grad=pl.BlockSpec((keys, 2 * width), lambda g, j: (0, g)),
+        both=pl.BlockSpec((count, rows, 2 * width), lambda g, j: (0, 0, g)),
         gain=pl.BlockSpec((1, width), lambda g, j: (0, 0)),
         table=pl.BlockSpec((rows, width), lambda g, j: (0, 0)),
     )
@@ -403,43 +593,276 @@
             pltpu.VMEM((width, keys), jnp.bfloat16),
         ],
         compiler_params=params,
-        cost_estimate=pl.CostEstimate(
-            flops=4 * work, bytes_accessed=4 * rows * heads * width, transcendentals=work // width
-        ),
+        cost_estimate=SMALL,
     )(place, raw, both, gain, cosine, sine)
 
 
-def attend_back(raw, grad, both, gain, cosine, sine, place, step, per=2):
+def attend_back(raw, grad, both, gain, cosine, sine, place, step, rows_out, per=2):
     rows, width = cosine.shape
     kv_heads, heads, steps, keys, specs, params, work = attention_specs(
         raw, both, width, rows, step, per
     )
+    count = rows_out.shape[0]
+    anywhere = pl.BlockSpec(memory_space=pl.ANY)
     return pl.pallas_call(
         functools.partial(
-            attend_back_kernel, per, steps, width ** (-0.5) * math.log2(math.e), width ** (-0.5)
+            attend_back_kernel,
+            per,
+            steps,
+            width ** (-0.5) * math.log2(math.e),
+            width ** (-0.5),
+            count,
+            both.shape[0],
         ),
         grid=(kv_heads, steps),
-        in_specs=[specs[k] for k in ("place", "raw", "heads", "both", "gain", "table", "table")],
+        in_specs=[specs[k] for k in ("place", "raw", "heads", "both", "gain", "table", "table")]
+        + [anywhere],
         out_specs=(
             specs["heads"],
-            specs["both_grad"],
+            anywhere,
             pl.BlockSpec((8, width), lambda g, j: (0, 0)),
+            anywhere,
         ),
         out_shape=(
             jax.ShapeDtypeStruct((rows, heads * width), jnp.bfloat16),
-            jax.ShapeDtypeStruct((keys, both.shape[2]), jnp.bfloat16),
+            jax.ShapeDtypeStruct((both.shape[0], kv_heads, rows, 2 * width), jnp.bfloat16),
             jax.ShapeDtypeStruct((8, width), jnp.float32),
+            jax.ShapeDtypeStruct(rows_out.shape, rows_out.dtype),
         ),
         scratch_shapes=[
             pltpu.VMEM((keys, rows), jnp.float32),
             pltpu.VMEM((width, keys), jnp.bfloat16),
             pltpu.VMEM((keys, 2 * width), jnp.float32),
+            pltpu.VMEM((kv_heads, keys, 2 * width), jnp.bfloat16),
+        ]
+        + PlaneExchange.scratch(count)
+        + RowExchange.scratch(both.shape[0], kv_heads),
+        compiler_params=pltpu.CompilerParams(
+            vmem_limit_bytes=VMEM_BYTES, collective_id=1 + step, has_side_effects=True
+        ),
+        cost_estimate=SMALL,
+    )(place, raw, grad, both, gain, cosine, sine, rows_out)
+
+
+class GradSums:
+    def __init__(self, ring, sizes, refs):
+        self.ring = ring
+        self.sizes = sizes
+        kinds = len(sizes)
+        self.left, self.right = refs[:kinds], refs[kinds : 2 * kinds]
+        self.out = refs[2 * kinds : 3 * kinds]
+        scratch = refs[3 * kinds :]
+        self.left_v, self.right_v = scratch[:kinds], scratch[kinds : 2 * kinds]
+        self.part, self.first, self.second, self.last = (
+            scratch[(2 + i) * kinds : (3 + i) * kinds] for i in range(4)
+        )
+        self.load_sem, self.first_sem, self.second_sem, self.last_sem = scratch[6 * kinds :]
+        e = lax.axis_index("exp")
+        self.y, self.x = lax.div(e, 4), lax.rem(lax.div(e, 2), 2)
+        self.across_x, self.across_y = e + 2 - 4 * self.x, e + 4 - 8 * self.y
+        self.z = lax.axis_index("ctx")
+        self.order = [
+            (kind, chunk) for kind, size in enumerate(sizes) for chunk in range(size[2] // size[3])
+        ]
+
+    @staticmethod
+    def scratch(ring, sizes):
+        chunks = [size[2] // size[3] for size in sizes]
+        total = sum(chunks)
+        shapes = [pltpu.VMEM((4, size[0], size[1]), jnp.bfloat16) for size in sizes]
+        shapes += [pltpu.VMEM((2, size[0], size[3]), jnp.bfloat16) for size in sizes]
+        for lead, share in (((4,), 1), ((2,), 1), ((), 1), ((ring,), ring)):
+            for size, count in zip(sizes, chunks):
+                shapes.append(
+                    pltpu.VMEM((count,) + lead + (size[1] // share, size[3]), jnp.bfloat16)
+                )
+        shapes += [
+            pltpu.SemaphoreType.DMA((len(sizes) + total,)),
+            pltpu.SemaphoreType.DMA((2, total, 2)),
+            pltpu.SemaphoreType.DMA((2, total)),
+            pltpu.SemaphoreType.DMA((2, total, ring)),
+        ]
+        return shapes
+
+    def x_first(self, i):
+        return i % 2 == 0
+
+    def load(self, i):
+        kind, chunk = self.order[i]
+        wide = self.sizes[kind][3]
+        return pltpu.make_async_copy(
+            self.right[kind].at[:, pl.ds(chunk * wide, wide)],
+            self.right_v[kind].at[chunk % 2],
+            self.load_sem.at[len(self.sizes) + i],
+        )
+
+    def load_left(self, kind):
+        return pltpu.make_async_copy(
+            self.left[kind], self.left_v[kind], self.load_sem.at[kind]
+        )
+
+    def step_first(self, i, k):
+        kind, chunk = self.order[i]
+        if self.x_first(i):
+            piece, to = 2 * k + 1 - self.x, self.across_x
+        else:
+            piece, to = 2 * (1 - self.y) + k, self.across_y
+        return pltpu.make_async_remote_copy(
+            src_ref=self.part[kind].at[chunk, piece],
+            dst_ref=self.first[kind].at[chunk, k],
+            send_sem=self.first_sem.at[0, i, k],
+            recv_sem=self.first_sem.at[1, i, k],
+            device_id={"exp": to},
+            device_id_type=pl.DeviceIdType.MESH,
+        )
+
+    def step_second(self, i):
+        kind, chunk = self.order[i]
+        if self.x_first(i):
+            piece, to = 2 * (1 - self.y) + self.x, self.across_y
+        else:
+            piece, to = 2 * self.y + 1 - self.x, self.across_x
+        return pltpu.make_async_remote_copy(
+            src_ref=self.part[kind].at[chunk, piece],
+            dst_ref=self.second[kind].at[chunk],
+            send_sem=self.second_sem.at[0, i],
+            recv_sem=self.second_sem.at[1, i],
+            device_id={"exp": to},
+            device_id_type=pl.DeviceIdType.MESH,
+        )
+
+    def mine(self, i):
+        kind, chunk = self.order[i]
+        return self.part[kind].at[chunk, 2 * self.y + self.x]
+
+    def step_last(self, i, k, slot):
+        kind, chunk = self.order[i]
+        to = lax.rem(self.z + k, self.ring)
+        rows = self.sizes[kind][1] // self.ring
+        return pltpu.make_async_remote_copy(
+            src_ref=self.mine(i).at[pl.ds(to * rows, rows)],
+            dst_ref=self.last[kind].at[chunk, slot],
+            send_sem=self.last_sem.at[0, i, k],
+            recv_sem=self.last_sem.at[1, i, k],
+            device_id={"ctx": to},
+            device_id_type=pl.DeviceIdType.MESH,
+        )
+
+    def multiply(self, i):
+        kind, chunk = self.order[i]
+        self.load(i).wait()
+
+        def piece(p, carry):
+            term = lax.dot_general(
+                self.left_v[kind][p],
+                self.right_v[kind][chunk % 2],
+                (((0,), (0,)), ((), ())),
+                preferred_element_type=jnp.float32,
+            )
+            self.part[kind][chunk, p] = term.astype(jnp.bfloat16)
+            return carry
+
+        lax.fori_loop(0, 4, piece, 0)
+        for k in range(2):
+            self.step_first(i, k).start()
+
+    def add_first(self, i):
+        kind, chunk = self.order[i]
+        for k in range(2):
+            self.step_first(i, k).wait_recv()
+        for k in range(2):
+            piece = 2 * k + self.x if self.x_first(i) else 2 * self.y + k
+            self.part[kind][chunk, piece] = (
+                self.part[kind][chunk, piece].astype(jnp.float32)
+                + self.first[kind][chunk, k].astype(jnp.float32)
+            ).astype(jnp.bfloat16)
+        self.step_second(i).start()
+
+    def add_second(self, i):
+        kind, chunk = self.order[i]
+        self.step_second(i).wait_recv()
+        piece = 2 * self.y + self.x
+        self.part[kind][chunk, piece] = (
+            self.part[kind][chunk, piece].astype(jnp.float32)
+            + self.second[kind][chunk].astype(jnp.float32)
+        ).astype(jnp.bfloat16)
+        for k in range(1, self.ring):
+            self.step_last(i, k, k).start()
+
+    def add_last(self, i):
+        kind, chunk = self.order[i]
+        rows, wide = self.sizes[kind][1] // self.ring, self.sizes[kind][3]
+        for k in range(1, self.ring):
+            self.step_last(i, k, k).wait_recv()
+        total = self.part[kind][
+            chunk, 2 * self.y + self.x, pl.ds(pl.multiple_of(self.z * rows, rows), rows), :
+        ].astype(jnp.float32)
+        for k in range(1, self.ring):
+            total += self.last[kind][chunk, k].astype(jnp.float32)
+        self.out[kind][:, chunk * wide : (chunk + 1) * wide] = total
+
+    def run(self):
+        chunks = len(self.order)
+        for kind in range(len(self.sizes)):
+            self.load_left(kind).start()
+        self.load(0).start()
+        barrier = pltpu.get_barrier_semaphore()
+        for other in (self.across_x, self.across_y):
+            pl.semaphore_signal(
+                barrier, inc=1, device_id={"exp": other}, device_id_type=pl.DeviceIdType.MESH
+            )
+        for k in range(1, self.ring):
+            pl.semaphore_signal(
+                barrier,
+                inc=1,
+                device_id={"ctx": lax.rem(self.z + k, self.ring)},
+                device_id_type=pl.DeviceIdType.MESH,
+            )
+        pl.semaphore_wait(barrier, self.ring + 1)
+        for i in range(chunks + 6):
+            if i < chunks:
+                if i + 1 < chunks:
+                    self.load(i + 1).start()
+                if self.order[i][1] == 0:
+                    self.load_left(self.order[i][0]).wait()
+                self.multiply(i)
+            if 0 <= i - 2 < chunks:
+                self.add_first(i - 2)
+            if 0 <= i - 4 < chunks:
+                self.add_second(i - 4)
+            if 0 <= i - 6 < chunks:
+                self.add_last(i - 6)
+        for i in range(chunks):
+            for k in range(2):
+                self.step_first(i, k).wait_send()
+            self.step_second(i).wait_send()
+            for k in range(1, self.ring):
+                self.step_last(i, k, k).wait_send()
+
+
+def grad_sums_kernel(ring, sizes, *refs):
+    GradSums(ring, sizes, refs).run()
+
+
+def grad_sums(ring, lefts, rights, wides, number):
+    sizes = [
+        (left.shape[1], left.shape[2], right.shape[1], wide)
+        for left, right, wide in zip(lefts, rights, wides)
+    ]
+    anywhere = pl.BlockSpec(memory_space=pl.ANY)
+    return pl.pallas_call(
+        functools.partial(grad_sums_kernel, ring, sizes),
+        in_specs=[anywhere] * (2 * len(sizes)),
+        out_specs=[pl.BlockSpec(memory_space=pltpu.VMEM)] * len(sizes),
+        out_shape=[
+            jax.ShapeDtypeStruct((size[1] // ring, size[2]), jnp.float32) for size in sizes
         ],
-        compiler_params=params,
-        cost_estimate=pl.CostEstimate(
-            flops=10 * work, bytes_accessed=8 * rows * heads * width, transcendentals=work // width
+        scratch_shapes=GradSums.scratch(ring, sizes),
+        compiler_params=pltpu.CompilerParams(
+            vmem_limit_bytes=60 * 2**20, collective_id=number, has_side_effects=True
         ),
-    )(place, raw, grad, both, gain, cosine, sine)
+        cost_estimate=SMALL,
+    )(*lefts, *rights)
 
 
 def per_device(
@@ -501,7 +924,7 @@
 
     meta = jnp.concatenate([routes[:, 0].astype(jnp.float32), route_weights[:, 0]], -1)
     grads_low = [cotangent[step, 0] for step in range(micro)]
-    *grad_blocks, meta = line_gather(*grads_low, meta.reshape(-1, 128))
+    *grad_blocks, meta = line_gather(*grads_low, meta.reshape(-1, 128), number=0)
     meta = meta.reshape(ring, micro, local, 2 * top)
     tables = [
         plane_tables(
@@ -514,18 +937,13 @@
         place.transpose(1, 0, 2)[:, :, None, :] == slots[None, None, :, None] for place, _ in tables
     ]
 
-    def exchange(rows, *waits):
-        if waits:
-            rows = after(rows, *waits)
-        rows = rows.reshape(plane, ring * capacity, width)
-        return lax.all_to_all(rows, "exp", split_axis=0, concat_axis=0, tiled=True).reshape(
-            plane * ring * capacity, width
-        )
+    def exchange(rows):
+        return lax.all_to_all(rows, "exp", split_axis=0, concat_axis=0, tiled=True)
 
     def pick(blocks, step, weighted):
         return pick_rows(*tables[step], blocks, capacity, weighted)
 
-    def from_experts(back, step, weighted):
+    def combine(back, step, weighted):
         back = back.reshape(plane, ring, capacity, width)
         factor = chosen[step]
         if weighted:
@@ -537,20 +955,25 @@
             back,
             preferred_element_type=jnp.float32,
         )
-        return lax.psum_scatter(
-            part.astype(jnp.bfloat16).reshape(seq_len, width),
-            "ctx",
-            scatter_dimension=0,
-            tiled=True,
-        ).astype(jnp.float32)
-
-    incoming = [exchange(pick(grad_blocks[0], 0, True))]
-    for step in range(1, micro):
-        incoming.append(exchange(pick(grad_blocks[step], step, True), incoming[-1]))
+        return part.astype(jnp.bfloat16).reshape(seq_len, width)
+
+    def scatter(part):
+        return lax.psum_scatter(part, "ctx", scatter_dimension=0, tiled=True).astype(jnp.float32)
+
+    picked = pick_rows(
+        jnp.concatenate([place for place, _ in tables]),
+        jnp.concatenate([weight for _, weight in tables]),
+        jnp.concatenate(grad_blocks),
+        capacity,
+        True,
+    )
+    incoming = exchange(picked.reshape(plane, micro * ring * capacity, width)).reshape(
+        plane, micro, ring * capacity, width
+    )
 
     rows = tokens[:, 0].astype(jnp.float32).reshape(micro * local, width)
     hidden, first_scale = norm_rows(rows, norm_attn)
-    hidden = after(hidden.astype(jnp.bfloat16), grad_blocks[0])
+    hidden = after(hidden.astype(jnp.bfloat16), picked)
     raw = dot(hidden, in_weight)
     pair_raw = raw[:, query_width:].reshape(micro * local, kv_heads, 2, head_dim)
     key_raw = pair_raw[:, :, 0]
@@ -561,94 +984,144 @@
     pairs = jnp.stack([keys, pair_raw[:, :, 1].astype(jnp.bfloat16)], 2).reshape(
         micro * local, 2 * pair_width
     )
-    both = lax.all_gather(pairs, "ctx", axis=0)
     gain_row = q_gain[None, :]
-    places, attended, middles, feeds, scales = [], [], [], [], []
+    both, places, attended, middles, feeds, scales = [], [], [], [], [], []
     for step in range(micro):
         part = slice(step * local, (step + 1) * local)
+        own_pairs = pairs[part]
+        if feeds:
+            own_pairs = after(own_pairs, feeds[-1])
+        (gathered,) = line_gather(own_pairs, number=3 + step)
+        both.append(gathered.reshape(ring, local, 2 * pair_width))
         places.append(jnp.stack([base, bounds[step, 0]]).astype(jnp.int32))
-        attended.append(attend(raw, both, gain_row, cosine, sine, places[step], step))
+        attended.append(attend(raw, both[step], gain_row, cosine, sine, places[step], step))
         middles.append(rows[part] + dot(attended[step], out_weight))
         feed_in, second_scale = norm_rows(middles[step], norm_ffn)
         feeds.append(feed_in.astype(jnp.bfloat16))
         scales.append(second_scale)
     feed_blocks = [lax.all_gather(feed, "ctx", axis=0, tiled=True) for feed in feeds]
 
+    def slotted(rows):
+        return rows.reshape(plane, ring * capacity, width)
+
     received = []
-    last = incoming[-1]
+    last = incoming
     for step in range(micro):
-        received.append(exchange(pick(feed_blocks[step], step, False), last))
+        received.append(exchange(after(slotted(pick(feed_blocks[step], step, False)), last)))
         last = received[-1]
 
     active, gate_grad, up_grad, produced, backs, pair_values = [], [], [], [], [], []
     for step in range(micro):
-        parts = run_expert(received[step], incoming[step], gate_weight, up_weight, down_weight)
+        parts = run_expert(received[step], incoming, gate_weight, up_weight, down_weight, step)
         for held, item in zip((active, gate_grad, up_grad, produced, backs, pair_values), parts):
             held.append(item)
 
     returned = []
     for step in range(micro):
-        returned.append(exchange(backs[step], last))
+        returned.append(exchange(after(slotted(backs[step]), last)))
         last = returned[-1]
+    gate_term, up_term, down_term = expert_weight_grads(
+        received, incoming, active, gate_grad, up_grad
+    )
+    returned[-1] = after(returned[-1], down_term)
+    parts = [combine(returned[step], step, False) for step in range(micro)]
 
     branches, raw_grads, middle_grads, gain_list, results = [], [], [], [], []
+    waits = (parts[-1],)
     for step in range(micro):
-        results.append(exchange(produced[step], last, *raw_grads))
-        last = results[-1]
-        part = slice(step * local, (step + 1) * local)
-        feed_grad = from_experts(returned[step], step, False)
-        middle_norm_grad, second_gain = norm_back(middles[step], scales[step], norm_ffn, feed_grad)
+        middle_norm_grad, second_gain = norm_back(
+            middles[step], scales[step], norm_ffn, scatter(parts[step])
+        )
         middle_grads.append(grads_low[step].astype(jnp.float32) + middle_norm_grad)
         branches.append(middle_grads[step].astype(jnp.bfloat16))
         attended_grad = dot_t(branches[step], out_weight).astype(jnp.bfloat16)
-        raw_grad, pair_part, query_gain_part = attend_back(
-            raw, attended_grad, both, gain_row, cosine, sine, places[step], step
-        )
+        raw_grad, pair_part, query_gain_part, result = attend_back(
+            raw,
+            attended_grad,
+            both[step],
+            gain_row,
+            cosine,
+            sine,
+            places[step],
+            step,
+            after(slotted(produced[step]), *waits),
+        )
+        waits = (result,)
+        results.append(result)
         raw_grads.append(raw_grad)
         gain_list.append([jnp.sum(second_gain, 0), query_gain_part[0], pair_part])
     pair_grads = []
+    key_cos, key_sin = cosine[None], sine[None]
     for step in range(micro):
         part = slice(step * local, (step + 1) * local)
-        pair_grad = lax.psum_scatter(
-            gain_list[step][2], "ctx", scatter_dimension=0, tiled=True
-        ).reshape(local, kv_heads, 2, head_dim)
-        key_grad = pair_grad[:, :, 0].astype(jnp.float32)
-        key_turned = key_grad * cosine[:, None, :] - swap_halves(key_grad) * sine[:, None, :]
-        key_raw_grad, key_gain_part = norm_back(key_raw[part], key_scale[part], k_gain, key_turned)
-        pair_grad = jnp.stack([key_raw_grad.astype(jnp.bfloat16), pair_grad[:, :, 1]], 2)
-        pair_grads.append(pair_grad.reshape(local, 2 * pair_width))
+        landed = jnp.sum(gain_list[step][2].astype(jnp.float32), 0).astype(jnp.bfloat16)
+        key_grad = landed[..., :head_dim].astype(jnp.float32)
+        key_turned = key_grad * key_cos - swap_halves(key_grad) * key_sin
+        key_raw_grad, key_gain_part = norm_back(
+            key_raw[part].transpose(1, 0, 2), key_scale[part].transpose(1, 0, 2), k_gain, key_turned
+        )
+        pair_grad = jnp.concatenate(
+            [key_raw_grad.astype(jnp.bfloat16), landed[..., head_dim:]], -1
+        )
+        pair_grads.append(pair_grad.transpose(1, 0, 2).reshape(local, 2 * pair_width))
         gain_list[step][2] = jnp.sum(key_gain_part, (0, 1))
-    results[-1] = after(results[-1], raw_grads[-1])
-
-    def sum_over_devices(left, right):
-        share = left.shape[1] // experts
-        left = left.reshape(-1, ring, plane, share).transpose(0, 2, 1, 3)
-        term = t_dot(left.reshape(-1, experts * share), right)
-        term = lax.psum_scatter(term.astype(jnp.bfloat16), "exp", scatter_dimension=0, tiled=True)
-        return lax.psum_scatter(term, "ctx", scatter_dimension=0, tiled=True).astype(jnp.float32)
-
-    out_total = sum_over_devices(jnp.concatenate(attended, 0), jnp.concatenate(branches, 0))
-    query_grad, pair_grad = jnp.concatenate(raw_grads, 0), jnp.concatenate(pair_grads, 0)
-    query_total = sum_over_devices(hidden, query_grad)
-    pair_total = sum_over_devices(hidden, pair_grad).reshape(-1, kv_heads, 2, head_dim)
-    hidden_grad = dot_t(query_grad, in_weight[:, :query_width]) + dot_t(
-        pair_grad, in_weight[:, query_width:]
-    )
+
+    attended_all, branch_all = jnp.concatenate(attended, 0), jnp.concatenate(branches, 0)
+    raw_grad = jnp.concatenate(
+        [jnp.concatenate(raw_grads, 0), jnp.concatenate(pair_grads, 0)], 1
+    )
+    if plane == 8:
+        core = lax.rem(lax.axis_index("exp"), 2)
+
+        def swapped(array):
+            return lax.ppermute(array, "exp", [(i, i + 1 - 2 * (i % 2)) for i in range(plane)])
+
+        def left_part(array):
+            share = array.shape[1] // experts
+            array = array.reshape(-1, ring, 2, 2, 2, share).transpose(4, 2, 3, 0, 1, 5)
+            array = array.reshape(2, 4, micro * local, ring * share)
+            own = lax.dynamic_index_in_dim(array, core, 0, False)
+            other = lax.dynamic_index_in_dim(array, 1 - core, 0, False)
+            return jnp.concatenate([own, swapped(other)], 1)
+
+        def right_part(array):
+            return jnp.concatenate([array, swapped(array)], 0)
+
+        out_total, in_total = grad_sums(
+            ring,
+            (left_part(attended_all), left_part(hidden)),
+            (right_part(branch_all), right_part(raw_grad)),
+            (512, 1024),
+            5,
+        )
+    else:
+
+        def sum_over_devices(left, right):
+            share = left.shape[1] // experts
+            left = left.reshape(-1, ring, plane, share).transpose(0, 2, 1, 3)
+            term = t_dot(left.reshape(-1, experts * share), right).astype(jnp.bfloat16)
+            term = lax.psum_scatter(term, "exp", scatter_dimension=0, tiled=True)
+            return lax.psum_scatter(term, "ctx", scatter_dimension=0, tiled=True).astype(
+                jnp.float32
+            )
+
+        out_total = sum_over_devices(attended_all, branch_all)
+        in_total = sum_over_devices(hidden, raw_grad)
+    query_total = in_total[:, :query_width]
+    pair_total = in_total[:, query_width:].reshape(-1, kv_heads, 2, head_dim)
+    hidden_grad = dot_t(raw_grad, in_weight)
     first_grad, first_gain = norm_back(rows, first_scale, norm_attn, hidden_grad)
     tokens_grad = jnp.concatenate(middle_grads, 0) + first_grad
-    gain_total = lax.psum_scatter(
-        jnp.concatenate([jnp.sum(first_gain, 0)] + [sum(parts) for parts in zip(*gain_list)]),
-        ("ctx", "exp"),
-        scatter_dimension=0,
-        tiled=True,
-    )
-    received_all = jnp.concatenate(received, 0)
-    gate_term = t_dot(received_all, jnp.concatenate(gate_grad, 0))[None]
-    up_term = t_dot(received_all, jnp.concatenate(up_grad, 0))[None]
-    down_term = t_dot(jnp.concatenate(active, 0), jnp.concatenate(incoming, 0))[None]
+    gains = jnp.concatenate([jnp.sum(first_gain, 0)] + [sum(parts) for parts in zip(*gain_list)])
+    gain_total = jnp.sum(
+        lax.all_to_all(
+            gains.reshape(experts, -1), ("ctx", "exp"), split_axis=0, concat_axis=0, tiled=True
+        ),
+        0,
+    )
 
     outputs = [
-        (middles[step] + from_experts(results[step], step, True)).astype(jnp.bfloat16)
+        (middles[step] + scatter(combine(results[step], step, True))).astype(jnp.bfloat16)
         for step in range(micro)
     ]
 

time: 2100 us -> 1750 us (0.83)
  waiting for transfers between devices: 1160 us -> 393 us
  Pallas kernels: 443 us -> 959 us
  matrix products: 243 us -> 129 us
  other arithmetic: 55.1 us -> 116 us
  blocking collectives: 43.2 us -> 0 us
    all_to_all x8 -> x6, waiting for transfers between devices: 634 us -> 152 us  [the longest x5 151 us: exchange(): return lax.all_to_all(rows, 'exp', split_axis=0, concat_axis=0, tiled=True)]
    pallas_call x2 -> x4, Pallas kernels: 115 us -> 400 us  [the longest x1 192 us: grad_sums(): pl.pallas_call(functools.partial(grad_sums_kernel, ring, sizes), in_specs...]
    reduce_scatter x12 -> x4, waiting for transfers between devices: 251 us -> 73.6 us  [scatter(): lax.psum_scatter(part, 'ctx', scatter_dimension=0, tiled=True)]
    pallas_call x2, Pallas kernels: 85.5 us -> 238 us  [attend_back(): pl.pallas_call(functools.partial(attend_back_kernel, per, steps, width **...]
    dot_general x10 -> x4, matrix products: 153 us -> 37.8 us  [combine(): jnp.einsum('jcst,jcsd->ctd', factor.astype(jnp.bfloat16), back, preferred...]
    all_gather x1, waiting for transfers between devices: 84 us -> 0.02 us  [per_device(): out_weight = lax.all_gather(w_o, 'exp', axis=0, tiled=True)]
    pallas_call x1 -> x3, Pallas kernels: 145 us -> 228 us  [line_gather(): pl.pallas_call(functools.partial(gather_kernel, count, arrays), in_specs=...]
    concatenate x0 -> x10, other arithmetic: none -> 58 us  [the longest x1 18.4 us: per_device(): jnp.concatenate([jnp.concatenate(raw_grads, 0), jnp.concatenate(pair_grad...]
  transfers between devices with their start and end apart: 27 -> 20, of which waited for: 17 -> 10; matrix products, arithmetic and copies ran while one was open for 14% -> 14% of each run, Pallas kernels for 19% -> 42%
where the time goes in v3:
time: 1750 us; the launch traced here: 1740 us
  Pallas kernels  959 us (55%)
  waiting for transfers between devices  393 us (22%)
  matrix products  129 us (7%)
  other arithmetic  116 us (7%)
  local copies, waits for them, and re-layouts  84.7 us (5%)
  starting transfers between devices  40.5 us (2%)
    pallas_call x2, Pallas kernels, attend_back(): pl.pallas_call(functools.partial(attend_back_kernel, per, steps, width **...  238 us
    pallas_call x3, Pallas kernels, line_gather(): pl.pallas_call(functools.partial(gather_kernel, count, arrays), in_specs=...  228 us
    pallas_call x1, Pallas kernels, grad_sums(): pl.pallas_call(functools.partial(grad_sums_kernel, ring, sizes), in_specs...  192 us
    all_gather x2, waiting for transfers between devices, per_device(): lax.all_gather(feed, 'ctx', axis=0, tiled=True)  160 us
    all_to_all x5, waiting for transfers between devices, exchange(): return lax.all_to_all(rows, 'exp', split_axis=0, concat_axis=0, tiled=True)  151 us
    pallas_call x2, Pallas kernels, run_expert(): pl.pallas_call(expert_kernel, grid=(sources,), in_specs=[pl.BlockSpec((No...  115 us
    pallas_call x1, Pallas kernels, expert_weight_grads(): pl.pallas_call(functools.partial(weight_kernel, sources, micro), grid=(mi...  92.7 us
    reduce_scatter x4, waiting for transfers between devices, scatter(): lax.psum_scatter(part, 'ctx', scatter_dimension=0, tiled=True)  73.6 us
  transfers between devices with their start and end apart: 20, of which 10 were waited for; matrix products, arithmetic and copies ran while one was open for 14% of the time, Pallas kernels for 42%

profile of v3, /device:TPU:0, one launch (start us, length us, event | category | flops | bytes accessed | tf_op | source)
XLA Modules:
  0.0 1737.6 jit_solution(3184232470958635583)
XLA Ops:
  17.5 145.2 %shard_map.239 = (bf16[1024,2048]{1,0:T(8,128)(2,1)}, bf16[1024,2048]{1,0:T(8,128)(2,1)}, f32[256,128]{1,0:T(8,128)}) custom-call(bf16[256,2048]{1,0:T(8,128)(2,1)} %get-tuple-element.164.refs_0_, bf16[256,2048]{1,0:T(8,128)(2,1)} %get-tuple-element.163.refs_1_, f32[64,128]{1,0:T(8,128)} %reshape.333.refs_2_), custom_call_target="tpu_custom_call" | custom-call | bytes 209715200 | tf_op jit(solution)/shard_map/pallas_call | solution.py:127
  168.8 8.6 pad_maximum_fusion.1.rows_ref
  177.5 22.3 %shard_map.240.refs_1_ = bf16[8,8,80,2048]{3,2,1,0:T(8,128)(2,1)} custom-call(s32[8,2,4,256]{3,2,1,0:T(4,128)} %reshape.335.place_ref, f32[8,2,4,256]{3,2,1,0:T(4,128)} %reshape.336.weight_ref, bf16[2048,2048]{1,0:T(8,128)(2,1)} %pad_maximum_fusion.1.rows_ref), custom_call_target="tpu_custom_call" | custom-call | flops 1048576 | bytes 1048576 | tf_op jit(solution)/shard_map/pallas_call | solution.py:243
  199.8 6.2 all-to-all-start
  215.5 15.0 fusion.79.raw_ref
  230.4 3.9 copy-done
  247.4 41.7 %shard_map.242 = bf16[1024,1024]{1,0:T(8,128)(2,1)} custom-call(bf16[256,1024]{1,0:T(8,128)(2,1)} %slice.155.refs_0_), custom_call_target="tpu_custom_call" | custom-call | bytes 209715200 | tf_op jit(solution)/shard_map/pallas_call | solution.py:127
  289.2 24.0 %shard_map.243 = bf16[256,4096]{1,0:T(8,128)(2,1)} custom-call(s32[2]{0:T(128)} %get-tuple-element.212.place_ref, f32[512,5120]{1,0:T(8,128)} %copy-done, bf16[4,256,1024]{2,1,0:T(8,128)(2,1)} %bitcast.246, f32[1,128]{1,0:T(1,128)} %bitcast.294, f32[256,128]{1,0:T(8,128)} %copy-done.21, f32[256,128]{1,0:T(8,128)} %copy-done.23), custom_call_target="tpu_custom_call" | custom-call | flops 1048576 | bytes 1048576 | tf_op jit(solution)/shard_map/pallas_call | solution.py:585
  313.3 11.6 multiply_reduce_fusion.1
  328.6 79.7 %all-gather.9.cloned.1.call-done.rows_ref = bf16[1024,2048]{1,0:T(8,128)(2,1)} async-done(((bf16[256,2048]{1,0:T(8,128)(2,1)}), bf16[1024,2048]{1,0:T(8,128)(2,1)}) %all-gather.9.cloned.1.call-update) | async-done | bytes 4194320 | tf_op jit(solution)/shard_map/all_gather | solution.py:1002
  408.3 11.9 shard_map.244
  420.2 19.6 %all-to-all-done = bf16[8,640,2048]{2,1,0:T(8,128)(2,1)} async-done(((bf16[8,640,2048]{2,1,0:T(8,128)(2,1)}), bf16[8,640,2048]{2,1,0:T(8,128)(2,1)}, u32[]{:S(2)}, u32[]{:S(2)}) %all-to-all-start) | async-done | bytes 20971552 | tf_op jit(solution)/shard_map/all_to_all | solution.py:941
  439.8 5.2 all-to-all-start.1
  447.0 41.1 %shard_map.248 = bf16[1024,1024]{1,0:T(8,128)(2,1)} custom-call(bf16[256,1024]{1,0:T(8,128)(2,1)} %shard_map.247.refs_0_), custom_call_target="tpu_custom_call" | custom-call | bytes 209715200 | tf_op jit(solution)/shard_map/pallas_call | solution.py:127
  488.1 23.8 %shard_map.249 = bf16[256,4096]{1,0:T(8,128)(2,1)} custom-call(s32[2]{0:T(128)} %get-tuple-element.213.place_ref, f32[512,5120]{1,0:T(8,128)} %copy-done, bf16[4,256,1024]{2,1,0:T(8,128)(2,1)} %bitcast.248, f32[1,128]{1,0:T(1,128)} %bitcast.295, f32[256,128]{1,0:T(8,128)} %copy-done.21, f32[256,128]{1,0:T(8,128)} %copy-done.23), custom_call_target="tpu_custom_call" | custom-call | flops 1048576 | bytes 1048576 | tf_op jit(solution)/shard_map/pallas_call | solution.py:585
  511.9 8.8 multiply_reduce_fusion
  524.6 80.0 %all-gather.11.cloned.1.call-done.rows_ref = bf16[1024,2048]{1,0:T(8,128)(2,1)} async-done(((bf16[256,2048]{1,0:T(8,128)(2,1)}), bf16[1024,2048]{1,0:T(8,128)(2,1)}) %all-gather.11.cloned.1.call-update) | async-done | bytes 4194320 | tf_op jit(solution)/shard_map/all_gather | solution.py:1002
  604.6 11.9 shard_map.250
  616.6 5.3 all-to-all-start.2
  621.9 57.5 %shard_map.246 = (bf16[2560,768]{1,0:T(8,128)(2,1)}, bf16[2560,768]{1,0:T(8,128)(2,1)}, bf16[2560,768]{1,0:T(8,128)(2,1)}, bf16[2560,2048]{1,0:T(8,128)(2,1)}, b...) custom-call(bf16[8,320,2048]{2,1,0:T(8,128)(2,1)} %all-to-all-done.1.rows_ref.refs_1_.refs_0_, ...), custom_call_target="tpu_custom_call" | custom-call | flops 1048576 | bytes 1048576 | tf_op jit(solution)/shard_map/pallas_call | solution.py:188
  679.4 59.0 %all-to-all-done.2.refs_1_.rows_ref = bf16[8,320,2048]{2,1,0:T(8,128)(2,1)} async-done(((bf16[8,320,2048]{2,1,0:T(8,128)(2,1)}), bf16[8,320,2048]{2,1,0:T(8,128)(2,1)}, u32[]{:S(2)}, u32[]{:S(2)}) %all-to-all-start.2) | async-done | bytes 10485792 | tf_op jit(solution)/shard_map/all_to_all | solution.py:941
  738.4 5.2 all-to-all-start.3
  743.6 57.6 %shard_map.253 = (bf16[2560,768]{1,0:T(8,128)(2,1)}, bf16[2560,768]{1,0:T(8,128)(2,1)}, bf16[2560,768]{1,0:T(8,128)(2,1)}, bf16[2560,2048]{1,0:T(8,128)(2,1)}, b...) custom-call(bf16[8,320,2048]{2,1,0:T(8,128)(2,1)} %all-to-all-done.2.refs_1_.rows_ref, ...), custom_call_target="tpu_custom_call" | custom-call | flops 1048576 | bytes 1048576 | tf_op jit(solution)/shard_map/pallas_call | solution.py:188
  801.2 58.9 %all-to-all-done.3.refs_1_ = bf16[8,320,2048]{2,1,0:T(8,128)(2,1)} async-done(((bf16[8,320,2048]{2,1,0:T(8,128)(2,1)}), bf16[8,320,2048]{2,1,0:T(8,128)(2,1)}, u32[]{:S(2)}, u32[]{:S(2)}) %all-to-all-start.3) | async-done | bytes 10485792 | tf_op jit(solution)/shard_map/all_to_all | solution.py:941
  860.1 5.3 all-to-all-start.4
  865.5 9.5 bitcast_convert_fusion.3
  875.8 92.7 %shard_map.255 = (f32[1,2048,768]{2,1,0:T(8,128)}, f32[1,2048,768]{2,1,0:T(8,128)}, f32[1,768,2048]{2,1,0:T(8,128)}) custom-call(bf16[8,320,2048]{2,1,0:T(8,128)(2,1)} %all-to-all-done.1.rows_ref.refs_1_.refs_0_, bf16[8,320,2048]{2,1,0:T(8,128)(2,1)} %all-to-all-done.2.refs_1_.rows_ref, bf16[8,2,320,2048]{3,2,1,0:T(8,128)(2,1)} %bitcast.29.refs_1_.grad_ref.refs_2_, ...), custom_call_target="tpu_custom_call" | custom-call | flops 1048576 | bytes 1048576 | tf_op jit(solution)/shard_map/pallas_call | solution.py:309
  968.4 13.5 all-to-all-done.4.refs_0_
  982.0 9.4 bitcast_convert_fusion.2
  991.5 73.5 %reduce-scatter.9.cloned.1.call-done = bf16[256,2048]{1,0:T(8,128)(2,1)} async-done(((bf16[1024,2048]{1,0:T(8,128)(2,1)}), bf16[256,2048]{1,0:T(8,128)(2,1)}) %reduce-scatter.9.cloned.1.call-update) | async-done | bytes 1048592 | tf_op jit(solution)/shard_map/reduce_scatter | solution.py:961
  1065.1 4.2 fusion.35
  1072.5 18.0 %convolution_convert_fusion.1.grad_ref = bf16[256,4096]{1,0:T(8,128)(2,1)} fusion(bf16[256,2048]{1,0:T(8,128)(2,1)S(1)} %get-tuple-element.151, bf16[4096,2048]{1,0:T(8,128)(2,1)} %all-gather.7.cloned.1.call-done), kind=kOutput, calls=%fused_computation.16 | convolution fusion | flops 4296015872 | bytes 19922944 | tf_op jit(solution)/shard_map/te,de->td/dot_general | solution.py:909
  1090.5 118.2 %shard_map.258 = (bf16[256,4096]{1,0:T(8,128)(2,1)}, bf16[4,4,256,256]{3,2,1,0:T(8,128)(2,1)}, f32[8,128]{1,0:T(8,128)}, bf16[8,320,2048]{2,1,0:T(8,128)(2,1)}) custom-call(s32[2]{0:T(128)} %get-tuple-element.212.place_ref, f32[512,5120]{1,0:T(8,128)} %copy-done, bf16[256,4096]{1,0:T(8,128)(2,1)} %convolution_convert_fusion.1.grad_ref, ...), custom_call_target="tpu_custom_call" | custom-call | flops 1048576 | bytes 1048576 | tf_op jit(solution)/shard_map/pallas_call | solution.py:607
  1209.9 18.0 %convolution_convert_fusion.grad_ref = bf16[256,4096]{1,0:T(8,128)(2,1)} fusion(bf16[256,2048]{1,0:T(8,128)(2,1)S(1)} %copy-done.11, bf16[4096,2048]{1,0:T(8,128)(2,1)} %all-gather.7.cloned.1.call-done), kind=kOutput, calls=%fused_computation.15 | convolution fusion | flops 4296015872 | bytes 19922944 | tf_op jit(solution)/shard_map/te,de->td/dot_general | solution.py:909
  1227.9 119.3 %shard_map.260 = (bf16[256,4096]{1,0:T(8,128)(2,1)}, bf16[4,4,256,256]{3,2,1,0:T(8,128)(2,1)}, f32[8,128]{1,0:T(8,128)}, bf16[8,320,2048]{2,1,0:T(8,128)(2,1)}) custom-call(s32[2]{0:T(128)} %get-tuple-element.213.place_ref, f32[512,5120]{1,0:T(8,128)} %copy-done, bf16[256,4096]{1,0:T(8,128)(2,1)} %convolution_convert_fusion.grad_ref, ...), custom_call_target="tpu_custom_call" | custom-call | flops 1048576 | bytes 1048576 | tf_op jit(solution)/shard_map/pallas_call | solution.py:607
  1347.3 9.5 bitcast_convert_fusion
  1368.7 4.7 pad_maximum_fusion.2
  1373.5 7.7 reshape.364
  1381.2 5.8 copy.191
  1387.0 7.2 reshape.365
  1394.2 4.5 dynamic-slice_bitcast_fusion.1
  1426.5 4.5 pad_maximum_fusion.3.refs_0_
  1443.1 9.4 bitcast_convert_fusion.1
  1457.0 18.4 %maximum_maximum_fusion = bf16[512,5120]{1,0:T(8,128)(2,1)} fusion(bf16[256,1024]{1,0:T(8,128)(2,1)S(1)} %bitcast.262, bf16[256,1024]{1,0:T(8,128)(2,1)S(1)} %bitcast.265, bf16[256,4096]{1,0:T(8,128)(2,1)S(1)} %copy-done.15, bf16[256,4096]{1,0:T(8,128)(2,1)S(1)} %copy-done.13), kind=kLoop, calls=%fused_computation.14 | loop fusion | flops 20971520 | bytes 10485760 | tf_op jit(solution)/shard_map/concatenate | solution.py:1070
  1478.1 17.8 %fusion.23 = (f32[2048]{0:T(1024)S(1)}, f32[512]{0:T(512)S(1)}, f32[512,2048]{1,0:T(8,128)}) fusion(bf16[2,1,256,2048]{3,2,1,0:T(8,128)(2,1)S(1)} %copy-done.2, f32[512]{0:T(512)S(1)} %bitcast.292, f32[2048]{0:T(1024)S(1)} %copy-done.58, bf16[2048,5120]{1,0:T(8,128)(2,1)} %all-gather.5.cloned.1.call-done, bf16[256,1024]{1,0:T(8,128)(2,1)S(1)} %bitcast.263, ...), kind=kOutput, calls=%fused_computation.33 | convolution fusion | flops 10765727744 | bytes 32526336 | tf_op jit(solution)/shard_map/te,de->td/dot_general | solution.py:909
  1500.1 6.6 maximum_add_fusion
  1513.3 13.2 pad_maximum_fusion.refs_3_
  1526.6 191.8 %shard_map.261 = (f32[128,2048]{1,0:T(8,128)}, f32[64,5120]{1,0:T(8,128)}) custom-call(bf16[4,1024,512]{2,1,0:T(8,128)(2,1)} %pad_maximum_fusion.3.refs_0_, bf16[4,1024,256]{2,1,0:T(8,128)(2,1)} %pad_maximum_fusion.6.refs_1_, bf16[1024,2048]{1,0:T(8,128)(2,1)} %pad_maximum_fusion.4.refs_2_, bf16[1024,5120]{1,0:T(8,128)(2,1)} %pad_maximum_fusion.refs_3_), custom_call_target="tpu_custom_call" | custom-call | flops 1048576 | bytes 1048576 | tf_op jit(solution)/shard_map/pallas_call | solution.py:853
  (325 shorter events, 134.6 us)
Async XLA Ops:
  7.2 208.3 %all-gather.5.cloned.1.call-start = ((), (), s32[]{:S(2)}) async-start(), calls=%async_computation.12 | async-start | bytes 23592960 | tf_op jit(solution)/shard_map/all_gather | solution.py:920
  10.9 5.2 copy-start.17
  14.3 298.9 %all-gather.7.cloned.1.call-start = ((), (), s32[]{:S(2)}) async-start(), calls=%async_computation.13 | async-start | bytes 18874368 | tf_op jit(solution)/shard_map/all_gather | solution.py:923
  165.6 11.9 copy-start.49
  166.4 11.1 copy-start.51
  199.8 6.3 copy-start.1
  199.8 240.0 %all-to-all-start = ((bf16[8,640,2048]{2,1,0:T(8,128)(2,1)}), bf16[8,640,2048]{2,1,0:T(8,128)(2,1)}, u32[]{:S(2)}, u32[]{:S(2)}) async-start(bf16[8,640,2048]{2,1,0:T(8,128)(2,1)} %bitcast.239), calls=%async_computation | async-start | bytes 41943040 | tf_op jit(solution)/shard_map/all_to_all | solution.py:941
  206.0 202.3 %all-gather.9.cloned.1.call-start = ((), (), s32[]{:S(2)}) async-start(), calls=%async_computation.14 | async-start | bytes 5242880 | tf_op jit(solution)/shard_map/all_gather | solution.py:1002
  215.4 27.8 %copy-start.23 = (f32[256,128]{1,0:T(8,128)}, f32[256,128]{1,0:T(8,128)S(1)}, u32[]{:S(2)}) copy-start(f32[256,128]{1,0:T(8,128)S(1)} %get-tuple-element.215.sin_ref) | copy-start | bytes 393220
  215.4 27.8 %copy-start.21 = (f32[256,128]{1,0:T(8,128)}, f32[256,128]{1,0:T(8,128)S(1)}, u32[]{:S(2)}) copy-start(f32[256,128]{1,0:T(8,128)S(1)} %get-tuple-element.214.cos_ref) | copy-start | bytes 393220
  313.2 12.9 copy-start.45
  325.4 94.8 %copy-start.69 = (f32[256]{0:T(256)}, f32[256]{0:T(256)S(1)}, u32[]{:S(2)}) copy-start(f32[256]{0:T(256)S(1)} %get-tuple-element.196) | copy-start | bytes 3076
  439.8 176.8 %all-to-all-start.1 = ((bf16[8,320,2048]{2,1,0:T(8,128)(2,1)}), bf16[8,320,2048]{2,1,0:T(8,128)(2,1)}, u32[]{:S(2)}, u32[]{:S(2)}) async-start(bf16[8,320,2048]{2,1,0:T(8,128)(2,1)} %shard_map.245), calls=%async_computation.1 | async-start | bytes 20971520 | tf_op jit(solution)/shard_map/all_to_all | solution.py:941
  445.0 159.7 %all-gather.11.cloned.1.call-start = ((), (), s32[]{:S(2)}) async-start(), calls=%async_computation.15 | async-start | bytes 5242880 | tf_op jit(solution)/shard_map/all_gather | solution.py:1002
  488.1 23.9 %copy-start.32 = (f32[2,1,256,2048]{3,2,1,0:T(8,128)S(1)}, f32[2,1,256,2048]{3,2,1,0:T(8,128)}, u32[]{:S(2)}) copy-start(f32[2,1,256,2048]{3,2,1,0:T(8,128)} %convert_element_type.148) | copy-start | bytes 12582916
  616.6 121.8 %all-to-all-start.2 = ((bf16[8,320,2048]{2,1,0:T(8,128)(2,1)}), bf16[8,320,2048]{2,1,0:T(8,128)(2,1)}, u32[]{:S(2)}, u32[]{:S(2)}) async-start(bf16[8,320,2048]{2,1,0:T(8,128)(2,1)} %shard_map.251), calls=%async_computation.2 | async-start | bytes 20971520 | tf_op jit(solution)/shard_map/all_to_all | solution.py:941
  738.4 121.7 %all-to-all-start.3 = ((bf16[8,320,2048]{2,1,0:T(8,128)(2,1)}), bf16[8,320,2048]{2,1,0:T(8,128)(2,1)}, u32[]{:S(2)}, u32[]{:S(2)}) async-start(bf16[8,320,2048]{2,1,0:T(8,128)(2,1)} %shard_map.252), calls=%async_computation.3 | async-start | bytes 20971520 | tf_op jit(solution)/shard_map/all_to_all | solution.py:941
  860.1 5.4 copy-start.66
  860.1 5.4 copy-start.68
  860.1 121.8 %all-to-all-start.4 = ((bf16[8,320,2048]{2,1,0:T(8,128)(2,1)}), bf16[8,320,2048]{2,1,0:T(8,128)(2,1)}, u32[]{:S(2)}, u32[]{:S(2)}) async-start(bf16[8,320,2048]{2,1,0:T(8,128)(2,1)} %shard_map.254), calls=%async_computation.5 | async-start | bytes 20971520 | tf_op jit(solution)/shard_map/all_to_all | solution.py:941
  865.4 126.1 %reduce-scatter.5.cloned.1.call-start = ((), (), s32[]{:S(2)}) async-start(), calls=%async_computation.16 | async-start | bytes 5242880 | tf_op jit(solution)/shard_map/reduce_scatter | solution.py:961
  865.5 9.5 copy-start.46
  875.0 190.1 %reduce-scatter.9.cloned.1.call-start = ((), (), s32[]{:S(2)}) async-start(), calls=%async_computation.18 | async-start | bytes 5242880 | tf_op jit(solution)/shard_map/reduce_scatter | solution.py:961
  875.8 471.5 %copy-start.48 = (s32[8,4,256]{2,0,1:T(8,128)}, s32[8,4,256]{2,0,1:T(8,128)S(1)}, u32[]{:S(2)}) copy-start(s32[8,4,256]{2,0,1:T(8,128)S(1)} %bitcast_select_fusion) | copy-start | bytes 98308
  991.4 732.7 %reduce-scatter.11.cloned.1.call-start = ((), (), s32[]{:S(2)}) async-start(), calls=%async_computation.19 | async-start | bytes 5242880 | tf_op jit(solution)/shard_map/reduce_scatter | solution.py:961
  991.5 73.6 %copy-start.4 = (f32[256,2048]{1,0:T(8,128)S(1)}, f32[256,2048]{1,0:T(8,128)}, u32[]{:S(2)}) copy-start(f32[256,2048]{1,0:T(8,128)} %copy-done.3) | copy-start | bytes 6291460
  991.5 73.6 %copy-start.70 = (f32[256]{0:T(256)S(1)}, f32[256]{0:T(256)}, u32[]{:S(2)}) copy-start(f32[256]{0:T(256)} %copy-done.69) | copy-start | bytes 3076
  991.5 77.8 %copy-start.74 = (f32[256]{0:T(256)S(1)}, f32[256]{0:T(256)}, u32[]{:S(2)}) copy-start(f32[256]{0:T(256)} %get-tuple-element.195) | copy-start | bytes 3076
  1227.9 119.4 %copy-start.44 = (f32[4,256,8]{1,2,0:T(8,128)S(1)}, f32[4,256,8]{1,2,0:T(8,128)}, u32[]{:S(2)}) copy-start(f32[4,256,8]{1,2,0:T(8,128)} %copy-done.42) | copy-start | bytes 98308
  1366.5 35.3 %collective-permute-start.1 = (bf16[4,512,256]{2,1,0:T(8,128)(2,1)}, bf16[4,512,256]{2,1,0:T(8,128)(2,1)}, u32[]{:S(2)}, u32[]{:S(2)}) collective-permute-start(bf16[4,512,256]{2,1,0:T(8,128)(2,1)} %bitcast.101), channel_id=1, source_target_pairs={{0,1},{1,0},{2,3},{3,2},{4,5},{5,4},{6,7},{7,6},{8,9},{9,8},{10,11... | collective-permute-start | bytes 3145736 | tf_op jit(solution)/shard_map/ppermute | solution.py:1077
  1394.2 6.9 copy-start.61
  1398.7 6.0 copy-start.20
  1398.7 6.7 copy-start.10
  1398.7 27.8 %collective-permute-start = (bf16[4,512,512]{2,1,0:T(8,128)(2,1)}, bf16[4,512,512]{2,1,0:T(8,128)(2,1)}, u32[]{:S(2)}, u32[]{:S(2)}) collective-permute-start(bf16[4,512,512]{2,1,0:T(8,128)(2,1)} %get-tuple-element.156), channel_id=1, source_target_pairs={{0,1},{1,0},{2,3},{3,2},{4,5},{5,4},{6,7},{7,6},{8,9},{9,8},{10,11... | collective-permute-start | bytes 6291464 | tf_op jit(solution)/shard_map/ppermute | solution.py:1077
  1411.4 8.5 all-to-all-start.5
  1423.2 11.4 all-to-all-start.6
  1426.5 299.8 %reduce-scatter.7.cloned.1.call-start = ((), (), s32[]{:S(2)}) async-start(), calls=%async_computation.17 | async-start | bytes 5242880 | tf_op jit(solution)/shard_map/reduce_scatter | solution.py:961
  1426.5 8.0 copy-start.56
  1456.0 22.1 %copy-start.25 = (bf16[4,32,8,256]{3,2,0,1:T(8,128)(2,1)}, bf16[4,32,8,256]{3,2,0,1:T(8,128)(2,1)S(1)}, u32[]{:S(2)}) copy-start(bf16[4,32,8,256]{3,2,0,1:T(8,128)(2,1)S(1)} %copy.210) | copy-start | bytes 1572868
  1457.0 18.6 %copy-start.54 = (f32[2,1,256,8]{2,3,1,0:T(8,128)S(1)}, f32[2,1,256,8]{2,3,1,0:T(8,128)}, u32[]{:S(2)}) copy-start(f32[2,1,256,8]{2,3,1,0:T(8,128)} %param.18) | copy-start | bytes 49156
  1457.0 19.2 %copy-start.12 = (bf16[256,2048]{1,0:T(8,128)(2,1)S(1)}, bf16[256,2048]{1,0:T(8,128)(2,1)}, u32[]{:S(2)}) copy-start(bf16[256,2048]{1,0:T(8,128)(2,1)} %get-tuple-element.157) | copy-start | bytes 3145732
  1475.4 36.9 %collective-permute-start.3 = (bf16[512,5120]{1,0:T(8,128)(2,1)}, bf16[512,5120]{1,0:T(8,128)(2,1)}, u32[]{:S(2)}, u32[]{:S(2)}) collective-permute-start(bf16[512,5120]{1,0:T(8,128)(2,1)} %maximum_maximum_fusion), channel_id=1, source_target_pairs={{0,1},{1,0},{2,3},{3,2},{4,5},{5,4},{6,7},{7,6},{8,9},{9,8},{10,11... | collective-permute-start | bytes 15728648 | tf_op jit(solution)/shard_map/ppermute | solution.py:1077
  1477.7 18.2 %copy-start.59 = (f32[2048]{0:T(1024)S(1)}, f32[2048]{0:T(1024)}, u32[]{:S(2)}) copy-start(f32[2048]{0:T(1024)} %get-tuple-element.191) | copy-start | bytes 24580
  1477.7 22.4 %copy-start.71 = (f32[512]{0:T(512)S(1)}, f32[512]{0:T(512)}, u32[]{:S(2)}) copy-start(f32[512]{0:T(512)} %multiply_multiply_fusion.2) | copy-start | bytes 6148
  1477.7 30.7 %collective-permute-start.2 = (bf16[512,2048]{1,0:T(8,128)(2,1)}, bf16[512,2048]{1,0:T(8,128)(2,1)}, u32[]{:S(2)}, u32[]{:S(2)}) collective-permute-start(bf16[512,2048]{1,0:T(8,128)(2,1)} %pad_maximum_fusion.7), channel_id=1, source_target_pairs={{0,1},{1,0},{2,3},{3,2},{4,5},{5,4},{6,7},{7,6},{8,9},{9,8},{10,11... | collective-permute-start | bytes 6291464 | tf_op jit(solution)/shard_map/ppermute | solution.py:1077
  1497.3 10.5 all-to-all-start.7
  1508.4 4.9 copy-start.28
  1718.4 7.9 copy-start.5
  (48 other events, 133.4 us)
Sparse Core Ops, SparseCore 0:
  14.5 110.2 all-gather.4
  126.7 94.7 all-gather.6
  327.5 80.7 all-gather.8
  523.5 81.1 all-gather.10
  875.1 75.6 reduce-scatter.4
  991.5 73.5 reduce-scatter.8
  1356.9 77.9 reduce-scatter.10
  1452.6 74.9 reduce-scatter.6

commit v4 on v3

--- a/solution.py
+++ b/solution.py
@@ -55,9 +55,11 @@
     )(value, *others)
 
 
-def gather_kernel(count, arrays, *refs):
-    own, full = refs[:arrays], refs[arrays : 2 * arrays]
-    send_sem, recv_sem, own_sem = refs[2 * arrays :]
+def gather_kernel(count, arrays, stacked, *refs):
+    own = refs[:arrays]
+    full = [refs[arrays].at[i] for i in range(stacked)]
+    full += refs[arrays + min(stacked, 1) : -3]
+    send_sem, recv_sem, own_sem = refs[-3:]
     me = lax.axis_index("ctx")
     barrier = pltpu.get_barrier_semaphore()
     for other in (lax.rem(me + 1, count), lax.rem(me + count - 1, count)):
@@ -121,17 +123,19 @@
                     passing(way, step, i, me - sign * step).wait_send()
 
 
-def line_gather(*blocks, number):
+def line_gather(*blocks, number, stacked=0):
     count = lax.axis_size("ctx")
     arrays = len(blocks)
+    shapes = [(count * block.shape[0],) + block.shape[1:] for block in blocks]
+    types = [block.dtype for block in blocks]
+    if stacked:
+        shapes = [(stacked,) + shapes[0]] + shapes[stacked:]
+        types = types[:1] + types[stacked:]
     return pl.pallas_call(
-        functools.partial(gather_kernel, count, arrays),
+        functools.partial(gather_kernel, count, arrays, stacked),
         in_specs=[pl.BlockSpec(memory_space=pl.ANY)] * arrays,
-        out_specs=[pl.BlockSpec(memory_space=pl.ANY)] * arrays,
-        out_shape=[
-            jax.ShapeDtypeStruct((count * block.shape[0],) + block.shape[1:], block.dtype)
-            for block in blocks
-        ],
+        out_specs=[pl.BlockSpec(memory_space=pl.ANY)] * len(shapes),
+        out_shape=[jax.ShapeDtypeStruct(*pair) for pair in zip(shapes, types)],
         scratch_shapes=[
             pltpu.SemaphoreType.DMA((2, count - 1, arrays)),
             pltpu.SemaphoreType.DMA((2, count - 1, arrays)),
@@ -221,6 +225,21 @@
     capacity = out_ref.shape[2]
     local = rows_ref.shape[0]
     slots = lax.broadcasted_iota(jnp.int32, (capacity, local), 0)
+    if capacity % 16 == 0:
+        chosen = [place_ref[0, 0, j : j + 1, :] == slots for j in range(planes)]
+        picked = jnp.dot(
+            jnp.concatenate([jnp.where(c, 1.0, 0.0).astype(jnp.bfloat16) for c in chosen], 0),
+            rows_ref[...],
+            preferred_element_type=jnp.float32,
+        )
+        for j in range(planes):
+            rows = picked[j * capacity : (j + 1) * capacity]
+            if weighted:
+                rows = rows * jnp.sum(
+                    jnp.where(chosen[j], weight_ref[0, 0, j : j + 1, :], 0.0), -1, keepdims=True
+                )
+            out_ref[j, 0] = rows.astype(jnp.bfloat16)
+        return
     for j in range(planes):
         chosen = place_ref[0, 0, j : j + 1, :] == slots
         picked = jnp.dot(
@@ -258,23 +277,28 @@
 def weight_kernel(steps, micro, *refs):
     rows, (grads_ref,) = refs[:micro], refs[micro : micro + 1]
     actives, gates, ups = (refs[micro * i + 1 : micro * i + 1 + micro] for i in (1, 2, 3))
-    gate_ref, up_ref, down_ref = refs[4 * micro + 1 :]
+    outs = refs[4 * micro + 1 : 4 * micro + 4]
+    sums, sem = refs[4 * micro + 4 : 4 * micro + 7], refs[-1]
     step = pl.program_id(0)
 
+    def flat(ref):
+        count, block, width = ref.shape
+        return ref[...].reshape(count * block, width)
+
     def add(which, fresh):
-        x = rows[which][...]
-        for out_ref, left, right in (
-            (gate_ref, x, gates[which][...]),
-            (up_ref, x, ups[which][...]),
-            (down_ref, actives[which][...], grads_ref[...]),
+        x = flat(rows[which])
+        for sum_ref, left, right in (
+            (sums[0], x, gates[which][...]),
+            (sums[1], x, ups[which][...]),
+            (sums[2], actives[which][...], flat(grads_ref)),
         ):
             term = lax.dot_general(
                 left, right, (((0,), (0,)), ((), ())), preferred_element_type=jnp.float32
             )
             if fresh:
-                out_ref[0] = term
+                sum_ref[0] = term
             else:
-                out_ref[0] += term
+                sum_ref[0] += term
 
     pl.when(step == 0)(lambda: add(0, True))
     pl.when((step > 0) & (step < steps))(lambda: add(0, False))
@@ -283,42 +307,52 @@
             functools.partial(add, which, False)
         )
 
+    @pl.when(step == micro * steps - 1)
+    def _():
+        copies = [pltpu.make_async_copy(sums[i], outs[i], sem.at[i]) for i in range(3)]
+        for copy in copies:
+            copy.start()
+        for copy in copies:
+            copy.wait()
+
 
 def expert_weight_grads(rows, grads, actives, gates, ups):
     sources, micro, block, width = grads.shape
     units = gates[0].shape[1]
+    steps = sources // 2
 
     def turn(i, which):
-        return jnp.clip(i - which * sources, 0, sources - 1)
+        return jnp.clip(i - which * steps, 0, steps - 1)
 
     def specs(size):
         return [
-            pl.BlockSpec((block, size), functools.partial(lambda w, i: (turn(i, w), 0), which))
+            pl.BlockSpec((2 * block, size), functools.partial(lambda w, i: (turn(i, w), 0), which))
             for which in range(micro)
         ]
 
     def row_specs():
         return [
             pl.BlockSpec(
-                (None, block, width), functools.partial(lambda w, i: (turn(i, w), 0, 0), which)
+                (2, block, width), functools.partial(lambda w, i: (turn(i, w), 0, 0), which)
             )
             for which in range(micro)
         ]
 
     shapes = [(1, width, units), (1, width, units), (1, units, width)]
     return pl.pallas_call(
-        functools.partial(weight_kernel, sources, micro),
-        grid=(micro * sources,),
+        functools.partial(weight_kernel, steps, micro),
+        grid=(micro * steps,),
         in_specs=row_specs()
         + [
             pl.BlockSpec(
-                (None, None, block, width),
-                lambda i: (lax.rem(i, sources), lax.div(i, sources), 0, 0),
+                (2, None, block, width), lambda i: (lax.rem(i, steps), lax.div(i, steps), 0, 0)
             )
         ]
         + specs(units) * 3,
-        out_specs=[pl.BlockSpec(shape, lambda i: (0, 0, 0)) for shape in shapes],
+        out_specs=[pl.BlockSpec(memory_space=pl.ANY)] * 3,
         out_shape=[jax.ShapeDtypeStruct(shape, jnp.float32) for shape in shapes],
+        scratch_shapes=[pltpu.VMEM(shape, jnp.float32) for shape in shapes]
+        + [pltpu.SemaphoreType.DMA((3,))],
         compiler_params=pltpu.CompilerParams(vmem_limit_bytes=VMEM_BYTES),
         cost_estimate=SMALL,
     )(*rows, grads, *actives, *gates, *ups)
@@ -354,8 +388,9 @@
 
 
 def attend_kernel(
-    per, factor, place_ref, raw_ref, both_ref, gain_ref, cos_ref, sin_ref, out_ref, mask_ref, turned_ref
+    per, factor, place_ref, raw_ref, both_ref, gain_ref, cos_ref, sin_ref, *rest
 ):
+    out_ref, mask_ref, turned_ref = rest[-3:]
     width = gain_ref.shape[1]
     group_step, step = pl.program_id(0), pl.program_id(1)
 
@@ -376,11 +411,12 @@
         out_ref[:, columns] = result.T.astype(jnp.bfloat16)
 
 
-class PlaneExchange:
-    def __init__(self, count, rows_ref, out_ref, send_sem, recv_sem, own_sem):
-        self.count, self.rows_ref, self.out_ref = count, rows_ref, out_ref
+class Exchange:
+    def __init__(self, axis, rows_ref, out_ref, send_sem, recv_sem, own_sem):
+        self.axis, self.count = axis, rows_ref.shape[0]
+        self.rows_ref, self.out_ref = rows_ref, out_ref
         self.send_sem, self.recv_sem, self.own_sem = send_sem, recv_sem, own_sem
-        self.me = lax.axis_index("exp")
+        self.me = lax.axis_index(axis)
 
     @staticmethod
     def scratch(count):
@@ -396,7 +432,7 @@
             dst_ref=self.out_ref.at[part],
             send_sem=self.send_sem.at[k],
             recv_sem=self.recv_sem.at[k],
-            device_id={"exp": lax.rem(self.me + k, self.count)},
+            device_id={self.axis: lax.rem(self.me + k, self.count)},
             device_id_type=pl.DeviceIdType.MESH,
         )
 
@@ -487,6 +523,7 @@
     scale,
     count,
     ring,
+    extra_axis,
     place_ref,
     raw_ref,
     grad_ref,
@@ -495,10 +532,12 @@
     cos_ref,
     sin_ref,
     rows_ref,
+    extra_ref,
     raw_grad_ref,
     landed_ref,
     gain_grad_ref,
     moved_ref,
+    extra_moved_ref,
     mask_ref,
     turned_ref,
     sums_ref,
@@ -507,13 +546,15 @@
 ):
     width = gain_ref.shape[1]
     group_step, step = pl.program_id(0), pl.program_id(1)
-    moving = PlaneExchange(count, rows_ref, moved_ref, *sems[:3])
-    landing = RowExchange(ring, held_ref, landed_ref, *sems[3:])
+    moving = Exchange("exp", rows_ref, moved_ref, *sems[:3])
+    extra_moving = Exchange(extra_axis, extra_ref, extra_moved_ref, *sems[3:6])
+    landing = RowExchange(ring, held_ref, landed_ref, *sems[6:])
 
     @pl.when((group_step == 0) & (step == 0))
     def _():
         greet(exp=count, ctx=ring)
         moving.begin()
+        extra_moving.begin()
 
     @pl.when((group_step == 0) & (step == 0))
     def _():
@@ -554,6 +595,7 @@
     @pl.when((group_step == pl.num_programs(0) - 1) & (step == steps - 1))
     def _():
         landing.finish()
+        extra_moving.finish()
         moving.finish()
 
 
@@ -577,7 +619,7 @@
     return kv_heads, heads, steps, keys, specs, params, work
 
 
-def attend(raw, both, gain, cosine, sine, place, step, per=2):
+def attend(raw, both, gain, cosine, sine, place, step, waits, per=2):
     rows, width = cosine.shape
     kv_heads, heads, steps, keys, specs, params, work = attention_specs(
         raw, both, width, rows, step, per
@@ -585,7 +627,8 @@
     return pl.pallas_call(
         functools.partial(attend_kernel, per, width ** (-0.5) * math.log2(math.e)),
         grid=(kv_heads, steps),
-        in_specs=[specs[k] for k in ("place", "raw", "both", "gain", "table", "table")],
+        in_specs=[specs[k] for k in ("place", "raw", "both", "gain", "table", "table")]
+        + [pl.BlockSpec(memory_space=pl.ANY)] * len(waits),
         out_specs=specs["heads"],
         out_shape=jax.ShapeDtypeStruct((rows, heads * width), jnp.bfloat16),
         scratch_shapes=[
@@ -594,10 +637,12 @@
         ],
         compiler_params=params,
         cost_estimate=SMALL,
-    )(place, raw, both, gain, cosine, sine)
-
-
-def attend_back(raw, grad, both, gain, cosine, sine, place, step, rows_out, per=2):
+    )(place, raw, both, gain, cosine, sine, *waits)
+
+
+def attend_back(
+    raw, grad, both, gain, cosine, sine, place, step, rows_out, extra, extra_axis, per=2
+):
     rows, width = cosine.shape
     kv_heads, heads, steps, keys, specs, params, work = attention_specs(
         raw, both, width, rows, step, per
@@ -613,14 +658,16 @@
             width ** (-0.5),
             count,
             both.shape[0],
+            extra_axis,
         ),
         grid=(kv_heads, steps),
         in_specs=[specs[k] for k in ("place", "raw", "heads", "both", "gain", "table", "table")]
-        + [anywhere],
+        + [anywhere] * 2,
         out_specs=(
             specs["heads"],
             anywhere,
             pl.BlockSpec((8, width), lambda g, j: (0, 0)),
+            anywhere,
             anywhere,
         ),
         out_shape=(
@@ -628,6 +675,7 @@
             jax.ShapeDtypeStruct((both.shape[0], kv_heads, rows, 2 * width), jnp.bfloat16),
             jax.ShapeDtypeStruct((8, width), jnp.float32),
             jax.ShapeDtypeStruct(rows_out.shape, rows_out.dtype),
+            jax.ShapeDtypeStruct(extra.shape, extra.dtype),
         ),
         scratch_shapes=[
             pltpu.VMEM((keys, rows), jnp.float32),
@@ -635,30 +683,79 @@
             pltpu.VMEM((keys, 2 * width), jnp.float32),
             pltpu.VMEM((kv_heads, keys, 2 * width), jnp.bfloat16),
         ]
-        + PlaneExchange.scratch(count)
+        + Exchange.scratch(count) + Exchange.scratch(extra.shape[0])
         + RowExchange.scratch(both.shape[0], kv_heads),
         compiler_params=pltpu.CompilerParams(
             vmem_limit_bytes=VMEM_BYTES, collective_id=1 + step, has_side_effects=True
         ),
         cost_estimate=SMALL,
-    )(place, raw, grad, both, gain, cosine, sine, rows_out)
+    )(place, raw, grad, both, gain, cosine, sine, rows_out, extra)
+
+
+def combine_kernel(place_ref, weight_ref, back_ref, out_ref, *, weighted):
+    experts, _, capacity, width = back_ref.shape
+    local = out_ref.shape[0]
+    slots = lax.broadcasted_iota(jnp.int32, (capacity, local), 0)
+    factors = []
+    for j in range(experts):
+        value = weight_ref[0, j : j + 1, :] if weighted else 1.0
+        chosen = place_ref[0, j : j + 1, :] == slots
+        factors.append(jnp.where(chosen, value, 0.0).astype(jnp.bfloat16))
+    out_ref[...] = lax.dot_general(
+        jnp.concatenate(factors, 0),
+        back_ref[...].reshape(experts * capacity, width),
+        (((0,), (0,)), ((), ())),
+        preferred_element_type=jnp.float32,
+    ).astype(jnp.bfloat16)
+
+
+def combine_rows(place, weight, back, weighted):
+    count, planned, local = place.shape
+    capacity, width = back.shape[2:]
+    return pl.pallas_call(
+        functools.partial(combine_kernel, weighted=weighted),
+        grid=(count,),
+        in_specs=[
+            pl.BlockSpec((1, planned, local), lambda c: (c, 0, 0)),
+            pl.BlockSpec((1, planned, local), lambda c: (c, 0, 0)),
+            pl.BlockSpec((planned, 1, capacity, width), lambda c: (0, c, 0, 0)),
+        ],
+        out_specs=pl.BlockSpec((local, width), lambda c: (c, 0)),
+        out_shape=jax.ShapeDtypeStruct((count * local, width), jnp.bfloat16),
+        compiler_params=pltpu.CompilerParams(vmem_limit_bytes=VMEM_BYTES),
+        cost_estimate=SMALL,
+    )(place, weight, back)
 
 
 class GradSums:
-    def __init__(self, ring, sizes, refs):
-        self.ring = ring
-        self.sizes = sizes
-        kinds = len(sizes)
-        self.left, self.right = refs[:kinds], refs[kinds : 2 * kinds]
-        self.out = refs[2 * kinds : 3 * kinds]
-        scratch = refs[3 * kinds :]
-        self.left_v, self.right_v = scratch[:kinds], scratch[kinds : 2 * kinds]
+    def __init__(self, ring, micro, sizes, refs):
+        self.ring, self.micro, self.sizes = ring, micro, sizes
+        self.attended, self.hidden = refs[:micro], refs[micro]
+        refs = refs[micro + 1 :]
+        self.branch, self.query, self.pair = (
+            refs[i * micro : (i + 1) * micro] for i in range(3)
+        )
+        self.weight = refs[3 * micro]
+        self.out = refs[3 * micro + 1 : 3 * micro + 3]
+        self.hidden_grad = refs[3 * micro + 3]
+        self.far = refs[3 * micro + 4 : 3 * micro + 7]
+        scratch = refs[3 * micro + 7 :]
+        self.left_v, self.right_v = scratch[:2], scratch[2:4]
         self.part, self.first, self.second, self.last = (
-            scratch[(2 + i) * kinds : (3 + i) * kinds] for i in range(4)
-        )
-        self.load_sem, self.first_sem, self.second_sem, self.last_sem = scratch[6 * kinds :]
+            scratch[4 + 2 * i : 6 + 2 * i] for i in range(4)
+        )
+        (
+            self.left_sem,
+            self.far_sem,
+            self.load_sem,
+            self.first_sem,
+            self.second_sem,
+            self.last_sem,
+            self.weight_sem,
+        ) = scratch[12:]
         e = lax.axis_index("exp")
-        self.y, self.x = lax.div(e, 4), lax.rem(lax.div(e, 2), 2)
+        self.core, self.y, self.x = lax.rem(e, 2), lax.div(e, 4), lax.rem(lax.div(e, 2), 2)
+        self.partner = e + 1 - 2 * self.core
         self.across_x, self.across_y = e + 2 - 4 * self.x, e + 4 - 8 * self.y
         self.z = lax.axis_index("ctx")
         self.order = [
@@ -666,7 +763,7 @@
         ]
 
     @staticmethod
-    def scratch(ring, sizes):
+    def scratch(ring, micro, sizes):
         chunks = [size[2] // size[3] for size in sizes]
         total = sum(chunks)
         shapes = [pltpu.VMEM((4, size[0], size[1]), jnp.bfloat16) for size in sizes]
@@ -677,29 +774,158 @@
                     pltpu.VMEM((count,) + lead + (size[1] // share, size[3]), jnp.bfloat16)
                 )
         shapes += [
-            pltpu.SemaphoreType.DMA((len(sizes) + total,)),
+            pltpu.SemaphoreType.DMA((3, micro + 1, 4, ring)),
+            pltpu.SemaphoreType.DMA((2, 3, micro)),
+            pltpu.SemaphoreType.DMA((total, 2, micro)),
             pltpu.SemaphoreType.DMA((2, total, 2)),
             pltpu.SemaphoreType.DMA((2, total)),
             pltpu.SemaphoreType.DMA((2, total, ring)),
+            pltpu.SemaphoreType.DMA((4,)),
         ]
         return shapes
 
+    def weight_loads(self, chunk):
+        _, high, wide = self.left_v[0].shape
+        return [
+            pltpu.make_async_copy(
+                self.weight.at[pl.ds(r * high, high), pl.ds((2 * chunk + h) * wide, wide)],
+                self.left_v[0].at[2 * r + h],
+                self.weight_sem.at[2 * r + h],
+            )
+            for r in (0, 1)
+            for h in (0, 1)
+        ]
+
+    def add_hidden(self, chunk):
+        _, high, wide = self.left_v[0].shape
+        half = self.sizes[1][0] // 2
+        for copy in self.weight_loads(chunk):
+            copy.wait()
+        for r in (0, 1):
+            columns = slice(r * high, (r + 1) * high)
+            for h in (0, 1):
+                term = across(
+                    self.right_v[1][chunk % 2, :half, h * wide : (h + 1) * wide],
+                    self.left_v[0][2 * r + h],
+                )
+                if chunk == 0 and h == 0:
+                    self.hidden_grad[:, columns] = term
+                else:
+                    self.hidden_grad[:, columns] += term
+
+    def to_partner(self, src, dst, send_sem, recv_sem):
+        return pltpu.make_async_remote_copy(
+            src_ref=src,
+            dst_ref=dst,
+            send_sem=send_sem,
+            recv_sem=recv_sem,
+            device_id={"exp": self.partner},
+            device_id_type=pl.DeviceIdType.MESH,
+        )
+
+    def left_copies(self, kind):
+        half = self.sizes[kind][0] // 2
+        own, sent = [], []
+        if kind == 1:
+            place = (self.micro, 0, 0)
+            own.append(
+                pltpu.make_async_copy(
+                    self.hidden.at[self.core],
+                    self.left_v[1].at[:, pl.ds(0, half)],
+                    self.left_sem.at[(0,) + place],
+                )
+            )
+            sent.append(
+                self.to_partner(
+                    self.hidden.at[1 - self.core],
+                    self.left_v[1].at[:, pl.ds(half, half)],
+                    self.left_sem.at[(1,) + place],
+                    self.left_sem.at[(2,) + place],
+                )
+            )
+            return own, sent
+        share = self.sizes[kind][1] // self.ring
+        rows = half // self.micro
+        for m in range(self.micro):
+            for piece in range(4):
+                for c in range(self.ring):
+
+                    def columns(core):
+                        block = c * 8 + piece * 2 + core
+                        return self.attended[m].at[
+                            :, pl.ds(pl.multiple_of(block * share, share), share)
+                        ]
+
+                    def place(base):
+                        return self.left_v[0].at[
+                            piece, pl.ds(base + m * rows, rows), pl.ds(c * share, share)
+                        ]
+
+                    own.append(
+                        pltpu.make_async_copy(
+                            columns(self.core), place(0), self.left_sem.at[0, m, piece, c]
+                        )
+                    )
+                    sent.append(
+                        self.to_partner(
+                            columns(1 - self.core),
+                            place(half),
+                            self.left_sem.at[1, m, piece, c],
+                            self.left_sem.at[2, m, piece, c],
+                        )
+                    )
+        return own, sent
+
+    def right_copies(self, which):
+        near = (self.branch, self.query, self.pair)[which]
+        return [
+            self.to_partner(
+                near[m],
+                self.far[which].at[m],
+                self.far_sem.at[0, which, m],
+                self.far_sem.at[1, which, m],
+            )
+            for m in range(self.micro)
+        ]
+
+    def source(self, i):
+        kind, chunk = self.order[i]
+        wide = self.sizes[kind][3]
+        if kind == 0:
+            return 0, chunk * wide
+        query_width = self.query[0].shape[1]
+        if chunk * wide < query_width:
+            return 1, chunk * wide
+        return 2, chunk * wide - query_width
+
+    def loads(self, i, far):
+        kind, chunk = self.order[i]
+        which, start = self.source(i)
+        wide = self.sizes[kind][3]
+        half = self.sizes[kind][0] // 2
+        rows = half // self.micro
+        near = (self.branch, self.query, self.pair)[which]
+        return [
+            pltpu.make_async_copy(
+                (self.far[which].at[m] if far else near[m]).at[:, pl.ds(start, wide)],
+                self.right_v[kind].at[chunk % 2, pl.ds(far * half + m * rows, rows)],
+                self.load_sem.at[i, far, m],
+            )
+            for m in range(self.micro)
+        ]
+
+    def start_loads(self, i):
+        which, start = self.source(i)
+        for copy in self.loads(i, 0):
+            copy.start()
+        if start == 0:
+            for copy in self.right_copies(which):
+                copy.wait_recv()
+        for copy in self.loads(i, 1):
+            copy.start()
+
     def x_first(self, i):
         return i % 2 == 0
-
-    def load(self, i):
-        kind, chunk = self.order[i]
-        wide = self.sizes[kind][3]
-        return pltpu.make_async_copy(
-            self.right[kind].at[:, pl.ds(chunk * wide, wide)],
-            self.right_v[kind].at[chunk % 2],
-            self.load_sem.at[len(self.sizes) + i],
-        )
-
-    def load_left(self, kind):
-        return pltpu.make_async_copy(
-            self.left[kind], self.left_v[kind], self.load_sem.at[kind]
-        )
 
     def step_first(self, i, k):
         kind, chunk = self.order[i]
@@ -750,7 +976,9 @@
 
     def multiply(self, i):
         kind, chunk = self.order[i]
-        self.load(i).wait()
+        for far in (0, 1):
+            for copy in self.loads(i, far):
+                copy.wait()
 
         def piece(p, carry):
             term = lax.dot_general(
@@ -803,11 +1031,8 @@
 
     def run(self):
         chunks = len(self.order)
-        for kind in range(len(self.sizes)):
-            self.load_left(kind).start()
-        self.load(0).start()
         barrier = pltpu.get_barrier_semaphore()
-        for other in (self.across_x, self.across_y):
+        for other in (self.partner, self.across_x, self.across_y):
             pl.semaphore_signal(
                 barrier, inc=1, device_id={"exp": other}, device_id_type=pl.DeviceIdType.MESH
             )
@@ -818,20 +1043,41 @@
                 device_id={"ctx": lax.rem(self.z + k, self.ring)},
                 device_id_type=pl.DeviceIdType.MESH,
             )
-        pl.semaphore_wait(barrier, self.ring + 1)
+        pl.semaphore_wait(barrier, self.ring + 2)
+        lefts = [self.left_copies(kind) for kind in (0, 1)]
+        rights = [self.right_copies(which) for which in range(3)]
+        for copies in (rights[0], lefts[0][1], lefts[0][0], rights[1], *lefts[1], rights[2]):
+            for copy in copies:
+                copy.start()
+        self.start_loads(0)
         for i in range(chunks + 6):
             if i < chunks:
                 if i + 1 < chunks:
-                    self.load(i + 1).start()
-                if self.order[i][1] == 0:
-                    self.load_left(self.order[i][0]).wait()
+                    self.start_loads(i + 1)
+                kind, chunk = self.order[i]
+                if chunk == 0:
+                    for copy in lefts[kind][0]:
+                        copy.wait()
+                    for copy in lefts[kind][1]:
+                        copy.wait_recv()
                 self.multiply(i)
+                if kind == 0 and chunk == self.sizes[0][2] // self.sizes[0][3] - 1:
+                    for copy in self.weight_loads(0):
+                        copy.start()
+                if kind == 1:
+                    self.add_hidden(chunk)
+                    if i + 1 < chunks:
+                        for copy in self.weight_loads(chunk + 1):
+                            copy.start()
             if 0 <= i - 2 < chunks:
                 self.add_first(i - 2)
             if 0 <= i - 4 < chunks:
                 self.add_second(i - 4)
             if 0 <= i - 6 < chunks:
                 self.add_last(i - 6)
+        for copies in (lefts[0][1], lefts[1][1], *rights):
+            for copy in copies:
+                copy.wait_send()
         for i in range(chunks):
             for k in range(2):
                 self.step_first(i, k).wait_send()
@@ -840,29 +1086,38 @@
                 self.step_last(i, k, k).wait_send()
 
 
-def grad_sums_kernel(ring, sizes, *refs):
-    GradSums(ring, sizes, refs).run()
-
-
-def grad_sums(ring, lefts, rights, wides, number):
+def grad_sums_kernel(ring, micro, sizes, *refs):
+    GradSums(ring, micro, sizes, refs).run()
+
+
+def grad_sums(ring, attended, hidden, branch, query, pair, weight, number):
+    micro, rows = len(attended), attended[0].shape[0]
+    tokens = 2 * micro * rows
     sizes = [
-        (left.shape[1], left.shape[2], right.shape[1], wide)
-        for left, right, wide in zip(lefts, rights, wides)
+        (tokens, attended[0].shape[1] // 8, branch[0].shape[1], 512),
+        (tokens, hidden.shape[3], query[0].shape[1] + pair[0].shape[1], 1024),
     ]
     anywhere = pl.BlockSpec(memory_space=pl.ANY)
+    assert weight.shape[0] == 2 * tokens and sizes[1][3] == 2 * sizes[0][1]
+    outs = [
+        jax.ShapeDtypeStruct((size[1] // ring, size[2]), jnp.float32) for size in sizes
+    ]
+    outs.append(jax.ShapeDtypeStruct((micro * rows, weight.shape[0]), jnp.float32))
+    outs += [
+        jax.ShapeDtypeStruct((micro,) + arrays[0].shape, jnp.bfloat16)
+        for arrays in (branch, query, pair)
+    ]
     return pl.pallas_call(
-        functools.partial(grad_sums_kernel, ring, sizes),
-        in_specs=[anywhere] * (2 * len(sizes)),
-        out_specs=[pl.BlockSpec(memory_space=pltpu.VMEM)] * len(sizes),
-        out_shape=[
-            jax.ShapeDtypeStruct((size[1] // ring, size[2]), jnp.float32) for size in sizes
-        ],
-        scratch_shapes=GradSums.scratch(ring, sizes),
+        functools.partial(grad_sums_kernel, ring, micro, sizes),
+        in_specs=[anywhere] * (4 * micro + 2),
+        out_specs=[pl.BlockSpec(memory_space=pltpu.VMEM)] * 3 + [anywhere] * 3,
+        out_shape=outs,
+        scratch_shapes=GradSums.scratch(ring, micro, sizes),
         compiler_params=pltpu.CompilerParams(
             vmem_limit_bytes=60 * 2**20, collective_id=number, has_side_effects=True
         ),
         cost_estimate=SMALL,
-    )(*lefts, *rights)
+    )(*attended, hidden, *branch, *query, *pair, weight)[:3]
 
 
 def per_device(
@@ -924,7 +1179,9 @@
 
     meta = jnp.concatenate([routes[:, 0].astype(jnp.float32), route_weights[:, 0]], -1)
     grads_low = [cotangent[step, 0] for step in range(micro)]
-    *grad_blocks, meta = line_gather(*grads_low, meta.reshape(-1, 128), number=0)
+    grad_blocks, meta = line_gather(
+        *grads_low, meta.reshape(-1, 128), number=0, stacked=micro
+    )
     meta = meta.reshape(ring, micro, local, 2 * top)
     tables = [
         plane_tables(
@@ -945,6 +1202,8 @@
 
     def combine(back, step, weighted):
         back = back.reshape(plane, ring, capacity, width)
+        if capacity % 16 == 0:
+            return combine_rows(*tables[step], back, weighted)
         factor = chosen[step]
         if weighted:
             weight = tables[step][1].transpose(1, 0, 2)
@@ -958,12 +1217,12 @@
         return part.astype(jnp.bfloat16).reshape(seq_len, width)
 
     def scatter(part):
-        return lax.psum_scatter(part, "ctx", scatter_dimension=0, tiled=True).astype(jnp.float32)
+        return lax.psum_scatter(part, "ctx", scatter_dimension=0, tiled=True)
 
     picked = pick_rows(
         jnp.concatenate([place for place, _ in tables]),
         jnp.concatenate([weight for _, weight in tables]),
-        jnp.concatenate(grad_blocks),
+        grad_blocks.reshape(micro * seq_len, width),
         capacity,
         True,
     )
@@ -975,6 +1234,10 @@
     hidden, first_scale = norm_rows(rows, norm_attn)
     hidden = after(hidden.astype(jnp.bfloat16), picked)
     raw = dot(hidden, in_weight)
+    hidden_parts = hidden.reshape(-1, ring, plane // 2, 2, width // experts)
+    hidden_parts = hidden_parts.transpose(3, 2, 0, 1, 4).reshape(
+        2, plane // 2, micro * local, ring * width // experts
+    )
     pair_raw = raw[:, query_width:].reshape(micro * local, kv_heads, 2, head_dim)
     key_raw = pair_raw[:, :, 0]
     key_normed, key_scale = norm_rows(key_raw, k_gain)
@@ -985,16 +1248,17 @@
         micro * local, 2 * pair_width
     )
     gain_row = q_gain[None, :]
-    both, places, attended, middles, feeds, scales = [], [], [], [], [], []
+    both = line_gather(
+        *[pairs[step * local : (step + 1) * local] for step in range(micro)], number=3
+    )
+    both = [gathered.reshape(ring, local, 2 * pair_width) for gathered in both]
+    places, attended, middles, feeds, scales = [], [], [], [], []
     for step in range(micro):
         part = slice(step * local, (step + 1) * local)
-        own_pairs = pairs[part]
-        if feeds:
-            own_pairs = after(own_pairs, feeds[-1])
-        (gathered,) = line_gather(own_pairs, number=3 + step)
-        both.append(gathered.reshape(ring, local, 2 * pair_width))
         places.append(jnp.stack([base, bounds[step, 0]]).astype(jnp.int32))
-        attended.append(attend(raw, both[step], gain_row, cosine, sine, places[step], step))
+        attended.append(
+            attend(raw, both[step], gain_row, cosine, sine, places[step], step, feeds[-1:])
+        )
         middles.append(rows[part] + dot(attended[step], out_weight))
         feed_in, second_scale = norm_rows(middles[step], norm_ffn)
         feeds.append(feed_in.astype(jnp.bfloat16))
@@ -1005,10 +1269,12 @@
         return rows.reshape(plane, ring * capacity, width)
 
     received = []
-    last = incoming
+    waits = (incoming,)
+    feed_blocks[0] = after(feed_blocks[0], feeds[-1])
     for step in range(micro):
-        received.append(exchange(after(slotted(pick(feed_blocks[step], step, False)), last)))
-        last = received[-1]
+        picked = slotted(pick(feed_blocks[step], step, False))
+        received.append(exchange(after(picked, *waits)))
+        waits = (received[-1], hidden_parts)
 
     active, gate_grad, up_grad, produced, backs, pair_values = [], [], [], [], [], []
     for step in range(micro):
@@ -1017,25 +1283,38 @@
             held.append(item)
 
     returned = []
+    last = received[-1]
     for step in range(micro):
         returned.append(exchange(after(slotted(backs[step]), last)))
         last = returned[-1]
     gate_term, up_term, down_term = expert_weight_grads(
         received, incoming, active, gate_grad, up_grad
     )
-    returned[-1] = after(returned[-1], down_term)
-    parts = [combine(returned[step], step, False) for step in range(micro)]
+
+    sums = jnp.stack([value.reshape(plane, ring * capacity) for value in pair_values], 1)
+    sums = sums.reshape(plane, -1)
+    spare = -sums.shape[1] % 1024
+    extra = jnp.pad(sums, ((0, 0), (0, spare))).reshape(plane, -1, 128)
 
     branches, raw_grads, middle_grads, gain_list, results = [], [], [], [], []
-    waits = (parts[-1],)
+    waits = ()
     for step in range(micro):
+        if step > 0:
+            feed_grad = after(feed_grad, *waits)
+        else:
+            feed_grad = scatter(combine(after(returned[0], active[-1]), 0, False))
         middle_norm_grad, second_gain = norm_back(
-            middles[step], scales[step], norm_ffn, scatter(parts[step])
+            middles[step], scales[step], norm_ffn, feed_grad.astype(jnp.float32)
         )
         middle_grads.append(grads_low[step].astype(jnp.float32) + middle_norm_grad)
         branches.append(middle_grads[step].astype(jnp.bfloat16))
         attended_grad = dot_t(branches[step], out_weight).astype(jnp.bfloat16)
-        raw_grad, pair_part, query_gain_part, result = attend_back(
+        if step == 0:
+            returned[1] = after(returned[1], down_term, attended_grad)
+            part_sums = combine(returned[1], 1, False)
+            feed_grad = scatter(part_sums)
+            waits = (part_sums,)
+        raw_grad, pair_part, query_gain_part, result, extra = attend_back(
             raw,
             attended_grad,
             both[step],
@@ -1045,7 +1324,17 @@
             places[step],
             step,
             after(slotted(produced[step]), *waits),
-        )
+            extra,
+            ("exp", "ctx")[min(step, 1)],
+        )
+        if step == 0:
+            sums = extra.reshape(plane, -1)[:, : micro * ring * capacity]
+            sums = sums.reshape(plane, micro, ring, capacity)
+            values = [
+                jnp.sum(jnp.where(chosen[m], sums[:, m, :, :, None], 0.0), 2) for m in range(micro)
+            ]
+            values = jnp.stack(values, 1).transpose(2, 1, 0, 3)
+            extra = values.reshape(ring, -1, 128)
         waits = (result,)
         results.append(result)
         raw_grads.append(raw_grad)
@@ -1066,33 +1355,9 @@
         pair_grads.append(pair_grad.transpose(1, 0, 2).reshape(local, 2 * pair_width))
         gain_list[step][2] = jnp.sum(key_gain_part, (0, 1))
 
-    attended_all, branch_all = jnp.concatenate(attended, 0), jnp.concatenate(branches, 0)
-    raw_grad = jnp.concatenate(
-        [jnp.concatenate(raw_grads, 0), jnp.concatenate(pair_grads, 0)], 1
-    )
     if plane == 8:
-        core = lax.rem(lax.axis_index("exp"), 2)
-
-        def swapped(array):
-            return lax.ppermute(array, "exp", [(i, i + 1 - 2 * (i % 2)) for i in range(plane)])
-
-        def left_part(array):
-            share = array.shape[1] // experts
-            array = array.reshape(-1, ring, 2, 2, 2, share).transpose(4, 2, 3, 0, 1, 5)
-            array = array.reshape(2, 4, micro * local, ring * share)
-            own = lax.dynamic_index_in_dim(array, core, 0, False)
-            other = lax.dynamic_index_in_dim(array, 1 - core, 0, False)
-            return jnp.concatenate([own, swapped(other)], 1)
-
-        def right_part(array):
-            return jnp.concatenate([array, swapped(array)], 0)
-
-        out_total, in_total = grad_sums(
-            ring,
-            (left_part(attended_all), left_part(hidden)),
-            (right_part(branch_all), right_part(raw_grad)),
-            (512, 1024),
-            5,
+        out_total, in_total, hidden_grad = grad_sums(
+            ring, attended, hidden_parts, branches, raw_grads, pair_grads, in_weight, 5
         )
     else:
 
@@ -1105,11 +1370,14 @@
                 jnp.float32
             )
 
-        out_total = sum_over_devices(attended_all, branch_all)
+        out_total = sum_over_devices(jnp.concatenate(attended, 0), jnp.concatenate(branches, 0))
+        raw_grad = jnp.concatenate(
+            [jnp.concatenate(raw_grads, 0), jnp.concatenate(pair_grads, 0)], 1
+        )
         in_total = sum_over_devices(hidden, raw_grad)
+        hidden_grad = dot_t(raw_grad, in_weight)
     query_total = in_total[:, :query_width]
     pair_total = in_total[:, query_width:].reshape(-1, kv_heads, 2, head_dim)
-    hidden_grad = dot_t(raw_grad, in_weight)
     first_grad, first_gain = norm_back(rows, first_scale, norm_attn, hidden_grad)
     tokens_grad = jnp.concatenate(middle_grads, 0) + first_grad
     gains = jnp.concatenate([jnp.sum(first_gain, 0)] + [sum(parts) for parts in zip(*gain_list)])
@@ -1121,28 +1389,14 @@
     )
 
     outputs = [
-        (middles[step] + scatter(combine(results[step], step, True))).astype(jnp.bfloat16)
+        (middles[step] + scatter(combine(results[step], step, True)).astype(jnp.float32)).astype(
+            jnp.bfloat16
+        )
         for step in range(micro)
     ]
 
-    pair_values = lax.all_to_all(
-        jnp.stack([v.reshape(plane, ring, capacity) for v in pair_values], 1),
-        "exp",
-        split_axis=0,
-        concat_axis=0,
-        tiled=True,
-    )
-    values = jnp.stack(
-        [
-            jnp.sum(jnp.where(chosen[step], pair_values[:, step, :, :, None], 0.0), 2)
-            for step in range(micro)
-        ],
-        1,
-    )
-    values = lax.all_to_all(
-        values.transpose(2, 1, 3, 0), "ctx", split_axis=0, concat_axis=0, tiled=True
-    )
-    values = values.transpose(1, 2, 0, 3).reshape(micro, local, experts)
+    values = extra.reshape(ring, micro, plane, local).transpose(1, 3, 0, 2)
+    values = values.reshape(micro, local, experts)
     match = routes[:, 0, :, :, None] == jnp.arange(experts, dtype=jnp.int32)
     route_grads = jnp.sum(jnp.where(match, values[:, :, None, :], 0.0), -1) / route_weights[:, 0]
 

time: 1750 us -> 1490 us (0.85)
  waiting for transfers between devices: 393 us -> 276 us
  other arithmetic: 116 us -> 52.8 us
  matrix products: 129 us -> 74 us
  local copies, waits for them, and re-layouts: 84.7 us -> 59 us
    reduce_scatter x4, waiting for transfers between devices: 73.6 us -> 0.03 us  [scatter(): return lax.psum_scatter(part, 'ctx', scatter_dimension=0, tiled=True)]
    concatenate x8 -> x0, other arithmetic: 58 us -> none  [the longest x1 18.4 us: per_device(): jnp.concatenate([jnp.concatenate(raw_grads, 0), jnp.concatenate(pair_grad...]
    all_gather x2, waiting for transfers between devices: 160 us -> 114 us  [per_device(): lax.all_gather(feed, 'ctx', axis=0, tiled=True)]
    dot_general x4 -> x0, matrix products: 37.8 us -> none  [combine(): jnp.einsum('jcst,jcsd->ctd', factor.astype(jnp.bfloat16), back, preferred...]
    dot_general x3 -> x2, matrix products: 53.8 us -> 36.9 us  [dot_t(): return jnp.einsum('te,de->td', a, b, preferred_element_type=jnp.float32)]
    pallas_call x5 -> x8, Pallas kernels: 512 us -> 526 us  [the longest x2 220 us: line_gather(): pl.pallas_call(functools.partial(gather_kernel, count, arrays, stacked),...]
  transfers between devices with their start and end apart: 20 -> 14, of which waited for: 10 -> 6; matrix products, arithmetic and copies ran while one was open for 14% -> 11% of each run, Pallas kernels for 42% -> 64%
where the time goes in v4:
time: 1490 us; the launch traced here: 1480 us
  Pallas kernels  971 us (65%)
  waiting for transfers between devices  276 us (19%)
  matrix products  74 us (5%)
  local copies, waits for them, and re-layouts  59 us (4%)
  other arithmetic  52.8 us (4%)
  starting transfers between devices  34.3 us (2%)
  between operations  15.4 us (1%)
    pallas_call x2, Pallas kernels, attend_back(): pl.pallas_call(functools.partial(attend_back_kernel, per, steps, width **...  237 us
    pallas_call x2, Pallas kernels, line_gather(): pl.pallas_call(functools.partial(gather_kernel, count, arrays, stacked),...  220 us
    pallas_call x1, Pallas kernels, grad_sums(): pl.pallas_call(functools.partial(grad_sums_kernel, ring, micro, sizes), i...  199 us
    all_to_all x5, waiting for transfers between devices, exchange(): return lax.all_to_all(rows, 'exp', split_axis=0, concat_axis=0, tiled=True)  161 us
    pallas_call x2, Pallas kernels, run_expert(): pl.pallas_call(expert_kernel, grid=(sources,), in_specs=[pl.BlockSpec((No...  115 us
    all_gather x2, waiting for transfers between devices, per_device(): lax.all_gather(feed, 'ctx', axis=0, tiled=True)  114 us
    pallas_call x1, Pallas kernels, expert_weight_grads(): pl.pallas_call(functools.partial(weight_kernel, steps, micro), grid=(micr...  73.3 us
    pallas_call x2, Pallas kernels, attend(): pl.pallas_call(functools.partial(attend_kernel, per, width ** (-0.5) * ma...  47.9 us
  transfers between devices with their start and end apart: 14, of which 6 were waited for; matrix products, arithmetic and copies ran while one was open for 11% of the time, Pallas kernels for 64%

profile of v4, /device:TPU:0, one launch (start us, length us, event | category | flops | bytes accessed | tf_op | source)
XLA Modules:
  0.0 1482.6 jit_solution(11229747930352897598)
XLA Ops:
  7.2 2.0 stack_reshape.16
  12.9 3.3 pad_maximum_fusion
  19.3 145.2 %shard_map.239 = (bf16[2,1024,2048]{2,1,0:T(8,128)(2,1)}, f32[256,128]{1,0:T(8,128)}) custom-call(bf16[256,2048]{1,0:T(8,128)(2,1)} %get-tuple-element.177.refs_0_, bf16[256,2048]{1,0:T(8,128)(2,1)} %get-tuple-element.176.refs_1_, f32[64,128]{1,0:T(8,128)} %reshape.334.refs_2_), custom_call_target="tpu_custom_call" | custom-call | bytes 209715200 | tf_op jit(solution)/shard_map/pallas_call | solution.py:134
  170.0 22.6 %shard_map.240.refs_1_ = bf16[8,8,80,2048]{3,2,1,0:T(8,128)(2,1)} custom-call(s32[8,2,4,256]{3,2,1,0:T(4,128)} %reshape.336.place_ref, f32[8,2,4,256]{3,2,1,0:T(4,128)} %reshape.337.weight_ref, bf16[2048,2048]{1,0:T(8,128)(2,1)} %bitcast.244), custom_call_target="tpu_custom_call" | custom-call | flops 1048576 | bytes 1048576 | tf_op jit(solution)/shard_map/pallas_call | solution.py:262
  192.7 6.2 all-to-all-start
  199.0 2.5 convert_element_type.130
  208.0 15.0 %fusion.52.raw_ref = f32[512,5120]{1,0:T(8,128)S(1)} fusion(bf16[512,2048]{1,0:T(8,128)(2,1)} %shard_map.241, bf16[2048,5120]{1,0:T(8,128)(2,1)} %all-gather.5.cloned.1.call-done.refs_9_), kind=kOutput, calls=%fused_computation.161 | convolution fusion | flops 10737418240 | bytes 33554432 | tf_op jit(solution)/shard_map/dot_general | solution.py:1161
  223.0 3.9 copy-done
  228.3 3.0 reshape.340
  241.9 74.4 %shard_map.242 = (bf16[1024,1024]{1,0:T(8,128)(2,1)}, bf16[1024,1024]{1,0:T(8,128)(2,1)}) custom-call(bf16[256,1024]{1,0:T(8,128)(2,1)} %slice.158.refs_0_, bf16[256,1024]{1,0:T(8,128)(2,1)} %slice.160.refs_1_), custom_call_target="tpu_custom_call" | custom-call | bytes 209715200 | tf_op jit(solution)/shard_map/pallas_call | solution.py:134
  316.3 24.1 %shard_map.243.refs_0_ = bf16[256,4096]{1,0:T(8,128)(2,1)} custom-call(s32[2]{0:T(128)} %get-tuple-element.222.place_ref, f32[512,5120]{1,0:T(8,128)} %copy-done, bf16[4,256,1024]{2,1,0:T(8,128)(2,1)} %bitcast.249, f32[1,128]{1,0:T(1,128)} %bitcast.280, f32[256,128]{1,0:T(8,128)} %copy-done.16, f32[256,128]{1,0:T(8,128)} %copy-done.18), custom_call_target="tpu_custom_call" | custom-call | flops 1048576 | bytes 1048576 | tf_op jit(solution)/shard_map/pallas_call | solution.py:627
  340.4 11.6 multiply_reduce_fusion.1
  354.8 23.8 %shard_map.244.refs_1_ = bf16[256,4096]{1,0:T(8,128)(2,1)} custom-call(s32[2]{0:T(128)} %get-tuple-element.223.place_ref, f32[512,5120]{1,0:T(8,128)} %copy-done, bf16[4,256,1024]{2,1,0:T(8,128)(2,1)} %bitcast.245, f32[1,128]{1,0:T(1,128)} %bitcast.281, f32[256,128]{1,0:T(8,128)} %copy-done.16, f32[256,128]{1,0:T(8,128)} %copy-done.18, ...), custom_call_target="tpu_custom_call" | custom-call | flops 1048576 | bytes 1048576 | tf_op jit(solution)/shard_map/pallas_call | solution.py:627
  378.6 8.9 multiply_reduce_fusion
  390.0 44.5 %all-gather.9.cloned.1.call-done.refs_0_ = bf16[1024,2048]{1,0:T(8,128)(2,1)} async-done(((bf16[256,2048]{1,0:T(8,128)(2,1)}), bf16[1024,2048]{1,0:T(8,128)(2,1)}) %all-gather.9.cloned.1.call-update) | async-done | bytes 4194320 | tf_op jit(solution)/shard_map/all_gather | solution.py:1266
  434.6 11.4 shard_map.246
  445.9 5.2 all-to-all-start.1
  453.0 3.9 copy.180
  456.9 3.1 copy.181
  460.0 4.2 copy.182.refs_2_
  464.3 69.3 %all-gather.11.cloned.1.call-done.rows_ref = bf16[1024,2048]{1,0:T(8,128)(2,1)} async-done(((bf16[256,2048]{1,0:T(8,128)(2,1)}), bf16[1024,2048]{1,0:T(8,128)(2,1)}) %all-gather.11.cloned.1.call-update) | async-done | bytes 4194320 | tf_op jit(solution)/shard_map/all_gather | solution.py:1266
  533.6 11.4 shard_map.249
  544.9 22.7 %all-to-all-done.1.rows_ref.refs_1_.refs_0_ = bf16[8,320,2048]{2,1,0:T(8,128)(2,1)} async-done(((bf16[8,320,2048]{2,1,0:T(8,128)(2,1)}), bf16[8,320,2048]{2,1,0:T(8,128)(2,1)}, u32[]{:S(2)}, u32[]{:S(2)}) %all-to-all-start.1) | async-done | bytes 10485792 | tf_op jit(solution)/shard_map/all_to_all | solution.py:1198
  567.6 5.3 all-to-all-start.2
  573.0 57.6 %shard_map.248 = (bf16[2560,768]{1,0:T(8,128)(2,1)}, bf16[2560,768]{1,0:T(8,128)(2,1)}, bf16[2560,768]{1,0:T(8,128)(2,1)}, bf16[2560,2048]{1,0:T(8,128)(2,1)}, b...) custom-call(bf16[8,320,2048]{2,1,0:T(8,128)(2,1)} %all-to-all-done.1.rows_ref.refs_1_.refs_0_, ...), custom_call_target="tpu_custom_call" | custom-call | flops 1048576 | bytes 1048576 | tf_op jit(solution)/shard_map/pallas_call | solution.py:192
  630.6 58.9 %all-to-all-done.2.refs_1_.rows_ref = bf16[8,320,2048]{2,1,0:T(8,128)(2,1)} async-done(((bf16[8,320,2048]{2,1,0:T(8,128)(2,1)}), bf16[8,320,2048]{2,1,0:T(8,128)(2,1)}, u32[]{:S(2)}, u32[]{:S(2)}) %all-to-all-start.2) | async-done | bytes 10485792 | tf_op jit(solution)/shard_map/all_to_all | solution.py:1198
  689.5 5.2 all-to-all-start.3
  694.8 57.6 %shard_map.252 = (bf16[2560,768]{1,0:T(8,128)(2,1)}, bf16[2560,768]{1,0:T(8,128)(2,1)}, bf16[2560,768]{1,0:T(8,128)(2,1)}, bf16[2560,2048]{1,0:T(8,128)(2,1)}, b...) custom-call(bf16[8,320,2048]{2,1,0:T(8,128)(2,1)} %all-to-all-done.2.refs_1_.rows_ref, ...), custom_call_target="tpu_custom_call" | custom-call | flops 1048576 | bytes 1048576 | tf_op jit(solution)/shard_map/pallas_call | solution.py:192
  752.3 58.9 %all-to-all-done.3.refs_0_.refs_1_ = bf16[8,320,2048]{2,1,0:T(8,128)(2,1)} async-done(((bf16[8,320,2048]{2,1,0:T(8,128)(2,1)}), bf16[8,320,2048]{2,1,0:T(8,128)(2,1)}, u32[]{:S(2)}, u32[]{:S(2)}) %all-to-all-start.3) | async-done | bytes 10485792 | tf_op jit(solution)/shard_map/all_to_all | solution.py:1198
  811.2 8.3 shard_map.254
  819.6 5.5 all-to-all-start.4
  825.2 73.3 %shard_map.256 = (f32[1,2048,768]{2,1,0:T(8,128)}, f32[1,2048,768]{2,1,0:T(8,128)}, f32[1,768,2048]{2,1,0:T(8,128)}) custom-call(bf16[8,320,2048]{2,1,0:T(8,128)(2,1)} %all-to-all-done.1.rows_ref.refs_1_.refs_0_, bf16[8,320,2048]{2,1,0:T(8,128)(2,1)} %all-to-all-done.2.refs_1_.rows_ref, bf16[8,2,320,2048]{3,2,1,0:T(8,128)(2,1)} %bitcast.30.refs_1_.grad_ref.refs_2_, ...), custom_call_target="tpu_custom_call" | custom-call | flops 1048576 | bytes 1048576 | tf_op jit(solution)/shard_map/pallas_call | solution.py:342
  900.7 2.1 fusion.46
  902.8 18.4 %convolution_convert_fusion.1.refs_2_.grad_ref = bf16[256,4096]{1,0:T(8,128)(2,1)} fusion(bf16[256,2048]{1,0:T(8,128)(2,1)S(1)} %get-tuple-element.172.refs_3_, bf16[4096,2048]{1,0:T(8,128)(2,1)} %all-gather.7.cloned.1.call-done), kind=kOutput, calls=%fused_computation.1 | convolution fusion | flops 4296015872 | bytes 19922944 | tf_op jit(solution)/shard_map/te,de->td/dot_general | solution.py:1164
  921.2 20.5 %all-to-all-done.4.refs_0_ = bf16[8,320,2048]{2,1,0:T(8,128)(2,1)} async-done(((bf16[8,320,2048]{2,1,0:T(8,128)(2,1)}), bf16[8,320,2048]{2,1,0:T(8,128)(2,1)}, u32[]{:S(2)}, u32[]{:S(2)}) %all-to-all-start.4) | async-done | bytes 10485792 | tf_op jit(solution)/shard_map/all_to_all | solution.py:1198
  941.7 8.3 shard_map.258.refs_1_
  953.0 119.7 %shard_map.260 = (bf16[256,4096]{1,0:T(8,128)(2,1)}, bf16[4,4,256,256]{3,2,1,0:T(8,128)(2,1)}, f32[8,128]{1,0:T(8,128)}, bf16[8,320,2048]{2,1,0:T(8,128)(2,1)}, f32[8,8,128]{2,1,0:T(8,128)}) custom-call(s32[2]{0:T(128)} %get-tuple-element.222.place_ref, f32[512,5120]{1,0:T(8,128)} %copy-done, bf16[256,4096]{1,0:T(8,128)(2,1)} %convolution_convert_fusion.1.refs_2_.grad_ref, ...), custom_call_target="tpu_custom_call" | custom-call | flops 1048576 | bytes 1048576 | tf_op jit(solution)/shard_map/pallas_call | solution.py:652
  1072.7 8.3 shard_map.261
  1084.4 2.1 copy-done.4
  1088.7 2.1 fusion.44
  1090.8 18.5 %convolution_convert_fusion.grad_ref = bf16[256,4096]{1,0:T(8,128)(2,1)} fusion(bf16[256,2048]{1,0:T(8,128)(2,1)S(1)} %get-tuple-element.170.refs_4_, bf16[4096,2048]{1,0:T(8,128)(2,1)} %all-gather.7.cloned.1.call-done), kind=kOutput, calls=%fused_computation | convolution fusion | flops 4296015872 | bytes 19922944 | tf_op jit(solution)/shard_map/te,de->td/dot_general | solution.py:1164
  1109.3 117.0 %shard_map.264 = (bf16[256,4096]{1,0:T(8,128)(2,1)}, bf16[4,4,256,256]{3,2,1,0:T(8,128)(2,1)}, f32[8,128]{1,0:T(8,128)}, bf16[8,320,2048]{2,1,0:T(8,128)(2,1)}, f32[4,32,128]{2,1,0:T(8,128)}) custom-call(s32[2]{0:T(128)} %get-tuple-element.223.place_ref, f32[512,5120]{1,0:T(8,128)} %copy-done, bf16[256,4096]{1,0:T(8,128)(2,1)} %convolution_convert_fusion.grad_ref, ...), custom_call_target="tpu_custom_call" | custom-call | flops 1048576 | bytes 1048576 | tf_op jit(solution)/shard_map/pallas_call | solution.py:652
  1226.4 8.4 shard_map.265
  1246.3 199.3 %shard_map.266 = (f32[128,2048]{1,0:T(8,128)}, f32[64,5120]{1,0:T(8,128)}, f32[512,2048]{1,0:T(8,128)}, bf16[2,256,2048]{2,1,0:T(8,128)(2,1)}, bf16[2,256,4096]{...) custom-call(bf16[256,4096]{1,0:T(8,128)(2,1)} %shard_map.243.refs_0_, bf16[256,4096]{1,0:T(8,128)(2,1)} %shard_map.244.refs_1_, ...), custom_call_target="tpu_custom_call" | custom-call | flops 1048576 | bytes 1048576 | tf_op jit(solution)/shard_map/pallas_call | solution.py:1110
  1446.3 3.5 fusion.7
  1450.6 6.6 all-to-all-start.5
  1459.2 2.3 fusion.22
  1462.3 5.4 maximum_add_fusion
  (268 shorter events, 71.5 us)
Async XLA Ops:
  7.2 200.8 %all-gather.5.cloned.1.call-start = ((), (), s32[]{:S(2)}) async-start(), calls=%async_computation.10 | async-start | bytes 23592960 | tf_op jit(solution)/shard_map/all_gather | solution.py:1175
  16.2 324.2 %all-gather.7.cloned.1.call-start = ((), (), s32[]{:S(2)}) async-start(), calls=%async_computation.11 | async-start | bytes 18874368 | tf_op jit(solution)/shard_map/all_gather | solution.py:1178
  167.0 186.5 %copy-start.29 = (f32[4,256,8]{1,2,0:T(8,128)}, f32[4,256,8]{1,2,0:T(8,128)S(1)}, u32[]{:S(2)}) copy-start(f32[4,256,8]{1,2,0:T(8,128)S(1)} %get-tuple-element.164) | copy-start | bytes 98308
  167.0 284.7 %copy-start.28 = (f32[4,256,8]{1,2,0:T(8,128)}, f32[4,256,8]{1,2,0:T(8,128)S(1)}, u32[]{:S(2)}) copy-start(f32[4,256,8]{1,2,0:T(8,128)S(1)} %get-tuple-element.165) | copy-start | bytes 98308
  167.8 24.9 %copy-start.42 = (pred[4,256,8]{1,2,0:T(8,128)(4,1)}, pred[4,256,8]{1,2,0:T(8,128)(4,1)S(1)}, u32[]{:S(2)}) copy-start(pred[4,256,8]{1,2,0:T(8,128)(4,1)S(1)} %get-tuple-element.167) | copy-start | bytes 24580
  167.8 24.9 %copy-start.44 = (pred[4,256,8]{1,2,0:T(8,128)(4,1)}, pred[4,256,8]{1,2,0:T(8,128)(4,1)S(1)}, u32[]{:S(2)}) copy-start(pred[4,256,8]{1,2,0:T(8,128)(4,1)S(1)} %get-tuple-element.166) | copy-start | bytes 24580
  168.6 283.7 %copy-start.30 = (s32[4,8,256]{2,1,0:T(8,128)}, s32[4,8,256]{2,1,0:T(8,128)S(1)}, u32[]{:S(2)}) copy-start(s32[4,8,256]{2,1,0:T(8,128)S(1)} %get-tuple-element.214.place_ref) | copy-start | bytes 98308
  169.4 184.7 %copy-start.31 = (s32[4,8,256]{2,1,0:T(8,128)}, s32[4,8,256]{2,1,0:T(8,128)S(1)}, u32[]{:S(2)}) copy-start(s32[4,8,256]{2,1,0:T(8,128)S(1)} %get-tuple-element.216.place_ref) | copy-start | bytes 98308
  192.7 6.3 copy-start.1
  192.7 253.3 %all-to-all-start = ((bf16[8,640,2048]{2,1,0:T(8,128)(2,1)}), bf16[8,640,2048]{2,1,0:T(8,128)(2,1)}, u32[]{:S(2)}, u32[]{:S(2)}) async-start(bf16[8,640,2048]{2,1,0:T(8,128)(2,1)} %bitcast.229), calls=%async_computation | async-start | bytes 41943040 | tf_op jit(solution)/shard_map/all_to_all | solution.py:1198
  198.9 235.6 %all-gather.9.cloned.1.call-start = ((), (), s32[]{:S(2)}) async-start(), calls=%async_computation.12 | async-start | bytes 5242880 | tf_op jit(solution)/shard_map/all_gather | solution.py:1266
  202.1 2.1 copy-start.40
  207.9 27.9 %copy-start.16 = (f32[256,128]{1,0:T(8,128)}, f32[256,128]{1,0:T(8,128)S(1)}, u32[]{:S(2)}) copy-start(f32[256,128]{1,0:T(8,128)S(1)} %get-tuple-element.224.cos_ref) | copy-start | bytes 393220
  207.9 27.9 %copy-start.18 = (f32[256,128]{1,0:T(8,128)}, f32[256,128]{1,0:T(8,128)S(1)}, u32[]{:S(2)}) copy-start(f32[256,128]{1,0:T(8,128)S(1)} %get-tuple-element.225.sin_ref) | copy-start | bytes 393220
  223.0 3.9 copy-start
  231.4 1.8 copy-start.8
  340.4 11.6 copy-start.32
  352.0 548.6 %copy-start.6 = (f32[256,2048]{1,0:T(8,128)}, f32[256,2048]{1,0:T(8,128)S(1)}, u32[]{:S(2)}) copy-start(f32[256,2048]{1,0:T(8,128)S(1)} %get-tuple-element.219) | copy-start | bytes 6291460
  354.8 23.8 %copy-start.22 = (f32[2,1,256,2048]{3,2,1,0:T(8,128)S(1)}, f32[2,1,256,2048]{3,2,1,0:T(8,128)}, u32[]{:S(2)}) copy-start(f32[2,1,256,2048]{3,2,1,0:T(8,128)} %convert_element_type.130) | copy-start | bytes 12582916
  388.1 46.5 %copy-start.49 = (f32[256]{0:T(256)}, f32[256]{0:T(256)S(1)}, u32[]{:S(2)}) copy-start(f32[256]{0:T(256)S(1)} %get-tuple-element.207) | copy-start | bytes 3076
  445.9 121.7 %all-to-all-start.1 = ((bf16[8,320,2048]{2,1,0:T(8,128)(2,1)}), bf16[8,320,2048]{2,1,0:T(8,128)(2,1)}, u32[]{:S(2)}, u32[]{:S(2)}) async-start(bf16[8,320,2048]{2,1,0:T(8,128)(2,1)} %shard_map.247), calls=%async_computation.1 | async-start | bytes 20971520 | tf_op jit(solution)/shard_map/all_to_all | solution.py:1198
  451.1 82.4 %all-gather.11.cloned.1.call-start = ((), (), s32[]{:S(2)}) async-start(), calls=%async_computation.13 | async-start | bytes 5242880 | tf_op jit(solution)/shard_map/all_gather | solution.py:1266
  567.6 121.9 %all-to-all-start.2 = ((bf16[8,320,2048]{2,1,0:T(8,128)(2,1)}), bf16[8,320,2048]{2,1,0:T(8,128)(2,1)}, u32[]{:S(2)}, u32[]{:S(2)}) async-start(bf16[8,320,2048]{2,1,0:T(8,128)(2,1)} %shard_map.250), calls=%async_computation.2 | async-start | bytes 20971520 | tf_op jit(solution)/shard_map/all_to_all | solution.py:1198
  689.5 121.7 %all-to-all-start.3 = ((bf16[8,320,2048]{2,1,0:T(8,128)(2,1)}), bf16[8,320,2048]{2,1,0:T(8,128)(2,1)}, u32[]{:S(2)}, u32[]{:S(2)}) async-start(bf16[8,320,2048]{2,1,0:T(8,128)(2,1)} %shard_map.251), calls=%async_computation.3 | async-start | bytes 20971520 | tf_op jit(solution)/shard_map/all_to_all | solution.py:1198
  694.7 203.8 %reduce-scatter.5.cloned.1.call-start = ((), (), s32[]{:S(2)}) async-start(), calls=%async_computation.14 | async-start | bytes 5242880 | tf_op jit(solution)/shard_map/reduce_scatter | solution.py:1220
  819.6 122.1 %all-to-all-start.4 = ((bf16[8,320,2048]{2,1,0:T(8,128)(2,1)}), bf16[8,320,2048]{2,1,0:T(8,128)(2,1)}, u32[]{:S(2)}, u32[]{:S(2)}) async-start(bf16[8,320,2048]{2,1,0:T(8,128)(2,1)} %shard_map.255), calls=%async_computation.5 | async-start | bytes 20971520 | tf_op jit(solution)/shard_map/all_to_all | solution.py:1198
  825.1 259.2 %reduce-scatter.9.cloned.1.call-start = ((), (), s32[]{:S(2)}) async-start(), calls=%async_computation.16 | async-start | bytes 5242880 | tf_op jit(solution)/shard_map/reduce_scatter | solution.py:1220
  898.5 2.1 copy-start.12
  898.6 2.2 copy-start.23
  902.8 18.4 %copy-start.20 = (bf16[256,2048]{1,0:T(8,128)(2,1)}, bf16[256,2048]{1,0:T(8,128)(2,1)S(1)}, u32[]{:S(2)}) copy-start(bf16[256,2048]{1,0:T(8,128)(2,1)S(1)} %get-tuple-element.172.refs_3_) | copy-start | bytes 3145732
  950.0 1.8 copy-start.25
  950.0 509.1 %reduce-scatter.7.cloned.1.call-start = ((), (), s32[]{:S(2)}) async-start(), calls=%async_computation.15 | async-start | bytes 5242880 | tf_op jit(solution)/shard_map/reduce_scatter | solution.py:1220
  1081.1 390.4 %reduce-scatter.11.cloned.1.call-start = ((), (), s32[]{:S(2)}) async-start(), calls=%async_computation.17 | async-start | bytes 5242880 | tf_op jit(solution)/shard_map/reduce_scatter | solution.py:1220
  1084.3 2.1 copy-start.4
  1084.3 2.1 copy-start.50
  1086.5 2.0 copy-start.10
  1086.5 2.2 copy-start.13
  1086.5 2.2 copy-start.53
  1090.8 18.5 %copy-start.21 = (bf16[256,2048]{1,0:T(8,128)(2,1)}, bf16[256,2048]{1,0:T(8,128)(2,1)S(1)}, u32[]{:S(2)}) copy-start(bf16[256,2048]{1,0:T(8,128)(2,1)S(1)} %get-tuple-element.170.refs_4_) | copy-start | bytes 3145732
  1246.3 200.0 %copy-start.2 = (bf16[2,1,256,2048]{3,2,1,0:T(8,128)(2,1)S(1)}, bf16[2,1,256,2048]{3,2,1,0:T(8,128)(2,1)}, u32[]{:S(2)}) copy-start(bf16[2,1,256,2048]{3,2,1,0:T(8,128)(2,1)} %param.16) | copy-start | bytes 6291460
  1246.3 200.0 %copy-start.34 = (f32[2048]{0:T(1024)S(1)}, f32[2048]{0:T(1024)}, u32[]{:S(2)}) copy-start(f32[2048]{0:T(1024)} %param.20) | copy-start | bytes 24580
  1446.3 12.1 copy-start.35
  1446.3 12.1 copy-start.39
  1446.3 12.2 copy-start.37
  1450.6 20.3 %all-to-all-start.5 = ((f32[32,1,136]{2,1,0:T(1,128)}), f32[32,1,136]{2,1,0:T(1,128)S(1)}, u32[]{:S(2)}, u32[]{:S(2)}) async-start(f32[32,1,136]{2,1,0:T(1,128)} %all_to_all.26), calls=%async_computation.9 | async-start | bytes 65536 | tf_op jit(solution)/shard_map/all_to_all | solution.py:1385
  1459.2 3.1 copy-start.7
  1462.3 6.2 copy-start.26
  1467.7 3.7 copy-start.5
  (21 other events, 21.7 us)
Sparse Core Ops, SparseCore 0:
  16.3 110.2 all-gather.4
  128.5 103.7 all-gather.6
  353.6 80.9 all-gather.8
  453.8 79.7 all-gather.10
  819.7 73.5 reduce-scatter.4
  950.1 108.3 reduce-scatter.8
  1081.2 105.0 reduce-scatter.6
  1234.9 79.5 reduce-scatter.10

commit v5 on v4

--- a/solution.py
+++ b/solution.py
@@ -11,6 +11,7 @@
 EPSILON = 1e-06
 ROPE_BASE = 1000000.0
 MASKED = -1e30
+LAGS = (2, 3, 5)
 VMEM_BYTES = 56 * 2**20
 SMALL = pl.CostEstimate(flops=2**20, bytes_accessed=2**20, transcendentals=0)
 
@@ -526,15 +527,18 @@
     extra_axis,
     place_ref,
     raw_ref,
-    grad_ref,
+    branch_ref,
+    weight_ref,
     both_ref,
+    pair_raw_ref,
     gain_ref,
+    key_gain_ref,
     cos_ref,
     sin_ref,
     rows_ref,
     extra_ref,
     raw_grad_ref,
-    landed_ref,
+    pair_grad_ref,
     gain_grad_ref,
     moved_ref,
     extra_moved_ref,
@@ -542,6 +546,7 @@
     turned_ref,
     sums_ref,
     held_ref,
+    landed_ref,
     *sems,
 ):
     width = gain_ref.shape[1]
@@ -555,9 +560,6 @@
         greet(exp=count, ctx=ring)
         moving.begin()
         extra_moving.begin()
-
-    @pl.when((group_step == 0) & (step == 0))
-    def _():
         fill_mask(place_ref, mask_ref)
         gain_grad_ref[...] = jnp.zeros_like(gain_grad_ref)
 
@@ -566,11 +568,20 @@
         turned_ref[...] = keyed(both_ref, width, 0).T
         sums_ref[...] = jnp.zeros_like(sums_ref)
 
+    def turned_back(grad, raw, norm, gain, row):
+        back = grad * cos_ref[...] - pltpu.roll(grad, width // 2, 1) * sin_ref[...]
+        inner = back * gain
+        gain_grad_ref[row : row + 1, :] += jnp.sum(back * raw * norm, 0, keepdims=True)
+        return (
+            norm * inner - raw * (norm * norm * norm) * jnp.mean(inner * raw, -1, keepdims=True)
+        ).astype(jnp.bfloat16)
+
+    grads = across(branch_ref[...], weight_ref[...]).astype(jnp.bfloat16)
     for head in range(per):
         columns = slice(head * width, (head + 1) * width)
         raw = raw_ref[:, columns]
         queries, norm = head_queries(raw, gain_ref[...], cos_ref[...], sin_ref[...])
-        grad = grad_ref[:, columns]
+        grad = grads[:, columns]
         chances = jnp.exp2(across(keyed(both_ref, width, 0), queries) * factor + mask_ref[...])
         chances = chances * (1.0 / jnp.sum(chances, 0, keepdims=True))
         chance_grad = across(keyed(both_ref, width, 1), grad)
@@ -579,12 +590,9 @@
         sums_ref[:, :width] += along(score_grad, queries)
         sums_ref[:, width:] += along(chances.astype(jnp.bfloat16), grad)
         query_grad = (along(turned_ref[...], score_grad) * scale).astype(jnp.bfloat16)
-        query_grad = query_grad.astype(jnp.float32).T
-        back = query_grad * cos_ref[...] - pltpu.roll(query_grad, width // 2, 1) * sin_ref[...]
-        inner = back * gain_ref[...]
-        first = norm * inner - raw * (norm * norm * norm) * jnp.mean(inner * raw, -1, keepdims=True)
-        raw_grad_ref[:, columns] = first.astype(jnp.bfloat16)
-        gain_grad_ref[0:1, :] += jnp.sum(back * raw * norm, 0, keepdims=True)
+        raw_grad_ref[:, columns] = turned_back(
+            query_grad.astype(jnp.float32).T, raw, norm, gain_ref[...], 0
+        )
 
     @pl.when(step == steps - 1)
     def _():
@@ -595,6 +603,18 @@
     @pl.when((group_step == pl.num_programs(0) - 1) & (step == steps - 1))
     def _():
         landing.finish()
+        for group in range(landed_ref.shape[1]):
+            total = landed_ref[0, group].astype(jnp.float32)
+            for other in range(1, ring):
+                total += landed_ref[other, group].astype(jnp.float32)
+            total = total.astype(jnp.bfloat16)
+            start = 2 * group * width
+            raw = pair_raw_ref[:, start : start + width]
+            norm = lax.rsqrt(jnp.mean(raw * raw, -1, keepdims=True) + EPSILON)
+            pair_grad_ref[:, start : start + width] = turned_back(
+                total[:, :width].astype(jnp.float32), raw, norm, key_gain_ref[...], 1
+            )
+            pair_grad_ref[:, start + width : start + 2 * width] = total[:, width:]
         extra_moving.finish()
         moving.finish()
 
@@ -641,14 +661,29 @@
 
 
 def attend_back(
-    raw, grad, both, gain, cosine, sine, place, step, rows_out, extra, extra_axis, per=2
+    raw,
+    branch,
+    weight,
+    both,
+    gain,
+    key_gain,
+    cosine,
+    sine,
+    place,
+    step,
+    rows_out,
+    extra,
+    extra_axis,
+    per=2,
 ):
     rows, width = cosine.shape
     kv_heads, heads, steps, keys, specs, params, work = attention_specs(
         raw, both, width, rows, step, per
     )
-    count = rows_out.shape[0]
+    count, ring = rows_out.shape[0], both.shape[0]
     anywhere = pl.BlockSpec(memory_space=pl.ANY)
+    pairs = 2 * kv_heads * width
+    pair_place = heads * width // pairs
     return pl.pallas_call(
         functools.partial(
             attend_back_kernel,
@@ -657,22 +692,34 @@
             width ** (-0.5) * math.log2(math.e),
             width ** (-0.5),
             count,
-            both.shape[0],
+            ring,
             extra_axis,
         ),
         grid=(kv_heads, steps),
-        in_specs=[specs[k] for k in ("place", "raw", "heads", "both", "gain", "table", "table")]
-        + [anywhere] * 2,
+        in_specs=[
+            specs["place"],
+            specs["raw"],
+            pl.BlockSpec(branch.shape, lambda g, j: (0, 0)),
+            pl.BlockSpec((per * width, weight.shape[1]), lambda g, j: (g * steps + j, 0)),
+            specs["both"],
+            pl.BlockSpec((rows, pairs), lambda g, j: (step, pair_place)),
+            specs["gain"],
+            specs["gain"],
+            specs["table"],
+            specs["table"],
+            anywhere,
+            anywhere,
+        ],
         out_specs=(
             specs["heads"],
-            anywhere,
+            pl.BlockSpec((rows, pairs), lambda g, j: (0, 0)),
             pl.BlockSpec((8, width), lambda g, j: (0, 0)),
             anywhere,
             anywhere,
         ),
         out_shape=(
             jax.ShapeDtypeStruct((rows, heads * width), jnp.bfloat16),
-            jax.ShapeDtypeStruct((both.shape[0], kv_heads, rows, 2 * width), jnp.bfloat16),
+            jax.ShapeDtypeStruct((rows, pairs), jnp.bfloat16),
             jax.ShapeDtypeStruct((8, width), jnp.float32),
             jax.ShapeDtypeStruct(rows_out.shape, rows_out.dtype),
             jax.ShapeDtypeStruct(extra.shape, extra.dtype),
@@ -682,14 +729,29 @@
             pltpu.VMEM((width, keys), jnp.bfloat16),
             pltpu.VMEM((keys, 2 * width), jnp.float32),
             pltpu.VMEM((kv_heads, keys, 2 * width), jnp.bfloat16),
+            pltpu.VMEM((ring, kv_heads, rows, 2 * width), jnp.bfloat16),
         ]
-        + Exchange.scratch(count) + Exchange.scratch(extra.shape[0])
-        + RowExchange.scratch(both.shape[0], kv_heads),
+        + Exchange.scratch(count)
+        + Exchange.scratch(extra.shape[0])
+        + RowExchange.scratch(ring, kv_heads),
         compiler_params=pltpu.CompilerParams(
             vmem_limit_bytes=VMEM_BYTES, collective_id=1 + step, has_side_effects=True
         ),
         cost_estimate=SMALL,
-    )(place, raw, grad, both, gain, cosine, sine, rows_out, extra)
+    )(
+        place,
+        raw,
+        branch,
+        weight,
+        both,
+        raw,
+        gain,
+        key_gain,
+        cosine,
+        sine,
+        rows_out,
+        extra,
+    )
 
 
 def combine_kernel(place_ref, weight_ref, back_ref, out_ref, *, weighted):
@@ -728,18 +790,19 @@
 
 
 class GradSums:
-    def __init__(self, ring, micro, sizes, refs):
+    def __init__(self, ring, micro, head_dim, sizes, refs):
         self.ring, self.micro, self.sizes = ring, micro, sizes
+        self.head_dim = head_dim
         self.attended, self.hidden = refs[:micro], refs[micro]
         refs = refs[micro + 1 :]
         self.branch, self.query, self.pair = (
             refs[i * micro : (i + 1) * micro] for i in range(3)
         )
         self.weight = refs[3 * micro]
-        self.out = refs[3 * micro + 1 : 3 * micro + 3]
-        self.hidden_grad = refs[3 * micro + 3]
-        self.far = refs[3 * micro + 4 : 3 * micro + 7]
-        scratch = refs[3 * micro + 7 :]
+        self.out = refs[3 * micro + 1 : 3 * micro + 5]
+        self.hidden_grad = refs[3 * micro + 5]
+        self.far = refs[3 * micro + 6 : 3 * micro + 9]
+        scratch = refs[3 * micro + 9 :]
         self.left_v, self.right_v = scratch[:2], scratch[2:4]
         self.part, self.first, self.second, self.last = (
             scratch[4 + 2 * i : 6 + 2 * i] for i in range(4)
@@ -788,30 +851,27 @@
         _, high, wide = self.left_v[0].shape
         return [
             pltpu.make_async_copy(
-                self.weight.at[pl.ds(r * high, high), pl.ds((2 * chunk + h) * wide, wide)],
-                self.left_v[0].at[2 * r + h],
-                self.weight_sem.at[2 * r + h],
+                self.weight.at[pl.ds(r * high, high), pl.ds(chunk * wide, wide)],
+                self.left_v[0].at[2 * (chunk % 2) + r],
+                self.weight_sem.at[2 * (chunk % 2) + r],
             )
             for r in (0, 1)
-            for h in (0, 1)
         ]
 
     def add_hidden(self, chunk):
-        _, high, wide = self.left_v[0].shape
+        high = self.left_v[0].shape[1]
         half = self.sizes[1][0] // 2
         for copy in self.weight_loads(chunk):
             copy.wait()
         for r in (0, 1):
             columns = slice(r * high, (r + 1) * high)
-            for h in (0, 1):
-                term = across(
-                    self.right_v[1][chunk % 2, :half, h * wide : (h + 1) * wide],
-                    self.left_v[0][2 * r + h],
-                )
-                if chunk == 0 and h == 0:
-                    self.hidden_grad[:, columns] = term
-                else:
-                    self.hidden_grad[:, columns] += term
+            term = across(
+                self.right_v[1][chunk % 2, :half], self.left_v[0][2 * (chunk % 2) + r]
+            )
+            if chunk == 0:
+                self.hidden_grad[:, columns] = term
+            else:
+                self.hidden_grad[:, columns] += term
 
     def to_partner(self, src, dst, send_sem, recv_sem):
         return pltpu.make_async_remote_copy(
@@ -1027,7 +1087,15 @@
         ].astype(jnp.float32)
         for k in range(1, self.ring):
             total += self.last[kind][chunk, k].astype(jnp.float32)
-        self.out[kind][:, chunk * wide : (chunk + 1) * wide] = total
+        which, start = self.source(i)
+        if which < 2:
+            self.out[which][:, start : start + wide] = total
+            return
+        half = self.head_dim
+        for at in range(0, wide, 2 * half):
+            to = (start + at) // 2
+            self.out[2][:, to : to + half] = total[:, at : at + half]
+            self.out[3][:, to : to + half] = total[:, at + half : at + 2 * half]
 
     def run(self):
         chunks = len(self.order)
@@ -1046,11 +1114,11 @@
         pl.semaphore_wait(barrier, self.ring + 2)
         lefts = [self.left_copies(kind) for kind in (0, 1)]
         rights = [self.right_copies(which) for which in range(3)]
-        for copies in (rights[0], lefts[0][1], lefts[0][0], rights[1], *lefts[1], rights[2]):
+        for copies in (rights[0], lefts[0][1], lefts[0][0]):
             for copy in copies:
                 copy.start()
         self.start_loads(0)
-        for i in range(chunks + 6):
+        for i in range(chunks + LAGS[-1]):
             if i < chunks:
                 if i + 1 < chunks:
                     self.start_loads(i + 1)
@@ -1061,20 +1129,21 @@
                     for copy in lefts[kind][1]:
                         copy.wait_recv()
                 self.multiply(i)
+                if i == 0:
+                    for copies in (rights[1], *lefts[1], rights[2]):
+                        for copy in copies:
+                            copy.start()
                 if kind == 0 and chunk == self.sizes[0][2] // self.sizes[0][3] - 1:
                     for copy in self.weight_loads(0):
                         copy.start()
                 if kind == 1:
-                    self.add_hidden(chunk)
                     if i + 1 < chunks:
                         for copy in self.weight_loads(chunk + 1):
                             copy.start()
-            if 0 <= i - 2 < chunks:
-                self.add_first(i - 2)
-            if 0 <= i - 4 < chunks:
-                self.add_second(i - 4)
-            if 0 <= i - 6 < chunks:
-                self.add_last(i - 6)
+                    self.add_hidden(chunk)
+            for lag, stage in zip(LAGS, (self.add_first, self.add_second, self.add_last)):
+                if 0 <= i - lag < chunks:
+                    stage(i - lag)
         for copies in (lefts[0][1], lefts[1][1], *rights):
             for copy in copies:
                 copy.wait_send()
@@ -1086,38 +1155,45 @@
                 self.step_last(i, k, k).wait_send()
 
 
-def grad_sums_kernel(ring, micro, sizes, *refs):
-    GradSums(ring, micro, sizes, refs).run()
-
-
-def grad_sums(ring, attended, hidden, branch, query, pair, weight, number):
+def grad_sums_kernel(ring, micro, head_dim, sizes, *refs):
+    GradSums(ring, micro, head_dim, sizes, refs).run()
+
+
+def grad_sums(ring, head_dim, attended, hidden, branch, query, pair, weight, number):
     micro, rows = len(attended), attended[0].shape[0]
     tokens = 2 * micro * rows
     sizes = [
-        (tokens, attended[0].shape[1] // 8, branch[0].shape[1], 512),
-        (tokens, hidden.shape[3], query[0].shape[1] + pair[0].shape[1], 1024),
+        (tokens, attended[0].shape[1] // 8, branch[0].shape[1], 256),
+        (tokens, hidden.shape[3], query[0].shape[1] + pair[0].shape[1], 512),
     ]
     anywhere = pl.BlockSpec(memory_space=pl.ANY)
-    assert weight.shape[0] == 2 * tokens and sizes[1][3] == 2 * sizes[0][1]
+    assert weight.shape[0] == 2 * tokens and sizes[1][3] == sizes[0][1]
+    share = sizes[1][1] // ring
     outs = [
-        jax.ShapeDtypeStruct((size[1] // ring, size[2]), jnp.float32) for size in sizes
+        jax.ShapeDtypeStruct(shape, jnp.float32)
+        for shape in (
+            (sizes[0][1] // ring, sizes[0][2]),
+            (share, query[0].shape[1]),
+            (share, pair[0].shape[1] // 2),
+            (share, pair[0].shape[1] // 2),
+            (micro * rows, weight.shape[0]),
+        )
     ]
-    outs.append(jax.ShapeDtypeStruct((micro * rows, weight.shape[0]), jnp.float32))
     outs += [
         jax.ShapeDtypeStruct((micro,) + arrays[0].shape, jnp.bfloat16)
         for arrays in (branch, query, pair)
     ]
     return pl.pallas_call(
-        functools.partial(grad_sums_kernel, ring, micro, sizes),
+        functools.partial(grad_sums_kernel, ring, micro, head_dim, sizes),
         in_specs=[anywhere] * (4 * micro + 2),
-        out_specs=[pl.BlockSpec(memory_space=pltpu.VMEM)] * 3 + [anywhere] * 3,
+        out_specs=[pl.BlockSpec(memory_space=pltpu.VMEM)] * 5 + [anywhere] * 3,
         out_shape=outs,
         scratch_shapes=GradSums.scratch(ring, micro, sizes),
         compiler_params=pltpu.CompilerParams(
             vmem_limit_bytes=60 * 2**20, collective_id=number, has_side_effects=True
         ),
         cost_estimate=SMALL,
-    )(*attended, hidden, *branch, *query, *pair, weight)[:3]
+    )(*attended, hidden, *branch, *query, *pair, weight)[:5]
 
 
 def per_device(
@@ -1248,9 +1324,13 @@
         micro * local, 2 * pair_width
     )
     gain_row = q_gain[None, :]
-    both = line_gather(
-        *[pairs[step * local : (step + 1) * local] for step in range(micro)], number=3
-    )
+    both = list(line_gather(pairs[:local], number=3))
+    both += [
+        lax.all_gather(
+            after(pairs[step * local : (step + 1) * local], both[0]), "ctx", axis=0, tiled=True
+        )
+        for step in range(1, micro)
+    ]
     both = [gathered.reshape(ring, local, 2 * pair_width) for gathered in both]
     places, attended, middles, feeds, scales = [], [], [], [], []
     for step in range(micro):
@@ -1296,7 +1376,8 @@
     spare = -sums.shape[1] % 1024
     extra = jnp.pad(sums, ((0, 0), (0, spare))).reshape(plane, -1, 128)
 
-    branches, raw_grads, middle_grads, gain_list, results = [], [], [], [], []
+    branches, raw_grads, pair_grads = [], [], []
+    middle_grads, gain_list, results = [], [], []
     waits = ()
     for step in range(micro):
         if step > 0:
@@ -1308,17 +1389,18 @@
         )
         middle_grads.append(grads_low[step].astype(jnp.float32) + middle_norm_grad)
         branches.append(middle_grads[step].astype(jnp.bfloat16))
-        attended_grad = dot_t(branches[step], out_weight).astype(jnp.bfloat16)
         if step == 0:
-            returned[1] = after(returned[1], down_term, attended_grad)
+            returned[1] = after(returned[1], down_term, branches[0])
             part_sums = combine(returned[1], 1, False)
             feed_grad = scatter(part_sums)
             waits = (part_sums,)
-        raw_grad, pair_part, query_gain_part, result, extra = attend_back(
+        raw_grad, pair_grad, gain_part, result, extra = attend_back(
             raw,
-            attended_grad,
+            branches[step],
+            out_weight,
             both[step],
             gain_row,
+            k_gain[None, :],
             cosine,
             sine,
             places[step],
@@ -1338,26 +1420,11 @@
         waits = (result,)
         results.append(result)
         raw_grads.append(raw_grad)
-        gain_list.append([jnp.sum(second_gain, 0), query_gain_part[0], pair_part])
-    pair_grads = []
-    key_cos, key_sin = cosine[None], sine[None]
-    for step in range(micro):
-        part = slice(step * local, (step + 1) * local)
-        landed = jnp.sum(gain_list[step][2].astype(jnp.float32), 0).astype(jnp.bfloat16)
-        key_grad = landed[..., :head_dim].astype(jnp.float32)
-        key_turned = key_grad * key_cos - swap_halves(key_grad) * key_sin
-        key_raw_grad, key_gain_part = norm_back(
-            key_raw[part].transpose(1, 0, 2), key_scale[part].transpose(1, 0, 2), k_gain, key_turned
-        )
-        pair_grad = jnp.concatenate(
-            [key_raw_grad.astype(jnp.bfloat16), landed[..., head_dim:]], -1
-        )
-        pair_grads.append(pair_grad.transpose(1, 0, 2).reshape(local, 2 * pair_width))
-        gain_list[step][2] = jnp.sum(key_gain_part, (0, 1))
-
+        pair_grads.append(pair_grad)
+        gain_list.append((jnp.sum(second_gain, 0), gain_part[0], gain_part[1]))
     if plane == 8:
-        out_total, in_total, hidden_grad = grad_sums(
-            ring, attended, hidden_parts, branches, raw_grads, pair_grads, in_weight, 5
+        out_total, query_total, key_total, value_total, hidden_grad = grad_sums(
+            ring, head_dim, attended, hidden_parts, branches, raw_grads, pair_grads, in_weight, 5
         )
     else:
 
@@ -1376,8 +1443,10 @@
         )
         in_total = sum_over_devices(hidden, raw_grad)
         hidden_grad = dot_t(raw_grad, in_weight)
-    query_total = in_total[:, :query_width]
-    pair_total = in_total[:, query_width:].reshape(-1, kv_heads, 2, head_dim)
+        query_total = in_total[:, :query_width]
+        pair_total = in_total[:, query_width:].reshape(-1, kv_heads, 2, head_dim)
+        key_total = pair_total[:, :, 0].reshape(-1, pair_width)
+        value_total = pair_total[:, :, 1].reshape(-1, pair_width)
     first_grad, first_gain = norm_back(rows, first_scale, norm_attn, hidden_grad)
     tokens_grad = jnp.concatenate(middle_grads, 0) + first_grad
     gains = jnp.concatenate([jnp.sum(first_gain, 0)] + [sum(parts) for parts in zip(*gain_list)])
@@ -1405,8 +1474,8 @@
         tokens_grad.reshape(micro, 1, local, width),
         route_grads[:, None],
         query_total,
-        pair_total[:, :, 0].reshape(-1, pair_width),
-        pair_total[:, :, 1].reshape(-1, pair_width),
+        key_total,
+        value_total,
         out_total,
         gain_total,
         gate_term,

time: 1490 us -> 1450 us (0.973)
  waiting for transfers between devices: 276 us -> 318 us
  matrix products: 74 us -> 36.9 us
  Pallas kernels: 971 us -> 940 us
    dot_general x2 -> x0, matrix products: 36.9 us -> none  [dot_t(): return jnp.einsum('te,de->td', a, b, preferred_element_type=jnp.float32)]
    pallas_call x2, Pallas kernels: 220 us -> 186 us  [line_gather(): pl.pallas_call(functools.partial(gather_kernel, count, arrays, stacked),...]
    all_to_all x5, waiting for transfers between devices: 161 us -> 187 us  [exchange(): return lax.all_to_all(rows, 'exp', split_axis=0, concat_axis=0, tiled=True)]
  transfers between devices with their start and end apart: 14 -> 15, of which waited for: 6 -> 8; matrix products, arithmetic and copies ran while one was open for 11% -> 8% of each run, Pallas kernels for 64% -> 64%
where the time goes in v5:
time: 1450 us
  Pallas kernels  940 us (65%)
  waiting for transfers between devices  318 us (22%)
  other arithmetic  53.1 us (4%)
  local copies, waits for them, and re-layouts  52.2 us (4%)
  matrix products  36.9 us (3%)
  starting transfers between devices  31.8 us (2%)
  between operations  14.9 us (1%)
    pallas_call x2, Pallas kernels, attend_back(): pl.pallas_call(functools.partial(attend_back_kernel, per, steps, width **...  242 us
    pallas_call x1, Pallas kernels, grad_sums(): pl.pallas_call(functools.partial(grad_sums_kernel, ring, micro, head_dim,...  198 us
    all_to_all x5, waiting for transfers between devices, exchange(): return lax.all_to_all(rows, 'exp', split_axis=0, concat_axis=0, tiled=True)  187 us
    pallas_call x2, Pallas kernels, line_gather(): pl.pallas_call(functools.partial(gather_kernel, count, arrays, stacked),...  186 us
    all_gather x2, waiting for transfers between devices, per_device(): lax.all_gather(feed, 'ctx', axis=0, tiled=True)  118 us
    pallas_call x2, Pallas kernels, run_expert(): pl.pallas_call(expert_kernel, grid=(sources,), in_specs=[pl.BlockSpec((No...  115 us
    pallas_call x1, Pallas kernels, expert_weight_grads(): pl.pallas_call(functools.partial(weight_kernel, steps, micro), grid=(micr...  73.5 us
    pallas_call x2, Pallas kernels, attend(): pl.pallas_call(functools.partial(attend_kernel, per, width ** (-0.5) * ma...  47.5 us
  transfers between devices with their start and end apart: 15, of which 8 were waited for; matrix products, arithmetic and copies ran while one was open for 8% of the time, Pallas kernels for 64%

profile of v5, /device:TPU:0, one launch (start us, length us, event | category | flops | bytes accessed | tf_op | source)
XLA Modules:
  0.0 1447.6 jit_solution(6424755862393946632)
XLA Ops:
  12.9 3.3 pad_maximum_fusion
  19.3 145.2 %shard_map.239 = (bf16[2,1024,2048]{2,1,0:T(8,128)(2,1)}, f32[256,128]{1,0:T(8,128)}) custom-call(bf16[256,2048]{1,0:T(8,128)(2,1)} %get-tuple-element.147.refs_0_, bf16[256,2048]{1,0:T(8,128)(2,1)} %get-tuple-element.146.refs_1_, f32[64,128]{1,0:T(8,128)} %reshape.299.refs_2_), custom_call_target="tpu_custom_call" | custom-call | bytes 209715200 | tf_op jit(solution)/shard_map/pallas_call | solution.py:135
  170.1 22.6 %shard_map.240.refs_1_ = bf16[8,8,80,2048]{3,2,1,0:T(8,128)(2,1)} custom-call(s32[8,2,4,256]{3,2,1,0:T(4,128)} %reshape.301.place_ref, f32[8,2,4,256]{3,2,1,0:T(4,128)} %reshape.302.weight_ref, bf16[2048,2048]{1,0:T(8,128)(2,1)} %bitcast.187), custom_call_target="tpu_custom_call" | custom-call | flops 1048576 | bytes 1048576 | tf_op jit(solution)/shard_map/pallas_call | solution.py:263
  192.7 6.2 all-to-all-start
  202.4 14.8 %fusion.42.raw_ref.pair_raw_ref = f32[512,5120]{1,0:T(8,128)S(1)} fusion(bf16[512,2048]{1,0:T(8,128)(2,1)} %shard_map.241, bf16[2048,5120]{1,0:T(8,128)(2,1)} %all-gather.6.cloned.1.call-done.refs_9_), kind=kOutput, calls=%fused_computation.126 | convolution fusion | flops 10737418240 | bytes 33554432 | tf_op jit(solution)/shard_map/dot_general | solution.py:1237
  217.2 3.9 copy-done
  222.6 4.0 reshape.305
  226.5 2.5 slice.121
  232.2 5.0 fusion.25
  237.3 2.4 fusion.26
  240.9 40.7 %shard_map.242.refs_1_ = bf16[1024,1024]{1,0:T(8,128)(2,1)} custom-call(bf16[256,1024]{1,0:T(8,128)(2,1)} %slice.102.refs_0_), custom_call_target="tpu_custom_call" | custom-call | bytes 209715200 | tf_op jit(solution)/shard_map/pallas_call | solution.py:135
  283.3 2.5 convert_element_type.108
  288.3 23.6 %shard_map.243.refs_0_ = bf16[256,4096]{1,0:T(8,128)(2,1)} custom-call(s32[2]{0:T(128)} %get-tuple-element.175.place_ref, f32[512,5120]{1,0:T(8,128)} %copy-done, bf16[4,256,1024]{2,1,0:T(8,128)(2,1)} %bitcast.176, f32[1,128]{1,0:T(1,128)} %bitcast.219, f32[256,128]{1,0:T(8,128)} %copy-done.12, f32[256,128]{1,0:T(8,128)} %copy-done.13), custom_call_target="tpu_custom_call" | custom-call | flops 1048576 | bytes 1048576 | tf_op jit(solution)/shard_map/pallas_call | solution.py:647
  312.0 11.6 multiply_reduce_fusion.1
  326.3 11.6 all-gather.12.cloned.1.call-done
  337.9 23.9 %shard_map.245.refs_1_ = bf16[256,4096]{1,0:T(8,128)(2,1)} custom-call(s32[2]{0:T(128)} %get-tuple-element.176.place_ref, f32[512,5120]{1,0:T(8,128)} %copy-done, bf16[4,256,1024]{2,1,0:T(8,128)(2,1)} %bitcast.188, f32[1,128]{1,0:T(1,128)} %bitcast.220, f32[256,128]{1,0:T(8,128)} %copy-done.12, f32[256,128]{1,0:T(8,128)} %copy-done.13, ...), custom_call_target="tpu_custom_call" | custom-call | flops 1048576 | bytes 1048576 | tf_op jit(solution)/shard_map/pallas_call | solution.py:647
  361.8 8.9 multiply_reduce_fusion
  373.2 46.1 %all-gather.10.cloned.1.call-done.refs_0_ = bf16[1024,2048]{1,0:T(8,128)(2,1)} async-done(((bf16[256,2048]{1,0:T(8,128)(2,1)}), bf16[1024,2048]{1,0:T(8,128)(2,1)}) %all-gather.10.cloned.1.call-update) | async-done | bytes 4194320 | tf_op jit(solution)/shard_map/all_gather | solution.py:1346
  419.4 11.4 shard_map.247
  430.8 10.9 all-to-all-done
  441.6 5.1 all-to-all-start.1
  448.7 3.9 copy.112
  452.6 3.1 copy.113
  455.7 4.2 copy.114.refs_2_
  459.9 71.8 %all-gather.14.cloned.1.call-done.rows_ref = bf16[1024,2048]{1,0:T(8,128)(2,1)} async-done(((bf16[256,2048]{1,0:T(8,128)(2,1)}), bf16[1024,2048]{1,0:T(8,128)(2,1)}) %all-gather.14.cloned.1.call-update) | async-done | bytes 4194320 | tf_op jit(solution)/shard_map/all_gather | solution.py:1346
  531.7 11.4 shard_map.250
  543.1 20.2 %all-to-all-done.1.rows_ref.refs_1_.refs_0_ = bf16[8,320,2048]{2,1,0:T(8,128)(2,1)} async-done(((bf16[8,320,2048]{2,1,0:T(8,128)(2,1)}), bf16[8,320,2048]{2,1,0:T(8,128)(2,1)}, u32[]{:S(2)}, u32[]{:S(2)}) %all-to-all-start.1) | async-done | bytes 10485792 | tf_op jit(solution)/shard_map/all_to_all | solution.py:1274
  563.3 5.3 all-to-all-start.2
  568.7 57.6 %shard_map.249 = (bf16[2560,768]{1,0:T(8,128)(2,1)}, bf16[2560,768]{1,0:T(8,128)(2,1)}, bf16[2560,768]{1,0:T(8,128)(2,1)}, bf16[2560,2048]{1,0:T(8,128)(2,1)}, b...) custom-call(bf16[8,320,2048]{2,1,0:T(8,128)(2,1)} %all-to-all-done.1.rows_ref.refs_1_.refs_0_, ...), custom_call_target="tpu_custom_call" | custom-call | flops 1048576 | bytes 1048576 | tf_op jit(solution)/shard_map/pallas_call | solution.py:193
  626.3 58.9 %all-to-all-done.2.refs_1_.rows_ref = bf16[8,320,2048]{2,1,0:T(8,128)(2,1)} async-done(((bf16[8,320,2048]{2,1,0:T(8,128)(2,1)}), bf16[8,320,2048]{2,1,0:T(8,128)(2,1)}, u32[]{:S(2)}, u32[]{:S(2)}) %all-to-all-start.2) | async-done | bytes 10485792 | tf_op jit(solution)/shard_map/all_to_all | solution.py:1274
  685.2 5.1 all-to-all-start.3
  690.4 57.6 %shard_map.253 = (bf16[2560,768]{1,0:T(8,128)(2,1)}, bf16[2560,768]{1,0:T(8,128)(2,1)}, bf16[2560,768]{1,0:T(8,128)(2,1)}, bf16[2560,2048]{1,0:T(8,128)(2,1)}, b...) custom-call(bf16[8,320,2048]{2,1,0:T(8,128)(2,1)} %all-to-all-done.2.refs_1_.rows_ref, ...), custom_call_target="tpu_custom_call" | custom-call | flops 1048576 | bytes 1048576 | tf_op jit(solution)/shard_map/pallas_call | solution.py:193
  748.0 58.9 %all-to-all-done.3.refs_0_.refs_1_ = bf16[8,320,2048]{2,1,0:T(8,128)(2,1)} async-done(((bf16[8,320,2048]{2,1,0:T(8,128)(2,1)}), bf16[8,320,2048]{2,1,0:T(8,128)(2,1)}, u32[]{:S(2)}, u32[]{:S(2)}) %all-to-all-start.3) | async-done | bytes 10485792 | tf_op jit(solution)/shard_map/all_to_all | solution.py:1274
  806.9 8.3 shard_map.255
  815.3 5.2 all-to-all-start.4
  820.5 73.5 %shard_map.257 = (f32[1,2048,768]{2,1,0:T(8,128)}, f32[1,2048,768]{2,1,0:T(8,128)}, f32[1,768,2048]{2,1,0:T(8,128)}) custom-call(bf16[8,320,2048]{2,1,0:T(8,128)(2,1)} %all-to-all-done.1.rows_ref.refs_1_.refs_0_, bf16[8,320,2048]{2,1,0:T(8,128)(2,1)} %all-to-all-done.2.refs_1_.rows_ref, bf16[8,2,320,2048]{3,2,1,0:T(8,128)(2,1)} %bitcast.31.refs_1_.grad_ref.refs_2_, ...), custom_call_target="tpu_custom_call" | custom-call | flops 1048576 | bytes 1048576 | tf_op jit(solution)/shard_map/pallas_call | solution.py:343
  896.1 2.4 fusion.38
  898.5 38.4 %all-to-all-done.4.refs_0_ = bf16[8,320,2048]{2,1,0:T(8,128)(2,1)} async-done(((bf16[8,320,2048]{2,1,0:T(8,128)(2,1)}), bf16[8,320,2048]{2,1,0:T(8,128)(2,1)}, u32[]{:S(2)}, u32[]{:S(2)}) %all-to-all-start.4) | async-done | bytes 10485792 | tf_op jit(solution)/shard_map/all_to_all | solution.py:1274
  937.0 8.3 shard_map.259.refs_1_
  948.3 121.7 %shard_map.261 = (bf16[256,4096]{1,0:T(8,128)(2,1)}, bf16[256,1024]{1,0:T(8,128)(2,1)}, f32[8,128]{1,0:T(8,128)}, bf16[8,320,2048]{2,1,0:T(8,128)(2,1)}, f32[8,8,128]{2,1,0:T(8,128)}) custom-call(s32[2]{0:T(128)} %get-tuple-element.175.place_ref, f32[512,5120]{1,0:T(8,128)} %copy-done, bf16[256,2048]{1,0:T(8,128)(2,1)} %get-tuple-element.142.refs_2_.branch_ref.refs_3_, ...), custom_call_target="tpu_custom_call" | custom-call | flops 1048576 | bytes 1048576 | tf_op jit(solution)/shard_map/pallas_call | solution.py:687
  1070.0 8.3 shard_map.262
  1085.8 2.4 fusion.36
  1088.2 120.3 %shard_map.265 = (bf16[256,4096]{1,0:T(8,128)(2,1)}, bf16[256,1024]{1,0:T(8,128)(2,1)}, f32[8,128]{1,0:T(8,128)}, bf16[8,320,2048]{2,1,0:T(8,128)(2,1)}, f32[4,32,128]{2,1,0:T(8,128)}) custom-call(s32[2]{0:T(128)} %get-tuple-element.176.place_ref, f32[512,5120]{1,0:T(8,128)} %copy-done, bf16[256,2048]{1,0:T(8,128)(2,1)} %get-tuple-element.140.branch_ref.refs_4_, ...), custom_call_target="tpu_custom_call" | custom-call | flops 1048576 | bytes 1048576 | tf_op jit(solution)/shard_map/pallas_call | solution.py:687
  1208.5 8.4 shard_map.266
  1217.6 197.6 %shard_map.267 = (f32[128,2048]{1,0:T(8,128)}, f32[64,4096]{1,0:T(8,128)}, f32[64,512]{1,0:T(8,128)}, f32[64,512]{1,0:T(8,128)}, f32[512,2048]{1,0:T(8,128)}, /*...) custom-call(bf16[256,4096]{1,0:T(8,128)(2,1)} %shard_map.243.refs_0_, ...), custom_call_target="tpu_custom_call" | custom-call | flops 1048576 | bytes 1048576 | tf_op jit(solution)/shard_map/pallas_call | solution.py:1186
  1416.0 3.5 fusion.7
  1420.2 3.8 all-to-all-start.5
  1427.4 5.3 maximum_add_fusion
  (228 shorter events, 60.7 us)
Async XLA Ops:
  7.2 195.2 %all-gather.6.cloned.1.call-start = ((), (), s32[]{:S(2)}) async-start(), calls=%async_computation.10 | async-start | bytes 23592960 | tf_op jit(solution)/shard_map/all_gather | solution.py:1251
  16.2 1.7 copy-start.9
  16.2 295.8 %all-gather.8.cloned.1.call-start = ((), (), s32[]{:S(2)}) async-start(), calls=%async_computation.11 | async-start | bytes 18874368 | tf_op jit(solution)/shard_map/all_gather | solution.py:1254
  167.0 158.1 %copy-start.21 = (f32[4,256,8]{1,2,0:T(8,128)}, f32[4,256,8]{1,2,0:T(8,128)S(1)}, u32[]{:S(2)}) copy-start(f32[4,256,8]{1,2,0:T(8,128)S(1)} %get-tuple-element.136) | copy-start | bytes 98308
  167.0 280.4 %copy-start.20 = (f32[4,256,8]{1,2,0:T(8,128)}, f32[4,256,8]{1,2,0:T(8,128)S(1)}, u32[]{:S(2)}) copy-start(f32[4,256,8]{1,2,0:T(8,128)S(1)} %get-tuple-element.137) | copy-start | bytes 98308
  167.8 24.9 %copy-start.36 = (pred[4,256,8]{1,2,0:T(8,128)(4,1)}, pred[4,256,8]{1,2,0:T(8,128)(4,1)S(1)}, u32[]{:S(2)}) copy-start(pred[4,256,8]{1,2,0:T(8,128)(4,1)S(1)} %get-tuple-element.139) | copy-start | bytes 24580
  167.8 24.9 %copy-start.38 = (pred[4,256,8]{1,2,0:T(8,128)(4,1)}, pred[4,256,8]{1,2,0:T(8,128)(4,1)S(1)}, u32[]{:S(2)}) copy-start(pred[4,256,8]{1,2,0:T(8,128)(4,1)S(1)} %get-tuple-element.138) | copy-start | bytes 24580
  168.6 279.4 %copy-start.22 = (s32[4,8,256]{2,1,0:T(8,128)}, s32[4,8,256]{2,1,0:T(8,128)S(1)}, u32[]{:S(2)}) copy-start(s32[4,8,256]{2,1,0:T(8,128)S(1)} %get-tuple-element.167.place_ref) | copy-start | bytes 98308
  169.4 156.3 %copy-start.23 = (s32[4,8,256]{2,1,0:T(8,128)}, s32[4,8,256]{2,1,0:T(8,128)S(1)}, u32[]{:S(2)}) copy-start(s32[4,8,256]{2,1,0:T(8,128)S(1)} %get-tuple-element.169.place_ref) | copy-start | bytes 98308
  192.7 6.5 copy-start.1
  192.7 249.0 %all-to-all-start = ((bf16[8,640,2048]{2,1,0:T(8,128)(2,1)}), bf16[8,640,2048]{2,1,0:T(8,128)(2,1)}, u32[]{:S(2)}, u32[]{:S(2)}) async-start(bf16[8,640,2048]{2,1,0:T(8,128)(2,1)} %bitcast.168), calls=%async_computation | async-start | bytes 41943040 | tf_op jit(solution)/shard_map/all_to_all | solution.py:1274
  199.0 139.0 %all-gather.12.cloned.1.call-start = ((), (), s32[]{:S(2)}) async-start(), calls=%async_computation.13 | async-start | bytes 2621440 | tf_op jit(solution)/shard_map/all_gather | solution.py:1329
  199.7 1.9 copy-start.34
  202.3 29.8 %copy-start.12 = (f32[256,128]{1,0:T(8,128)}, f32[256,128]{1,0:T(8,128)S(1)}, u32[]{:S(2)}) copy-start(f32[256,128]{1,0:T(8,128)S(1)} %get-tuple-element.177.cos_ref) | copy-start | bytes 393220
  202.3 29.8 %copy-start.13 = (f32[256,128]{1,0:T(8,128)}, f32[256,128]{1,0:T(8,128)S(1)}, u32[]{:S(2)}) copy-start(f32[256,128]{1,0:T(8,128)S(1)} %get-tuple-element.178.sin_ref) | copy-start | bytes 393220
  217.2 3.9 copy-start
  226.5 2.5 copy-start.7
  229.0 1.8 copy-start.45
  282.8 3.0 copy-start.47
  282.8 136.5 %all-gather.10.cloned.1.call-start = ((), (), s32[]{:S(2)}) async-start(), calls=%async_computation.12 | async-start | bytes 5242880 | tf_op jit(solution)/shard_map/all_gather | solution.py:1346
  311.9 11.7 copy-start.24
  323.6 572.4 %copy-start.5 = (f32[256,2048]{1,0:T(8,128)}, f32[256,2048]{1,0:T(8,128)S(1)}, u32[]{:S(2)}) copy-start(f32[256,2048]{1,0:T(8,128)S(1)} %get-tuple-element.172) | copy-start | bytes 6291460
  337.9 23.9 %copy-start.14 = (f32[2,1,256,2048]{3,2,1,0:T(8,128)S(1)}, f32[2,1,256,2048]{3,2,1,0:T(8,128)}, u32[]{:S(2)}) copy-start(f32[2,1,256,2048]{3,2,1,0:T(8,128)} %convert_element_type.108) | copy-start | bytes 12582916
  371.3 48.1 %copy-start.43 = (f32[256]{0:T(256)}, f32[256]{0:T(256)S(1)}, u32[]{:S(2)}) copy-start(f32[256]{0:T(256)S(1)} %get-tuple-element.162) | copy-start | bytes 3076
  441.6 121.7 %all-to-all-start.1 = ((bf16[8,320,2048]{2,1,0:T(8,128)(2,1)}), bf16[8,320,2048]{2,1,0:T(8,128)(2,1)}, u32[]{:S(2)}, u32[]{:S(2)}) async-start(bf16[8,320,2048]{2,1,0:T(8,128)(2,1)} %shard_map.248), calls=%async_computation.1 | async-start | bytes 20971520 | tf_op jit(solution)/shard_map/all_to_all | solution.py:1274
  446.8 84.9 %all-gather.14.cloned.1.call-start = ((), (), s32[]{:S(2)}) async-start(), calls=%async_computation.14 | async-start | bytes 5242880 | tf_op jit(solution)/shard_map/all_gather | solution.py:1346
  563.3 121.9 %all-to-all-start.2 = ((bf16[8,320,2048]{2,1,0:T(8,128)(2,1)}), bf16[8,320,2048]{2,1,0:T(8,128)(2,1)}, u32[]{:S(2)}, u32[]{:S(2)}) async-start(bf16[8,320,2048]{2,1,0:T(8,128)(2,1)} %shard_map.251), calls=%async_computation.2 | async-start | bytes 20971520 | tf_op jit(solution)/shard_map/all_to_all | solution.py:1274
  685.2 121.7 %all-to-all-start.3 = ((bf16[8,320,2048]{2,1,0:T(8,128)(2,1)}), bf16[8,320,2048]{2,1,0:T(8,128)(2,1)}, u32[]{:S(2)}, u32[]{:S(2)}) async-start(bf16[8,320,2048]{2,1,0:T(8,128)(2,1)} %shard_map.252), calls=%async_computation.3 | async-start | bytes 20971520 | tf_op jit(solution)/shard_map/all_to_all | solution.py:1274
  690.4 203.6 %reduce-scatter.5.cloned.1.call-start = ((), (), s32[]{:S(2)}) async-start(), calls=%async_computation.15 | async-start | bytes 5242880 | tf_op jit(solution)/shard_map/reduce_scatter | solution.py:1296
  815.3 121.7 %all-to-all-start.4 = ((bf16[8,320,2048]{2,1,0:T(8,128)(2,1)}), bf16[8,320,2048]{2,1,0:T(8,128)(2,1)}, u32[]{:S(2)}, u32[]{:S(2)}) async-start(bf16[8,320,2048]{2,1,0:T(8,128)(2,1)} %shard_map.256), calls=%async_computation.5 | async-start | bytes 20971520 | tf_op jit(solution)/shard_map/all_to_all | solution.py:1274
  820.4 261.3 %reduce-scatter.9.cloned.1.call-start = ((), (), s32[]{:S(2)}) async-start(), calls=%async_computation.17 | async-start | bytes 5242880 | tf_op jit(solution)/shard_map/reduce_scatter | solution.py:1296
  894.0 2.1 copy-start.10
  894.0 2.2 copy-start.15
  945.3 1.8 copy-start.17
  945.3 478.9 %reduce-scatter.7.cloned.1.call-start = ((), (), s32[]{:S(2)}) async-start(), calls=%async_computation.16 | async-start | bytes 5242880 | tf_op jit(solution)/shard_map/reduce_scatter | solution.py:1296
  1078.4 355.5 %reduce-scatter.11.cloned.1.call-start = ((), (), s32[]{:S(2)}) async-start(), calls=%async_computation.18 | async-start | bytes 5242880 | tf_op jit(solution)/shard_map/reduce_scatter | solution.py:1296
  1081.7 1.7 copy-start.44
  1083.4 2.1 copy-start.8
  1083.4 2.4 copy-start.11
  1083.4 2.4 copy-start.46
  1217.6 198.3 %copy-start.2 = (bf16[2,1,256,2048]{3,2,1,0:T(8,128)(2,1)S(1)}, bf16[2,1,256,2048]{3,2,1,0:T(8,128)(2,1)}, u32[]{:S(2)}) copy-start(bf16[2,1,256,2048]{3,2,1,0:T(8,128)(2,1)} %param.16) | copy-start | bytes 6291460
  1217.6 198.3 %copy-start.28 = (f32[2048]{0:T(1024)S(1)}, f32[2048]{0:T(1024)}, u32[]{:S(2)}) copy-start(f32[2048]{0:T(1024)} %param.20) | copy-start | bytes 24580
  1416.0 8.1 copy-start.29
  1416.0 8.1 copy-start.33
  1420.2 13.1 all-to-all-start.5
  1424.2 3.1 copy-start.6
  1427.4 5.4 copy-start.31
  1437.6 2.3 copy-start.18
  (15 other events, 15.5 us)
Sparse Core Ops, SparseCore 0:
  16.3 110.2 all-gather.5
  128.5 103.7 all-gather.7
  282.9 54.9 all-gather.11
  339.9 79.3 all-gather.9
  449.5 82.1 all-gather.13
  815.4 75.9 reduce-scatter.4
  945.4 110.1 reduce-scatter.8
  1078.5 109.6 reduce-scatter.6
  1217.1 106.1 reduce-scatter.10

commit v6 on v5

--- a/solution.py
+++ b/solution.py
@@ -11,7 +11,7 @@
 EPSILON = 1e-06
 ROPE_BASE = 1000000.0
 MASKED = -1e30
-LAGS = (2, 3, 5)
+LAGS = (2, 3, 8)
 VMEM_BYTES = 56 * 2**20
 SMALL = pl.CostEstimate(flops=2**20, bytes_accessed=2**20, transcendentals=0)
 
@@ -527,7 +527,10 @@
     extra_axis,
     place_ref,
     raw_ref,
-    branch_ref,
+    feed_grad_ref,
+    middle_ref,
+    out_grad_ref,
+    norm_ref,
     weight_ref,
     both_ref,
     pair_raw_ref,
@@ -540,6 +543,9 @@
     raw_grad_ref,
     pair_grad_ref,
     gain_grad_ref,
+    branch_ref,
+    middle_grad_ref,
+    norm_grad_ref,
     moved_ref,
     extra_moved_ref,
     mask_ref,
@@ -562,6 +568,17 @@
         extra_moving.begin()
         fill_mask(place_ref, mask_ref)
         gain_grad_ref[...] = jnp.zeros_like(gain_grad_ref)
+        norm_grad_ref[...] = jnp.zeros_like(norm_grad_ref)
+        rows = middle_ref.shape[0]
+        for at in range(0, rows, 64):
+            part = slice(at, at + 64)
+            value, grad = middle_ref[part, :], feed_grad_ref[part, :].astype(jnp.float32)
+            norm = lax.rsqrt(jnp.mean(value * value, -1, keepdims=True) + EPSILON)
+            first, gain_part = norm_back(value, norm, norm_ref[...], grad)
+            total = out_grad_ref[part, :].astype(jnp.float32) + first
+            middle_grad_ref[part, :] = total
+            branch_ref[part, :] = total.astype(jnp.bfloat16)
+            norm_grad_ref[0:1, :] += jnp.sum(gain_part, 0, keepdims=True)
 
     @pl.when(step == 0)
     def _():
@@ -662,7 +679,10 @@
 
 def attend_back(
     raw,
-    branch,
+    feed_grad,
+    middle,
+    out_grad,
+    norm,
     weight,
     both,
     gain,
@@ -699,7 +719,10 @@
         in_specs=[
             specs["place"],
             specs["raw"],
-            pl.BlockSpec(branch.shape, lambda g, j: (0, 0)),
+            pl.BlockSpec(middle.shape, lambda g, j: (0, 0)),
+            pl.BlockSpec(middle.shape, lambda g, j: (0, 0)),
+            pl.BlockSpec(middle.shape, lambda g, j: (0, 0)),
+            pl.BlockSpec(norm.shape, lambda g, j: (0, 0)),
             pl.BlockSpec((per * width, weight.shape[1]), lambda g, j: (g * steps + j, 0)),
             specs["both"],
             pl.BlockSpec((rows, pairs), lambda g, j: (step, pair_place)),
@@ -714,6 +737,9 @@
             specs["heads"],
             pl.BlockSpec((rows, pairs), lambda g, j: (0, 0)),
             pl.BlockSpec((8, width), lambda g, j: (0, 0)),
+            pl.BlockSpec(middle.shape, lambda g, j: (0, 0)),
+            pl.BlockSpec(middle.shape, lambda g, j: (0, 0)),
+            pl.BlockSpec((8, middle.shape[1]), lambda g, j: (0, 0)),
             anywhere,
             anywhere,
         ),
@@ -721,6 +747,9 @@
             jax.ShapeDtypeStruct((rows, heads * width), jnp.bfloat16),
             jax.ShapeDtypeStruct((rows, pairs), jnp.bfloat16),
             jax.ShapeDtypeStruct((8, width), jnp.float32),
+            jax.ShapeDtypeStruct(middle.shape, jnp.bfloat16),
+            jax.ShapeDtypeStruct(middle.shape, jnp.float32),
+            jax.ShapeDtypeStruct((8, middle.shape[1]), jnp.float32),
             jax.ShapeDtypeStruct(rows_out.shape, rows_out.dtype),
             jax.ShapeDtypeStruct(extra.shape, extra.dtype),
         ),
@@ -741,7 +770,10 @@
     )(
         place,
         raw,
-        branch,
+        feed_grad,
+        middle,
+        out_grad,
+        norm,
         weight,
         both,
         raw,
@@ -1381,22 +1413,20 @@
     waits = ()
     for step in range(micro):
         if step > 0:
-            feed_grad = after(feed_grad, *waits)
+            own_feed_grad = after(feed_grad, *waits)
         else:
-            feed_grad = scatter(combine(after(returned[0], active[-1]), 0, False))
-        middle_norm_grad, second_gain = norm_back(
-            middles[step], scales[step], norm_ffn, feed_grad.astype(jnp.float32)
-        )
-        middle_grads.append(grads_low[step].astype(jnp.float32) + middle_norm_grad)
-        branches.append(middle_grads[step].astype(jnp.bfloat16))
+            own_feed_grad = scatter(combine(after(returned[0], active[-1]), 0, False))
         if step == 0:
-            returned[1] = after(returned[1], down_term, branches[0])
+            returned[1] = after(returned[1], down_term)
             part_sums = combine(returned[1], 1, False)
             feed_grad = scatter(part_sums)
             waits = (part_sums,)
-        raw_grad, pair_grad, gain_part, result, extra = attend_back(
+        raw_grad, pair_grad, gain_part, branch, middle_grad, norm_part, result, extra = attend_back(
             raw,
-            branches[step],
+            own_feed_grad,
+            middles[step],
+            grads_low[step],
+            norm_ffn[None, :],
             out_weight,
             both[step],
             gain_row,
@@ -1421,7 +1451,9 @@
         results.append(result)
         raw_grads.append(raw_grad)
         pair_grads.append(pair_grad)
-        gain_list.append((jnp.sum(second_gain, 0), gain_part[0], gain_part[1]))
+        branches.append(branch)
+        middle_grads.append(middle_grad)
+        gain_list.append((norm_part[0], gain_part[0], gain_part[1]))
     if plane == 8:
         out_total, query_total, key_total, value_total, hidden_grad = grad_sums(
             ring, head_dim, attended, hidden_parts, branches, raw_grads, pair_grads, in_weight, 5

time: 1450 us -> 1430 us (0.986)
  transfers between devices with their start and end apart: 15 -> 15, of which waited for: 8 -> 8; matrix products, arithmetic and copies ran while one was open for 8% -> 7% of each run, Pallas kernels for 64% -> 65%
where the time goes in v6:
time: 1430 us
  Pallas kernels  932 us (65%)
  waiting for transfers between devices  316 us (22%)
  local copies, waits for them, and re-layouts  48.9 us (3%)
  other arithmetic  44.2 us (3%)
  matrix products  36.9 us (3%)
  starting transfers between devices  33.7 us (2%)
  between operations  14.9 us (1%)
    pallas_call x2, Pallas kernels, attend_back(): pl.pallas_call(functools.partial(attend_back_kernel, per, steps, width **...  247 us
    pallas_call x2, Pallas kernels, line_gather(): pl.pallas_call(functools.partial(gather_kernel, count, arrays, stacked),...  187 us
    pallas_call x1, Pallas kernels, grad_sums(): pl.pallas_call(functools.partial(grad_sums_kernel, ring, micro, head_dim,...  184 us
    all_to_all x5, waiting for transfers between devices, exchange(): return lax.all_to_all(rows, 'exp', split_axis=0, concat_axis=0, tiled=True)  183 us
    all_gather x2, waiting for transfers between devices, per_device(): lax.all_gather(feed, 'ctx', axis=0, tiled=True)  123 us
    pallas_call x2, Pallas kernels, run_expert(): pl.pallas_call(expert_kernel, grid=(sources,), in_specs=[pl.BlockSpec((No...  115 us
    pallas_call x1, Pallas kernels, expert_weight_grads(): pl.pallas_call(functools.partial(weight_kernel, steps, micro), grid=(micr...  73.3 us
    pallas_call x2, Pallas kernels, attend(): pl.pallas_call(functools.partial(attend_kernel, per, width ** (-0.5) * ma...  47.4 us
  transfers between devices with their start and end apart: 15, of which 8 were waited for; matrix products, arithmetic and copies ran while one was open for 7% of the time, Pallas kernels for 65%

profile of v6, /device:TPU:0, one launch (start us, length us, event | category | flops | bytes accessed | tf_op | source)
XLA Modules:
  0.0 1426.6 jit_solution(5650587741956730797)
XLA Ops:
  12.9 3.3 pad_maximum_fusion
  19.4 145.2 %shard_map.239 = (bf16[2,1024,2048]{2,1,0:T(8,128)(2,1)}, f32[256,128]{1,0:T(8,128)}) custom-call(bf16[256,2048]{1,0:T(8,128)(2,1)} %get-tuple-element.151.refs_0_.out_grad_ref, bf16[256,2048]{1,0:T(8,128)(2,1)} %get-tuple-element.150.refs_1_.out_grad_ref, f32[64,128]{1,0:T(8,128)} %reshape.280.refs_2_), custom_call_target="tpu_custom_call" | custom-call | bytes 209715200 | tf_op jit(solution)/shard_map/pallas_call | solution.py:135
  170.1 22.6 %shard_map.240.refs_1_ = bf16[8,8,80,2048]{3,2,1,0:T(8,128)(2,1)} custom-call(s32[8,2,4,256]{3,2,1,0:T(4,128)} %reshape.282.place_ref, f32[8,2,4,256]{3,2,1,0:T(4,128)} %reshape.283.weight_ref, bf16[2048,2048]{1,0:T(8,128)(2,1)} %bitcast.183), custom_call_target="tpu_custom_call" | custom-call | flops 1048576 | bytes 1048576 | tf_op jit(solution)/shard_map/pallas_call | solution.py:263
  192.8 6.3 all-to-all-start
  202.5 14.8 %fusion.24.raw_ref.pair_raw_ref = f32[512,5120]{1,0:T(8,128)S(1)} fusion(bf16[512,2048]{1,0:T(8,128)(2,1)} %shard_map.241, bf16[2048,5120]{1,0:T(8,128)(2,1)} %all-gather.6.cloned.1.call-done.refs_9_), kind=kOutput, calls=%fused_computation.103 | convolution fusion | flops 10737418240 | bytes 33554432 | tf_op jit(solution)/shard_map/dot_general | solution.py:1269
  217.2 3.9 copy-done
  222.6 4.0 reshape.286
  226.6 2.3 slice.129
  229.0 2.7 slice.171
  233.8 5.0 fusion.11
  238.8 2.4 fusion.12
  242.4 41.7 %shard_map.242.refs_1_ = bf16[1024,1024]{1,0:T(8,128)(2,1)} custom-call(bf16[256,1024]{1,0:T(8,128)(2,1)} %slice.108.refs_0_), custom_call_target="tpu_custom_call" | custom-call | bytes 209715200 | tf_op jit(solution)/shard_map/pallas_call | solution.py:135
  285.8 2.5 convert_element_type.90
  290.9 23.6 %shard_map.243.refs_0_ = bf16[256,4096]{1,0:T(8,128)(2,1)} custom-call(s32[2]{0:T(128)} %get-tuple-element.175.place_ref, f32[512,5120]{1,0:T(8,128)} %copy-done, bf16[4,256,1024]{2,1,0:T(8,128)(2,1)} %bitcast.172, f32[1,128]{1,0:T(1,128)} %bitcast.218, f32[256,128]{1,0:T(8,128)} %copy-done.8, f32[256,128]{1,0:T(8,128)} %copy-done.9), custom_call_target="tpu_custom_call" | custom-call | flops 1048576 | bytes 1048576 | tf_op jit(solution)/shard_map/pallas_call | solution.py:664
  314.5 11.6 multiply_reduce_fusion.1
  330.0 8.0 all-gather.12.cloned.1.call-done
  338.0 23.8 %shard_map.245.refs_1_ = bf16[256,4096]{1,0:T(8,128)(2,1)} custom-call(s32[2]{0:T(128)} %get-tuple-element.176.place_ref, f32[512,5120]{1,0:T(8,128)} %copy-done, bf16[4,256,1024]{2,1,0:T(8,128)(2,1)} %bitcast.184, f32[1,128]{1,0:T(1,128)} %bitcast.219, f32[256,128]{1,0:T(8,128)} %copy-done.8, f32[256,128]{1,0:T(8,128)} %copy-done.9, ...), custom_call_target="tpu_custom_call" | custom-call | flops 1048576 | bytes 1048576 | tf_op jit(solution)/shard_map/pallas_call | solution.py:664
  361.8 8.9 multiply_reduce_fusion
  373.2 46.6 %all-gather.10.cloned.1.call-done.refs_0_ = bf16[1024,2048]{1,0:T(8,128)(2,1)} async-done(((bf16[256,2048]{1,0:T(8,128)(2,1)}), bf16[1024,2048]{1,0:T(8,128)(2,1)}) %all-gather.10.cloned.1.call-update) | async-done | bytes 4194320 | tf_op jit(solution)/shard_map/all_gather | solution.py:1378
  419.8 11.3 shard_map.247
  431.1 10.6 all-to-all-done
  441.7 5.3 all-to-all-start.1
  448.8 2.5 copy.112
  453.1 2.3 copy.114.refs_2_
  455.4 76.5 %all-gather.14.cloned.1.call-done.rows_ref = bf16[1024,2048]{1,0:T(8,128)(2,1)} async-done(((bf16[256,2048]{1,0:T(8,128)(2,1)}), bf16[1024,2048]{1,0:T(8,128)(2,1)}) %all-gather.14.cloned.1.call-update) | async-done | bytes 4194320 | tf_op jit(solution)/shard_map/all_gather | solution.py:1378
  531.9 11.4 shard_map.250
  543.3 20.2 %all-to-all-done.1.rows_ref.refs_1_.refs_0_ = bf16[8,320,2048]{2,1,0:T(8,128)(2,1)} async-done(((bf16[8,320,2048]{2,1,0:T(8,128)(2,1)}), bf16[8,320,2048]{2,1,0:T(8,128)(2,1)}, u32[]{:S(2)}, u32[]{:S(2)}) %all-to-all-start.1) | async-done | bytes 10485792 | tf_op jit(solution)/shard_map/all_to_all | solution.py:1306
  563.5 5.3 all-to-all-start.2
  568.8 57.5 %shard_map.249 = (bf16[2560,768]{1,0:T(8,128)(2,1)}, bf16[2560,768]{1,0:T(8,128)(2,1)}, bf16[2560,768]{1,0:T(8,128)(2,1)}, bf16[2560,2048]{1,0:T(8,128)(2,1)}, b...) custom-call(bf16[8,320,2048]{2,1,0:T(8,128)(2,1)} %all-to-all-done.1.rows_ref.refs_1_.refs_0_, ...), custom_call_target="tpu_custom_call" | custom-call | flops 1048576 | bytes 1048576 | tf_op jit(solution)/shard_map/pallas_call | solution.py:193
  626.4 59.0 %all-to-all-done.2.refs_1_.rows_ref = bf16[8,320,2048]{2,1,0:T(8,128)(2,1)} async-done(((bf16[8,320,2048]{2,1,0:T(8,128)(2,1)}), bf16[8,320,2048]{2,1,0:T(8,128)(2,1)}, u32[]{:S(2)}, u32[]{:S(2)}) %all-to-all-start.2) | async-done | bytes 10485792 | tf_op jit(solution)/shard_map/all_to_all | solution.py:1306
  685.4 5.2 all-to-all-start.3
  690.5 57.6 %shard_map.253 = (bf16[2560,768]{1,0:T(8,128)(2,1)}, bf16[2560,768]{1,0:T(8,128)(2,1)}, bf16[2560,768]{1,0:T(8,128)(2,1)}, bf16[2560,2048]{1,0:T(8,128)(2,1)}, b...) custom-call(bf16[8,320,2048]{2,1,0:T(8,128)(2,1)} %all-to-all-done.2.refs_1_.rows_ref, ...), custom_call_target="tpu_custom_call" | custom-call | flops 1048576 | bytes 1048576 | tf_op jit(solution)/shard_map/pallas_call | solution.py:193
  748.2 58.9 %all-to-all-done.3.refs_0_.refs_1_ = bf16[8,320,2048]{2,1,0:T(8,128)(2,1)} async-done(((bf16[8,320,2048]{2,1,0:T(8,128)(2,1)}), bf16[8,320,2048]{2,1,0:T(8,128)(2,1)}, u32[]{:S(2)}, u32[]{:S(2)}) %all-to-all-start.3) | async-done | bytes 10485792 | tf_op jit(solution)/shard_map/all_to_all | solution.py:1306
  807.1 5.2 all-to-all-start.4
  812.3 8.4 shard_map.255
  820.8 73.3 %shard_map.257 = (f32[1,2048,768]{2,1,0:T(8,128)}, f32[1,2048,768]{2,1,0:T(8,128)}, f32[1,768,2048]{2,1,0:T(8,128)}) custom-call(bf16[8,320,2048]{2,1,0:T(8,128)(2,1)} %all-to-all-done.1.rows_ref.refs_1_.refs_0_, bf16[8,320,2048]{2,1,0:T(8,128)(2,1)} %all-to-all-done.2.refs_1_.rows_ref, bf16[8,2,320,2048]{3,2,1,0:T(8,128)(2,1)} %bitcast.31.refs_1_.grad_ref.refs_2_, ...), custom_call_target="tpu_custom_call" | custom-call | flops 1048576 | bytes 1048576 | tf_op jit(solution)/shard_map/pallas_call | solution.py:343
  894.1 34.7 %all-to-all-done.4.refs_0_ = bf16[8,320,2048]{2,1,0:T(8,128)(2,1)} async-done(((bf16[8,320,2048]{2,1,0:T(8,128)(2,1)}), bf16[8,320,2048]{2,1,0:T(8,128)(2,1)}, u32[]{:S(2)}, u32[]{:S(2)}) %all-to-all-start.4) | async-done | bytes 10485792 | tf_op jit(solution)/shard_map/all_to_all | solution.py:1306
  928.8 8.3 shard_map.259.refs_1_
  940.2 123.7 %shard_map.261 = (bf16[256,4096]{1,0:T(8,128)(2,1)}, bf16[256,1024]{1,0:T(8,128)(2,1)}, f32[8,128]{1,0:T(8,128)}, bf16[256,2048]{1,0:T(8,128)(2,1)}, f32[256,204...) custom-call(s32[2]{0:T(128)} %get-tuple-element.175.place_ref, ...), custom_call_target="tpu_custom_call" | custom-call | flops 1048576 | bytes 1048576 | tf_op jit(solution)/shard_map/pallas_call | solution.py:707
  1063.9 8.4 shard_map.262
  1075.6 123.3 %shard_map.265 = (bf16[256,4096]{1,0:T(8,128)(2,1)}, bf16[256,1024]{1,0:T(8,128)(2,1)}, f32[8,128]{1,0:T(8,128)}, bf16[256,2048]{1,0:T(8,128)(2,1)}, f32[256,204...) custom-call(s32[2]{0:T(128)} %get-tuple-element.176.place_ref, ...), custom_call_target="tpu_custom_call" | custom-call | flops 1048576 | bytes 1048576 | tf_op jit(solution)/shard_map/pallas_call | solution.py:707
  1198.8 8.4 shard_map.266
  1207.9 183.6 %shard_map.267 = (f32[128,2048]{1,0:T(8,128)}, f32[64,4096]{1,0:T(8,128)}, f32[64,512]{1,0:T(8,128)}, f32[64,512]{1,0:T(8,128)}, f32[512,2048]{1,0:T(8,128)}, /*...) custom-call(bf16[256,4096]{1,0:T(8,128)(2,1)} %shard_map.243.refs_0_, ...), custom_call_target="tpu_custom_call" | custom-call | flops 1048576 | bytes 1048576 | tf_op jit(solution)/shard_map/pallas_call | solution.py:1218
  1393.2 3.5 fusion.7
  1397.4 5.6 all-to-all-start.5
  1403.2 2.3 fusion.8
  1406.3 5.3 maximum_add_fusion
  1412.9 2.2 fusion.9
  (208 shorter events, 52.7 us)
Async XLA Ops:
  7.2 195.3 %all-gather.6.cloned.1.call-start = ((), (), s32[]{:S(2)}) async-start(), calls=%async_computation.10 | async-start | bytes 23592960 | tf_op jit(solution)/shard_map/all_gather | solution.py:1283
  12.9 4.1 copy-start.28
  12.9 4.1 copy-start.26
  16.2 1.7 copy-start.11
  16.2 298.3 %all-gather.8.cloned.1.call-start = ((), (), s32[]{:S(2)}) async-start(), calls=%async_computation.11 | async-start | bytes 18874368 | tf_op jit(solution)/shard_map/all_gather | solution.py:1286
  167.0 161.7 %copy-start.17 = (f32[4,256,8]{1,2,0:T(8,128)}, f32[4,256,8]{1,2,0:T(8,128)S(1)}, u32[]{:S(2)}) copy-start(f32[4,256,8]{1,2,0:T(8,128)S(1)} %get-tuple-element.144) | copy-start | bytes 98308
  167.0 280.5 %copy-start.16 = (f32[4,256,8]{1,2,0:T(8,128)}, f32[4,256,8]{1,2,0:T(8,128)S(1)}, u32[]{:S(2)}) copy-start(f32[4,256,8]{1,2,0:T(8,128)S(1)} %get-tuple-element.145) | copy-start | bytes 98308
  167.8 24.9 %copy-start.32 = (pred[4,256,8]{1,2,0:T(8,128)(4,1)}, pred[4,256,8]{1,2,0:T(8,128)(4,1)S(1)}, u32[]{:S(2)}) copy-start(pred[4,256,8]{1,2,0:T(8,128)(4,1)S(1)} %get-tuple-element.147) | copy-start | bytes 24580
  167.8 24.9 %copy-start.34 = (pred[4,256,8]{1,2,0:T(8,128)(4,1)}, pred[4,256,8]{1,2,0:T(8,128)(4,1)S(1)}, u32[]{:S(2)}) copy-start(pred[4,256,8]{1,2,0:T(8,128)(4,1)S(1)} %get-tuple-element.146) | copy-start | bytes 24580
  168.6 279.5 %copy-start.18 = (s32[4,8,256]{2,1,0:T(8,128)}, s32[4,8,256]{2,1,0:T(8,128)S(1)}, u32[]{:S(2)}) copy-start(s32[4,8,256]{2,1,0:T(8,128)S(1)} %get-tuple-element.167.place_ref) | copy-start | bytes 98308
  169.4 159.9 %copy-start.19 = (s32[4,8,256]{2,1,0:T(8,128)}, s32[4,8,256]{2,1,0:T(8,128)S(1)}, u32[]{:S(2)}) copy-start(s32[4,8,256]{2,1,0:T(8,128)S(1)} %get-tuple-element.169.place_ref) | copy-start | bytes 98308
  192.7 6.5 copy-start.1
  192.8 7.1 copy-start.23
  192.8 248.9 %all-to-all-start = ((bf16[8,640,2048]{2,1,0:T(8,128)(2,1)}), bf16[8,640,2048]{2,1,0:T(8,128)(2,1)}, u32[]{:S(2)}, u32[]{:S(2)}) async-start(bf16[8,640,2048]{2,1,0:T(8,128)(2,1)} %bitcast.164), calls=%async_computation | async-start | bytes 41943040 | tf_op jit(solution)/shard_map/all_to_all | solution.py:1306
  199.0 139.0 %all-gather.12.cloned.1.call-start = ((), (), s32[]{:S(2)}) async-start(), calls=%async_computation.13 | async-start | bytes 2621440 | tf_op jit(solution)/shard_map/all_gather | solution.py:1361
  199.8 1.9 copy-start.30
  202.4 31.2 %copy-start.8 = (f32[256,128]{1,0:T(8,128)}, f32[256,128]{1,0:T(8,128)S(1)}, u32[]{:S(2)}) copy-start(f32[256,128]{1,0:T(8,128)S(1)} %get-tuple-element.177.cos_ref) | copy-start | bytes 393220
  202.4 31.3 %copy-start.9 = (f32[256,128]{1,0:T(8,128)}, f32[256,128]{1,0:T(8,128)S(1)}, u32[]{:S(2)}) copy-start(f32[256,128]{1,0:T(8,128)S(1)} %get-tuple-element.178.sin_ref) | copy-start | bytes 393220
  217.2 3.9 copy-start
  226.6 5.7 copy-start.39
  232.2 1.6 copy-start.7
  285.3 3.0 copy-start.40
  285.3 134.5 %all-gather.10.cloned.1.call-start = ((), (), s32[]{:S(2)}) async-start(), calls=%async_computation.12 | async-start | bytes 5242880 | tf_op jit(solution)/shard_map/all_gather | solution.py:1378
  314.5 13.0 copy-start.22
  326.1 1.3 copy-start.4
  338.0 23.8 %copy-start.10 = (f32[2,1,256,2048]{3,2,1,0:T(8,128)S(1)}, f32[2,1,256,2048]{3,2,1,0:T(8,128)}, u32[]{:S(2)}) copy-start(f32[2,1,256,2048]{3,2,1,0:T(8,128)} %convert_element_type.90) | copy-start | bytes 12582916
  441.7 7.1 copy-start.5
  441.7 121.8 %all-to-all-start.1 = ((bf16[8,320,2048]{2,1,0:T(8,128)(2,1)}), bf16[8,320,2048]{2,1,0:T(8,128)(2,1)}, u32[]{:S(2)}, u32[]{:S(2)}) async-start(bf16[8,320,2048]{2,1,0:T(8,128)(2,1)} %shard_map.248), calls=%async_computation.1 | async-start | bytes 20971520 | tf_op jit(solution)/shard_map/all_to_all | solution.py:1306
  446.9 84.9 %all-gather.14.cloned.1.call-start = ((), (), s32[]{:S(2)}) async-start(), calls=%async_computation.14 | async-start | bytes 5242880 | tf_op jit(solution)/shard_map/all_gather | solution.py:1378
  563.5 121.9 %all-to-all-start.2 = ((bf16[8,320,2048]{2,1,0:T(8,128)(2,1)}), bf16[8,320,2048]{2,1,0:T(8,128)(2,1)}, u32[]{:S(2)}, u32[]{:S(2)}) async-start(bf16[8,320,2048]{2,1,0:T(8,128)(2,1)} %shard_map.251), calls=%async_computation.2 | async-start | bytes 20971520 | tf_op jit(solution)/shard_map/all_to_all | solution.py:1306
  685.4 121.7 %all-to-all-start.3 = ((bf16[8,320,2048]{2,1,0:T(8,128)(2,1)}), bf16[8,320,2048]{2,1,0:T(8,128)(2,1)}, u32[]{:S(2)}, u32[]{:S(2)}) async-start(bf16[8,320,2048]{2,1,0:T(8,128)(2,1)} %shard_map.252), calls=%async_computation.3 | async-start | bytes 20971520 | tf_op jit(solution)/shard_map/all_to_all | solution.py:1306
  807.1 121.7 %all-to-all-start.4 = ((bf16[8,320,2048]{2,1,0:T(8,128)(2,1)}), bf16[8,320,2048]{2,1,0:T(8,128)(2,1)}, u32[]{:S(2)}, u32[]{:S(2)}) async-start(bf16[8,320,2048]{2,1,0:T(8,128)(2,1)} %shard_map.256), calls=%async_computation.5 | async-start | bytes 20971520 | tf_op jit(solution)/shard_map/all_to_all | solution.py:1306
  812.2 127.9 %reduce-scatter.5.cloned.1.call-start = ((), (), s32[]{:S(2)}) async-start(), calls=%async_computation.15 | async-start | bytes 5242880 | tf_op jit(solution)/shard_map/reduce_scatter | solution.py:1328
  820.7 254.9 %reduce-scatter.9.cloned.1.call-start = ((), (), s32[]{:S(2)}) async-start(), calls=%async_computation.17 | async-start | bytes 5242880 | tf_op jit(solution)/shard_map/reduce_scatter | solution.py:1328
  937.1 1.8 copy-start.13
  937.1 466.0 %reduce-scatter.7.cloned.1.call-start = ((), (), s32[]{:S(2)}) async-start(), calls=%async_computation.16 | async-start | bytes 5242880 | tf_op jit(solution)/shard_map/reduce_scatter | solution.py:1328
  1072.3 340.6 %reduce-scatter.11.cloned.1.call-start = ((), (), s32[]{:S(2)}) async-start(), calls=%async_computation.18 | async-start | bytes 5242880 | tf_op jit(solution)/shard_map/reduce_scatter | solution.py:1328
  1207.9 185.2 %copy-start.2 = (bf16[2,1,256,2048]{3,2,1,0:T(8,128)(2,1)S(1)}, bf16[2,1,256,2048]{3,2,1,0:T(8,128)(2,1)}, u32[]{:S(2)}) copy-start(bf16[2,1,256,2048]{3,2,1,0:T(8,128)(2,1)} %param.16) | copy-start | bytes 6291460
  1207.9 185.2 %copy-start.24 = (f32[2048]{0:T(1024)S(1)}, f32[2048]{0:T(1024)}, u32[]{:S(2)}) copy-start(f32[2048]{0:T(1024)} %param.20) | copy-start | bytes 24580
  1391.5 11.4 copy-start.25
  1391.5 11.5 copy-start.29
  1397.4 14.9 %all-to-all-start.5 = ((f32[32,1,136]{2,1,0:T(1,128)}), f32[32,1,136]{2,1,0:T(1,128)S(1)}, u32[]{:S(2)}, u32[]{:S(2)}) async-start(f32[32,1,136]{2,1,0:T(1,128)} %all_to_all.26), calls=%async_computation.9 | async-start | bytes 65536 | tf_op jit(solution)/shard_map/all_to_all | solution.py:1486
  1403.2 3.1 copy-start.6
  1406.3 5.4 copy-start.27
  1412.9 3.8 copy-start.15
  1415.1 2.5 copy-start.21
  1415.1 3.2 copy-start.20
  1415.1 3.8 copy-start.14
  (8 other events, 7.2 us)
Sparse Core Ops, SparseCore 0:
  16.3 110.2 all-gather.5
  128.6 103.6 all-gather.7
  285.5 52.4 all-gather.11
  340.0 79.8 all-gather.9
  449.6 82.1 all-gather.13
  820.8 78.1 reduce-scatter.4
  937.3 109.1 reduce-scatter.8
  1072.4 110.3 reduce-scatter.6
  1207.4 111.6 reduce-scatter.10

commit v7 on v6

--- a/solution.py
+++ b/solution.py
@@ -79,7 +79,7 @@
             dst_ref=block(i, at),
             send_sem=send_sem.at[way, step, i],
             recv_sem=recv_sem.at[way, step, i],
-            device_id={"ctx": me + (1 if way == 0 else -1)},
+            device_id={"ctx": lax.rem(me + (1 if way == 0 else count - 1), count)},
             device_id_type=pl.DeviceIdType.MESH,
         )
 

time: 1430 us -> 1430 us (level)
  no operation moved by 1% of the time
where the time goes in v7:
time: 1430 us
  Pallas kernels  932 us (65%)
  waiting for transfers between devices  316 us (22%)
  local copies, waits for them, and re-layouts  48.9 us (3%)
  other arithmetic  44.2 us (3%)
  matrix products  36.9 us (3%)
  starting transfers between devices  33.7 us (2%)
  between operations  14.9 us (1%)
    pallas_call x2, Pallas kernels, attend_back(): pl.pallas_call(functools.partial(attend_back_kernel, per, steps, width **...  247 us
    pallas_call x2, Pallas kernels, line_gather(): pl.pallas_call(functools.partial(gather_kernel, count, arrays, stacked),...  187 us
    pallas_call x1, Pallas kernels, grad_sums(): pl.pallas_call(functools.partial(grad_sums_kernel, ring, micro, head_dim,...  184 us
    all_to_all x5, waiting for transfers between devices, exchange(): return lax.all_to_all(rows, 'exp', split_axis=0, concat_axis=0, tiled=True)  183 us
    all_gather x2, waiting for transfers between devices, per_device(): lax.all_gather(feed, 'ctx', axis=0, tiled=True)  123 us
    pallas_call x2, Pallas kernels, run_expert(): pl.pallas_call(expert_kernel, grid=(sources,), in_specs=[pl.BlockSpec((No...  115 us
    pallas_call x1, Pallas kernels, expert_weight_grads(): pl.pallas_call(functools.partial(weight_kernel, steps, micro), grid=(micr...  73.3 us
    pallas_call x2, Pallas kernels, attend(): pl.pallas_call(functools.partial(attend_kernel, per, width ** (-0.5) * ma...  47.4 us
  transfers between devices with their start and end apart: 15, of which 8 were waited for; matrix products, arithmetic and copies ran while one was open for 7% of the time, Pallas kernels for 65%

profile of v7, /device:TPU:0, one launch (start us, length us, event | category | flops | bytes accessed | tf_op | source)
XLA Modules:
  0.0 1426.6 jit_solution(11222803535082888698)
XLA Ops:
  12.9 3.3 pad_maximum_fusion
  19.4 145.2 %shard_map.239 = (bf16[2,1024,2048]{2,1,0:T(8,128)(2,1)}, f32[256,128]{1,0:T(8,128)}) custom-call(bf16[256,2048]{1,0:T(8,128)(2,1)} %get-tuple-element.151.refs_0_.out_grad_ref, bf16[256,2048]{1,0:T(8,128)(2,1)} %get-tuple-element.150.refs_1_.out_grad_ref, f32[64,128]{1,0:T(8,128)} %reshape.280.refs_2_), custom_call_target="tpu_custom_call" | custom-call | bytes 209715200 | tf_op jit(solution)/shard_map/pallas_call | solution.py:135
  170.1 22.6 %shard_map.240.refs_1_ = bf16[8,8,80,2048]{3,2,1,0:T(8,128)(2,1)} custom-call(s32[8,2,4,256]{3,2,1,0:T(4,128)} %reshape.282.place_ref, f32[8,2,4,256]{3,2,1,0:T(4,128)} %reshape.283.weight_ref, bf16[2048,2048]{1,0:T(8,128)(2,1)} %bitcast.183), custom_call_target="tpu_custom_call" | custom-call | flops 1048576 | bytes 1048576 | tf_op jit(solution)/shard_map/pallas_call | solution.py:263
  192.8 6.3 all-to-all-start
  202.5 14.8 %fusion.24.raw_ref.pair_raw_ref = f32[512,5120]{1,0:T(8,128)S(1)} fusion(bf16[512,2048]{1,0:T(8,128)(2,1)} %shard_map.241, bf16[2048,5120]{1,0:T(8,128)(2,1)} %all-gather.6.cloned.1.call-done.refs_9_), kind=kOutput, calls=%fused_computation.103 | convolution fusion | flops 10737418240 | bytes 33554432 | tf_op jit(solution)/shard_map/dot_general | solution.py:1269
  217.2 3.9 copy-done
  222.6 4.0 reshape.286
  226.6 2.3 slice.129
  229.0 2.7 slice.171
  233.8 5.0 fusion.11
  238.8 2.4 fusion.12
  242.4 41.7 %shard_map.242.refs_1_ = bf16[1024,1024]{1,0:T(8,128)(2,1)} custom-call(bf16[256,1024]{1,0:T(8,128)(2,1)} %slice.108.refs_0_), custom_call_target="tpu_custom_call" | custom-call | bytes 209715200 | tf_op jit(solution)/shard_map/pallas_call | solution.py:135
  285.8 2.5 convert_element_type.90
  290.9 23.6 %shard_map.243.refs_0_ = bf16[256,4096]{1,0:T(8,128)(2,1)} custom-call(s32[2]{0:T(128)} %get-tuple-element.175.place_ref, f32[512,5120]{1,0:T(8,128)} %copy-done, bf16[4,256,1024]{2,1,0:T(8,128)(2,1)} %bitcast.172, f32[1,128]{1,0:T(1,128)} %bitcast.218, f32[256,128]{1,0:T(8,128)} %copy-done.8, f32[256,128]{1,0:T(8,128)} %copy-done.9), custom_call_target="tpu_custom_call" | custom-call | flops 1048576 | bytes 1048576 | tf_op jit(solution)/shard_map/pallas_call | solution.py:664
  314.5 11.6 multiply_reduce_fusion.1
  330.0 8.0 all-gather.12.cloned.1.call-done
  338.0 23.8 %shard_map.245.refs_1_ = bf16[256,4096]{1,0:T(8,128)(2,1)} custom-call(s32[2]{0:T(128)} %get-tuple-element.176.place_ref, f32[512,5120]{1,0:T(8,128)} %copy-done, bf16[4,256,1024]{2,1,0:T(8,128)(2,1)} %bitcast.184, f32[1,128]{1,0:T(1,128)} %bitcast.219, f32[256,128]{1,0:T(8,128)} %copy-done.8, f32[256,128]{1,0:T(8,128)} %copy-done.9, ...), custom_call_target="tpu_custom_call" | custom-call | flops 1048576 | bytes 1048576 | tf_op jit(solution)/shard_map/pallas_call | solution.py:664
  361.8 8.9 multiply_reduce_fusion
  373.2 46.6 %all-gather.10.cloned.1.call-done.refs_0_ = bf16[1024,2048]{1,0:T(8,128)(2,1)} async-done(((bf16[256,2048]{1,0:T(8,128)(2,1)}), bf16[1024,2048]{1,0:T(8,128)(2,1)}) %all-gather.10.cloned.1.call-update) | async-done | bytes 4194320 | tf_op jit(solution)/shard_map/all_gather | solution.py:1378
  419.8 11.3 shard_map.247
  431.1 10.6 all-to-all-done
  441.7 5.3 all-to-all-start.1
  448.8 2.5 copy.112
  453.1 2.3 copy.114.refs_2_
  455.4 76.5 %all-gather.14.cloned.1.call-done.rows_ref = bf16[1024,2048]{1,0:T(8,128)(2,1)} async-done(((bf16[256,2048]{1,0:T(8,128)(2,1)}), bf16[1024,2048]{1,0:T(8,128)(2,1)}) %all-gather.14.cloned.1.call-update) | async-done | bytes 4194320 | tf_op jit(solution)/shard_map/all_gather | solution.py:1378
  531.9 11.4 shard_map.250
  543.3 20.2 %all-to-all-done.1.rows_ref.refs_1_.refs_0_ = bf16[8,320,2048]{2,1,0:T(8,128)(2,1)} async-done(((bf16[8,320,2048]{2,1,0:T(8,128)(2,1)}), bf16[8,320,2048]{2,1,0:T(8,128)(2,1)}, u32[]{:S(2)}, u32[]{:S(2)}) %all-to-all-start.1) | async-done | bytes 10485792 | tf_op jit(solution)/shard_map/all_to_all | solution.py:1306
  563.5 5.3 all-to-all-start.2
  568.8 57.5 %shard_map.249 = (bf16[2560,768]{1,0:T(8,128)(2,1)}, bf16[2560,768]{1,0:T(8,128)(2,1)}, bf16[2560,768]{1,0:T(8,128)(2,1)}, bf16[2560,2048]{1,0:T(8,128)(2,1)}, b...) custom-call(bf16[8,320,2048]{2,1,0:T(8,128)(2,1)} %all-to-all-done.1.rows_ref.refs_1_.refs_0_, ...), custom_call_target="tpu_custom_call" | custom-call | flops 1048576 | bytes 1048576 | tf_op jit(solution)/shard_map/pallas_call | solution.py:193
  626.4 59.0 %all-to-all-done.2.refs_1_.rows_ref = bf16[8,320,2048]{2,1,0:T(8,128)(2,1)} async-done(((bf16[8,320,2048]{2,1,0:T(8,128)(2,1)}), bf16[8,320,2048]{2,1,0:T(8,128)(2,1)}, u32[]{:S(2)}, u32[]{:S(2)}) %all-to-all-start.2) | async-done | bytes 10485792 | tf_op jit(solution)/shard_map/all_to_all | solution.py:1306
  685.4 5.2 all-to-all-start.3
  690.5 57.6 %shard_map.253 = (bf16[2560,768]{1,0:T(8,128)(2,1)}, bf16[2560,768]{1,0:T(8,128)(2,1)}, bf16[2560,768]{1,0:T(8,128)(2,1)}, bf16[2560,2048]{1,0:T(8,128)(2,1)}, b...) custom-call(bf16[8,320,2048]{2,1,0:T(8,128)(2,1)} %all-to-all-done.2.refs_1_.rows_ref, ...), custom_call_target="tpu_custom_call" | custom-call | flops 1048576 | bytes 1048576 | tf_op jit(solution)/shard_map/pallas_call | solution.py:193
  748.2 58.9 %all-to-all-done.3.refs_0_.refs_1_ = bf16[8,320,2048]{2,1,0:T(8,128)(2,1)} async-done(((bf16[8,320,2048]{2,1,0:T(8,128)(2,1)}), bf16[8,320,2048]{2,1,0:T(8,128)(2,1)}, u32[]{:S(2)}, u32[]{:S(2)}) %all-to-all-start.3) | async-done | bytes 10485792 | tf_op jit(solution)/shard_map/all_to_all | solution.py:1306
  807.1 5.2 all-to-all-start.4
  812.3 8.4 shard_map.255
  820.8 73.3 %shard_map.257 = (f32[1,2048,768]{2,1,0:T(8,128)}, f32[1,2048,768]{2,1,0:T(8,128)}, f32[1,768,2048]{2,1,0:T(8,128)}) custom-call(bf16[8,320,2048]{2,1,0:T(8,128)(2,1)} %all-to-all-done.1.rows_ref.refs_1_.refs_0_, bf16[8,320,2048]{2,1,0:T(8,128)(2,1)} %all-to-all-done.2.refs_1_.rows_ref, bf16[8,2,320,2048]{3,2,1,0:T(8,128)(2,1)} %bitcast.31.refs_1_.grad_ref.refs_2_, ...), custom_call_target="tpu_custom_call" | custom-call | flops 1048576 | bytes 1048576 | tf_op jit(solution)/shard_map/pallas_call | solution.py:343
  894.1 34.7 %all-to-all-done.4.refs_0_ = bf16[8,320,2048]{2,1,0:T(8,128)(2,1)} async-done(((bf16[8,320,2048]{2,1,0:T(8,128)(2,1)}), bf16[8,320,2048]{2,1,0:T(8,128)(2,1)}, u32[]{:S(2)}, u32[]{:S(2)}) %all-to-all-start.4) | async-done | bytes 10485792 | tf_op jit(solution)/shard_map/all_to_all | solution.py:1306
  928.8 8.3 shard_map.259.refs_1_
  940.2 123.7 %shard_map.261 = (bf16[256,4096]{1,0:T(8,128)(2,1)}, bf16[256,1024]{1,0:T(8,128)(2,1)}, f32[8,128]{1,0:T(8,128)}, bf16[256,2048]{1,0:T(8,128)(2,1)}, f32[256,204...) custom-call(s32[2]{0:T(128)} %get-tuple-element.175.place_ref, ...), custom_call_target="tpu_custom_call" | custom-call | flops 1048576 | bytes 1048576 | tf_op jit(solution)/shard_map/pallas_call | solution.py:707
  1063.9 8.4 shard_map.262
  1075.6 123.3 %shard_map.265 = (bf16[256,4096]{1,0:T(8,128)(2,1)}, bf16[256,1024]{1,0:T(8,128)(2,1)}, f32[8,128]{1,0:T(8,128)}, bf16[256,2048]{1,0:T(8,128)(2,1)}, f32[256,204...) custom-call(s32[2]{0:T(128)} %get-tuple-element.176.place_ref, ...), custom_call_target="tpu_custom_call" | custom-call | flops 1048576 | bytes 1048576 | tf_op jit(solution)/shard_map/pallas_call | solution.py:707
  1198.8 8.4 shard_map.266
  1207.9 183.6 %shard_map.267 = (f32[128,2048]{1,0:T(8,128)}, f32[64,4096]{1,0:T(8,128)}, f32[64,512]{1,0:T(8,128)}, f32[64,512]{1,0:T(8,128)}, f32[512,2048]{1,0:T(8,128)}, /*...) custom-call(bf16[256,4096]{1,0:T(8,128)(2,1)} %shard_map.243.refs_0_, ...), custom_call_target="tpu_custom_call" | custom-call | flops 1048576 | bytes 1048576 | tf_op jit(solution)/shard_map/pallas_call | solution.py:1218
  1393.2 3.5 fusion.7
  1397.4 5.6 all-to-all-start.5
  1403.2 2.3 fusion.8
  1406.3 5.3 maximum_add_fusion
  1412.9 2.2 fusion.9
  (208 shorter events, 52.7 us)
Async XLA Ops:
  7.2 195.3 %all-gather.6.cloned.1.call-start = ((), (), s32[]{:S(2)}) async-start(), calls=%async_computation.10 | async-start | bytes 23592960 | tf_op jit(solution)/shard_map/all_gather | solution.py:1283
  12.9 4.1 copy-start.28
  12.9 4.1 copy-start.26
  16.2 1.7 copy-start.11
  16.2 298.3 %all-gather.8.cloned.1.call-start = ((), (), s32[]{:S(2)}) async-start(), calls=%async_computation.11 | async-start | bytes 18874368 | tf_op jit(solution)/shard_map/all_gather | solution.py:1286
  167.0 161.7 %copy-start.17 = (f32[4,256,8]{1,2,0:T(8,128)}, f32[4,256,8]{1,2,0:T(8,128)S(1)}, u32[]{:S(2)}) copy-start(f32[4,256,8]{1,2,0:T(8,128)S(1)} %get-tuple-element.144) | copy-start | bytes 98308
  167.0 280.5 %copy-start.16 = (f32[4,256,8]{1,2,0:T(8,128)}, f32[4,256,8]{1,2,0:T(8,128)S(1)}, u32[]{:S(2)}) copy-start(f32[4,256,8]{1,2,0:T(8,128)S(1)} %get-tuple-element.145) | copy-start | bytes 98308
  167.8 24.9 %copy-start.32 = (pred[4,256,8]{1,2,0:T(8,128)(4,1)}, pred[4,256,8]{1,2,0:T(8,128)(4,1)S(1)}, u32[]{:S(2)}) copy-start(pred[4,256,8]{1,2,0:T(8,128)(4,1)S(1)} %get-tuple-element.147) | copy-start | bytes 24580
  167.8 24.9 %copy-start.34 = (pred[4,256,8]{1,2,0:T(8,128)(4,1)}, pred[4,256,8]{1,2,0:T(8,128)(4,1)S(1)}, u32[]{:S(2)}) copy-start(pred[4,256,8]{1,2,0:T(8,128)(4,1)S(1)} %get-tuple-element.146) | copy-start | bytes 24580
  168.6 279.5 %copy-start.18 = (s32[4,8,256]{2,1,0:T(8,128)}, s32[4,8,256]{2,1,0:T(8,128)S(1)}, u32[]{:S(2)}) copy-start(s32[4,8,256]{2,1,0:T(8,128)S(1)} %get-tuple-element.167.place_ref) | copy-start | bytes 98308
  169.4 159.9 %copy-start.19 = (s32[4,8,256]{2,1,0:T(8,128)}, s32[4,8,256]{2,1,0:T(8,128)S(1)}, u32[]{:S(2)}) copy-start(s32[4,8,256]{2,1,0:T(8,128)S(1)} %get-tuple-element.169.place_ref) | copy-start | bytes 98308
  192.7 6.5 copy-start.1
  192.8 7.1 copy-start.23
  192.8 248.9 %all-to-all-start = ((bf16[8,640,2048]{2,1,0:T(8,128)(2,1)}), bf16[8,640,2048]{2,1,0:T(8,128)(2,1)}, u32[]{:S(2)}, u32[]{:S(2)}) async-start(bf16[8,640,2048]{2,1,0:T(8,128)(2,1)} %bitcast.164), calls=%async_computation | async-start | bytes 41943040 | tf_op jit(solution)/shard_map/all_to_all | solution.py:1306
  199.0 139.0 %all-gather.12.cloned.1.call-start = ((), (), s32[]{:S(2)}) async-start(), calls=%async_computation.13 | async-start | bytes 2621440 | tf_op jit(solution)/shard_map/all_gather | solution.py:1361
  199.8 1.9 copy-start.30
  202.4 31.2 %copy-start.8 = (f32[256,128]{1,0:T(8,128)}, f32[256,128]{1,0:T(8,128)S(1)}, u32[]{:S(2)}) copy-start(f32[256,128]{1,0:T(8,128)S(1)} %get-tuple-element.177.cos_ref) | copy-start | bytes 393220
  202.4 31.3 %copy-start.9 = (f32[256,128]{1,0:T(8,128)}, f32[256,128]{1,0:T(8,128)S(1)}, u32[]{:S(2)}) copy-start(f32[256,128]{1,0:T(8,128)S(1)} %get-tuple-element.178.sin_ref) | copy-start | bytes 393220
  217.2 3.9 copy-start
  226.6 5.7 copy-start.39
  232.2 1.6 copy-start.7
  285.3 3.0 copy-start.40
  285.3 134.5 %all-gather.10.cloned.1.call-start = ((), (), s32[]{:S(2)}) async-start(), calls=%async_computation.12 | async-start | bytes 5242880 | tf_op jit(solution)/shard_map/all_gather | solution.py:1378
  314.5 13.0 copy-start.22
  326.1 1.3 copy-start.4
  338.0 23.8 %copy-start.10 = (f32[2,1,256,2048]{3,2,1,0:T(8,128)S(1)}, f32[2,1,256,2048]{3,2,1,0:T(8,128)}, u32[]{:S(2)}) copy-start(f32[2,1,256,2048]{3,2,1,0:T(8,128)} %convert_element_type.90) | copy-start | bytes 12582916
  441.7 7.1 copy-start.5
  441.7 121.8 %all-to-all-start.1 = ((bf16[8,320,2048]{2,1,0:T(8,128)(2,1)}), bf16[8,320,2048]{2,1,0:T(8,128)(2,1)}, u32[]{:S(2)}, u32[]{:S(2)}) async-start(bf16[8,320,2048]{2,1,0:T(8,128)(2,1)} %shard_map.248), calls=%async_computation.1 | async-start | bytes 20971520 | tf_op jit(solution)/shard_map/all_to_all | solution.py:1306
  446.9 84.9 %all-gather.14.cloned.1.call-start = ((), (), s32[]{:S(2)}) async-start(), calls=%async_computation.14 | async-start | bytes 5242880 | tf_op jit(solution)/shard_map/all_gather | solution.py:1378
  563.5 121.9 %all-to-all-start.2 = ((bf16[8,320,2048]{2,1,0:T(8,128)(2,1)}), bf16[8,320,2048]{2,1,0:T(8,128)(2,1)}, u32[]{:S(2)}, u32[]{:S(2)}) async-start(bf16[8,320,2048]{2,1,0:T(8,128)(2,1)} %shard_map.251), calls=%async_computation.2 | async-start | bytes 20971520 | tf_op jit(solution)/shard_map/all_to_all | solution.py:1306
  685.4 121.7 %all-to-all-start.3 = ((bf16[8,320,2048]{2,1,0:T(8,128)(2,1)}), bf16[8,320,2048]{2,1,0:T(8,128)(2,1)}, u32[]{:S(2)}, u32[]{:S(2)}) async-start(bf16[8,320,2048]{2,1,0:T(8,128)(2,1)} %shard_map.252), calls=%async_computation.3 | async-start | bytes 20971520 | tf_op jit(solution)/shard_map/all_to_all | solution.py:1306
  807.1 121.7 %all-to-all-start.4 = ((bf16[8,320,2048]{2,1,0:T(8,128)(2,1)}), bf16[8,320,2048]{2,1,0:T(8,128)(2,1)}, u32[]{:S(2)}, u32[]{:S(2)}) async-start(bf16[8,320,2048]{2,1,0:T(8,128)(2,1)} %shard_map.256), calls=%async_computation.5 | async-start | bytes 20971520 | tf_op jit(solution)/shard_map/all_to_all | solution.py:1306
  812.2 127.9 %reduce-scatter.5.cloned.1.call-start = ((), (), s32[]{:S(2)}) async-start(), calls=%async_computation.15 | async-start | bytes 5242880 | tf_op jit(solution)/shard_map/reduce_scatter | solution.py:1328
  820.7 254.9 %reduce-scatter.9.cloned.1.call-start = ((), (), s32[]{:S(2)}) async-start(), calls=%async_computation.17 | async-start | bytes 5242880 | tf_op jit(solution)/shard_map/reduce_scatter | solution.py:1328
  937.1 1.8 copy-start.13
  937.1 466.0 %reduce-scatter.7.cloned.1.call-start = ((), (), s32[]{:S(2)}) async-start(), calls=%async_computation.16 | async-start | bytes 5242880 | tf_op jit(solution)/shard_map/reduce_scatter | solution.py:1328
  1072.3 340.6 %reduce-scatter.11.cloned.1.call-start = ((), (), s32[]{:S(2)}) async-start(), calls=%async_computation.18 | async-start | bytes 5242880 | tf_op jit(solution)/shard_map/reduce_scatter | solution.py:1328
  1207.9 185.2 %copy-start.2 = (bf16[2,1,256,2048]{3,2,1,0:T(8,128)(2,1)S(1)}, bf16[2,1,256,2048]{3,2,1,0:T(8,128)(2,1)}, u32[]{:S(2)}) copy-start(bf16[2,1,256,2048]{3,2,1,0:T(8,128)(2,1)} %param.16) | copy-start | bytes 6291460
  1207.9 185.2 %copy-start.24 = (f32[2048]{0:T(1024)S(1)}, f32[2048]{0:T(1024)}, u32[]{:S(2)}) copy-start(f32[2048]{0:T(1024)} %param.20) | copy-start | bytes 24580
  1391.5 11.4 copy-start.25
  1391.5 11.5 copy-start.29
  1397.4 14.9 %all-to-all-start.5 = ((f32[32,1,136]{2,1,0:T(1,128)}), f32[32,1,136]{2,1,0:T(1,128)S(1)}, u32[]{:S(2)}, u32[]{:S(2)}) async-start(f32[32,1,136]{2,1,0:T(1,128)} %all_to_all.26), calls=%async_computation.9 | async-start | bytes 65536 | tf_op jit(solution)/shard_map/all_to_all | solution.py:1486
  1403.2 3.1 copy-start.6
  1406.3 5.4 copy-start.27
  1412.9 3.8 copy-start.15
  1415.1 2.5 copy-start.21
  1415.1 3.2 copy-start.20
  1415.1 3.8 copy-start.14
  (8 other events, 7.2 us)
Sparse Core Ops, SparseCore 0:
  16.3 110.2 all-gather.5
  128.6 103.6 all-gather.7
  285.5 52.4 all-gather.11
  340.0 79.8 all-gather.9
  449.6 82.1 all-gather.13
  820.8 78.1 reduce-scatter.4
  937.3 109.1 reduce-scatter.8
  1072.4 110.3 reduce-scatter.6
  1207.4 111.6 reduce-scatter.10
